TPU v7x, 768 devices: a whole 4x8x12 slice. The times are simulated.
768 devices in a mesh: blk: 16 (over z_hi, x), grp: 48 (over y, z_lo, core).
Axes of the slice: x: 4, y: 8, z: 12 (z_hi: 4, z_lo: 3; z = z_hi * 3 + z_lo), core: 2. Of those that a mesh axis runs over, the one named last changes fastest.
Arguments:
- query_states: bfloat16 [16, 48, 128, 1024], P('blk', 'grp'), may hold values from -96 to 96
- passages: bfloat16 [16, 48, 128, 1024], P('blk', 'grp'), may hold values from -6 to 6
- proj_weight: bfloat16 [1024, 1024], replicated, may hold values from -0.2 to 1.2
- neg_store: bfloat16 [16, 48, 512, 1024], P('blk', 'grp'), may hold values from -12 to 12
- positive: int32 [16, 48, 128], P('blk', 'grp'), may hold values from 0 to 127, each once within a row
- neg_owner: int32 [16, 48, 896, 1], P('blk', 'grp'), may hold values from 0 to 15; in each aligned block of 896 rows (0 to 895, 896 to 1791, ..., all dimensions but the last counted through in order) at most 64 rows name the same one
- neg_slot: int32 [16, 48, 128, 7], P('blk', 'grp'), may hold values from 0 to 511
- neg_count: int32 [16, 48, 128], P('blk', 'grp'), may hold values from 1 to 7
Outputs:
- state_grads: bfloat16 [16, 48, 128, 1024], P('blk', 'grp')
- passage_grads: bfloat16 [16, 48, 128, 1024], P('blk', 'grp')
- weight_grad: float32 [1024, 1024], P('blk')
Inputs may be any that keep to these rules, and one draw needn't show every extreme that they name: `neg_owner`: among the 896 slots of one device no owner is named more than 64 times, a bound that some block reaches.
All inputs are finite; a program needn't handle non-finite values.
Results may differ from a plain program's by a relative error of at most 0.017.
Values may be sent and summed in bfloat16 or wider, within the bound.
No kernel may reach another device: no remote copies, remote signals or barrier semaphores. Data moves between devices by JAX's collectives and lax.ppermute only.
A program may use at most 64 MiB of HBM per device.

v0:
```python
import jax
import jax.numpy as jnp
from jax import lax
from jax.sharding import PartitionSpec as P

STOPS = 4


def shifted(x, axis, by):
    count = lax.axis_size(axis)
    return lax.ppermute(x, axis, [(i, (i + by) % count) for i in range(count)])


def contract_rows(left, right):
    return lax.dot_general(
        left, right, (((0,), (0,)), ((), ())), preferred_element_type=jnp.float32
    )


def contract_cols(left, right):
    return lax.dot_general(
        left, right, (((1,), (1,)), ((), ())), preferred_element_type=jnp.float32
    )


def local(query_states, passages, proj_weight, neg_store, positive, neg_owner, neg_slot, neg_count):
    width = query_states.shape[-1]
    states = query_states.reshape(-1, width)
    rows = states.shape[0]
    per_query = neg_slot.shape[-1]
    factor = width ** (-0.5)
    members = lax.axis_size("blk")
    slots_per = 8 * rows // members
    queries = jnp.dot(states, proj_weight, preferred_element_type=jnp.float32).astype(jnp.bfloat16)
    owners = neg_owner.reshape(-1)
    targets = neg_slot.reshape(-1)
    owner_table = (owners[:, None] == jnp.arange(members, dtype=jnp.int32)[None, :]).astype(
        jnp.int32
    )
    ranking = jnp.sum((jnp.cumsum(owner_table, axis=0) - 1) * owner_table, axis=1)
    placed = owners * slots_per + ranking
    request = (
        jnp.zeros((members * slots_per,), jnp.int32)
        .at[placed]
        .set(targets)
        .reshape(members, slots_per)
    )
    incoming = lax.all_to_all(request, "blk", split_axis=0, concat_axis=0, tiled=True)
    store = neg_store.reshape(-1, width)
    served = jnp.take(store, incoming.reshape(-1), axis=0).reshape(members, slots_per, width)
    replies = lax.all_to_all(served, "blk", split_axis=0, concat_axis=0, tiled=True)
    negatives = jnp.take(replies.reshape(-1, width), placed, axis=0).reshape(rows, per_query, width)
    own_block = passages.reshape(rows, width)
    blocks = [own_block]
    moving = own_block
    for stop in range(1, STOPS):
        moving = shifted(moving, "blk", 1)
        blocks.append(moving)
    candidates = jnp.concatenate(blocks, axis=0)
    batch_scores = contract_cols(queries, candidates) * factor
    neg_scores = (
        jnp.einsum("rd,rkd->rk", queries, negatives, preferred_element_type=jnp.float32) * factor
    )
    live = jnp.arange(per_query, dtype=jnp.int32)[None, :] < neg_count.reshape(rows, 1)
    neg_scores = jnp.where(live, neg_scores, -jnp.inf)
    top = jnp.maximum(
        jnp.max(batch_scores, axis=1, keepdims=True), jnp.max(neg_scores, axis=1, keepdims=True)
    )
    batch_exp = jnp.exp(batch_scores - top)
    neg_exp = jnp.exp(neg_scores - top)
    total = jnp.sum(batch_exp, axis=1, keepdims=True) + jnp.sum(neg_exp, axis=1, keepdims=True)
    target = positive.reshape(rows, 1)
    hit = (jnp.arange(STOPS * rows, dtype=jnp.int32)[None, :] == target).astype(jnp.float32)
    batch_grad = (batch_exp / total - hit).astype(jnp.bfloat16)
    neg_grad = (neg_exp / total).astype(jnp.bfloat16)
    inner = jnp.dot(batch_grad, candidates, preferred_element_type=jnp.float32)
    inner = inner + jnp.einsum(
        "rk,rkd->rd", neg_grad, negatives, preferred_element_type=jnp.float32
    )
    query_grad = (factor * inner).astype(jnp.bfloat16)
    block_grads = factor * contract_rows(batch_grad, queries)
    pieces = [block_grads[stop * rows : (stop + 1) * rows] for stop in range(STOPS)]
    summed = pieces[0]
    for stop in range(1, STOPS):
        summed = summed + shifted(pieces[stop].astype(jnp.bfloat16), "blk", -stop).astype(
            jnp.float32
        )
    passage_grads = summed.astype(jnp.bfloat16).reshape(passages.shape)
    state_grads = (
        contract_cols(query_grad, proj_weight).astype(jnp.bfloat16).reshape(query_states.shape)
    )
    group_share = lax.psum_scatter(
        contract_rows(states, query_grad).astype(jnp.bfloat16),
        "blk",
        scatter_dimension=0,
        tiled=True,
    ).astype(jnp.float32)
    weight_grad = lax.psum(group_share, "grp")
    return (state_grads, passage_grads, weight_grad)


def solution(mesh):
    placed = (
        P("blk", "grp", None, None),
        P("blk", "grp", None, None),
        P(),
        P("blk", "grp", None, None),
        P("blk", "grp", None),
        P("blk", "grp", None, None),
        P("blk", "grp", None, None),
        P("blk", "grp", None),
    )
    return jax.shard_map(
        local,
        mesh=mesh,
        in_specs=placed,
        out_specs=(P("blk", "grp", None, None), P("blk", "grp", None, None), P("blk", None)),
        check_vma=False,
    )
```

profile of v0, /device:TPU:192, one launch (start us, length us, event | category | flops | bytes accessed | tf_op | source)
XLA Modules:
  0.0 568.5 jit_solution(9352193192940126769)
XLA Ops:
  7.2 0.9 multiply_reduce_fusion
  8.1 2.0 reduce-window.6
  11.2 0.8 copy.25
  12.2 5.3 scatter_custom_fusion
  17.5 23.8 %all_to_all.14 = s32[16,1,64]{2,1,0:T(1,128)S(1)} all-to-all(s32[16,1,64]{2,1,0:T(1,128)S(1)} %all_to_all.9), channel_id=1, replica_groups=mesh['blk'=16,'grp'=48] {'blk'}, dimensions={0} | all-to-all | bytes 8192 | tf_op jit(solution)/shard_map/all_to_all | solution.py:48
  42.6 7.4 %gather_fusion = bf16[1024,1024]{1,0:T(8,128)(2,1)} fusion(bf16[512,1024]{1,0:T(8,128)(2,1)} %bitcast.67, s32[1024]{0:T(1024)S(1)} %broadcast_clamp_fusion), kind=kCustom, calls=%fused_computation | custom fusion | bytes 4198400 | tf_op jit(solution)/shard_map/jit(_take)/gather | solution.py:50
  50.0 3.2 broadcast_select_fusion
  53.2 7.6 %all-to-all-start.1 = ((bf16[16,64,1024]{2,1,0:T(8,128)(2,1)}), bf16[16,64,1024]{2,1,0:T(8,128)(2,1)}, u32[]{:S(2)}, u32[]{:S(2)}) async-start(bf16[16,64,1024]{2,1,0:T(8,128)(2,1)} %broadcast_select_fusion), calls=%async_computation.1 | async-start | bytes 4194304 | tf_op jit(solution)/shard_map/all_to_all | solution.py:51
  60.8 3.4 collective-permute-start
  64.7 34.4 %collective-permute-done = bf16[128,1024]{1,0:T(8,128)(2,1)S(1)} collective-permute-done((bf16[128,1024]{1,0:T(8,128)(2,1)S(1)}, bf16[128,1024]{1,0:T(8,128)(2,1)S(1)}, u32[]{:S(2)}, u32[]{:S(2)}) %collective-permute-start) | collective-permute-done | bytes 262176 | tf_op jit(solution)/shard_map/ppermute | solution.py:11
  99.2 1.9 collective-permute-start.1
  101.3 42.4 %collective-permute-done.1 = bf16[128,1024]{1,0:T(8,128)(2,1)} collective-permute-done((bf16[128,1024]{1,0:T(8,128)(2,1)S(1)}, bf16[128,1024]{1,0:T(8,128)(2,1)}, u32[]{:S(2)}, u32[]{:S(2)}) %collective-permute-start.1) | collective-permute-done | bytes 262176 | tf_op jit(solution)/shard_map/ppermute | solution.py:11
  143.6 1.9 collective-permute-start.2
  146.0 18.9 %collective-permute-done.2 = bf16[128,1024]{1,0:T(8,128)(2,1)S(1)} collective-permute-done((bf16[128,1024]{1,0:T(8,128)(2,1)}, bf16[128,1024]{1,0:T(8,128)(2,1)S(1)}, u32[]{:S(2)}, u32[]{:S(2)}) %collective-permute-start.2) | collective-permute-done | bytes 262176 | tf_op jit(solution)/shard_map/ppermute | solution.py:11
  165.6 1.6 fusion.30
  167.2 7.4 %gather_fusion.1 = bf16[896,1024]{1,0:T(8,128)(2,1)} fusion(bf16[1024,1024]{1,0:T(8,128)(2,1)} %bitcast.10, s32[1024]{0:T(1024)S(1)} %pad_clamp_fusion), kind=kCustom, calls=%fused_computation.1 | custom fusion | bytes 3673600 | tf_op jit(solution)/shard_map/jit(_take)/gather | solution.py:52
  174.6 3.9 gather.15
  178.5 3.3 fusion.1
  182.3 2.4 fusion
  184.7 1.5 fusion.3
  186.2 2.0 convert_bitcast_fusion
  188.2 4.0 copy.31
  192.8 1.9 collective-permute-start.3
  194.8 1.9 collective-permute-start.4
  196.7 14.1 %collective-permute-start.5 = (bf16[128,1024]{1,0:T(8,128)(2,1)S(1)}, bf16[128,1024]{1,0:T(8,128)(2,1)S(1)}, u32[]{:S(2)}, u32[]{:S(2)}) collective-permute-start(bf16[128,1024]{1,0:T(8,128)(2,1)S(1)} %get-tuple-element.21), channel_id=1, source_target_pairs={{0,624},{48,672},{96,720},{144,0},{192,48},{240,96},{288,144},{336... | collective-permute-start | bytes 786440 | tf_op jit(solution)/shard_map/ppermute | solution.py:11
  210.8 1.5 fusion.4
  212.4 4.1 collective-permute-done.5
  216.4 0.9 fusion.11
  217.3 129.8 %reduce-scatter.4.cloned.1.call-done = bf16[64,1024]{1,0:T(8,128)(2,1)} async-done(((bf16[1024,1024]{1,0:T(8,128)(2,1)}), bf16[64,1024]{1,0:T(8,128)(2,1)}) %reduce-scatter.4.cloned.1.call-update) | async-done | bytes 131088
  347.1 1.1 copy.32
  348.2 212.6 %all-reduce.1 = f32[64,1024]{0,1:T(8,128)S(1)} all-reduce(bf16[64,1024]{0,1:T(8,128)(2,1)S(1)} %copy.32), channel_id=1, replica_groups=mesh['blk'=16,'grp'=48] {'grp'}, use_global_device_ids=true, to_apply=%region_9.10 | all-reduce | flops 65536 | bytes 393216 | tf_op jit(solution)/shard_map/psum | solution.py:98
  560.8 0.9 copy.26
  (50 shorter events, 5.7 us)
Async XLA Ops:
  7.2 138.4 %copy-start = (bf16[1024,1024]{1,0:T(8,128)(2,1)S(1)}, bf16[1024,1024]{1,0:T(8,128)(2,1)}, u32[]{:S(2)}) copy-start(bf16[1024,1024]{1,0:T(8,128)(2,1)} %param.10) | copy-start | bytes 6291460
  53.2 7.6 %copy-start.4 = (bf16[1,1,128,1024]{3,2,1,0:T(8,128)(2,1)S(1)}, bf16[1,1,128,1024]{3,2,1,0:T(8,128)(2,1)}, u32[]{:S(2)}) copy-start(bf16[1,1,128,1024]{3,2,1,0:T(8,128)(2,1)} %param.9) | copy-start | bytes 786436
  53.2 92.4 %copy-start.1 = (bf16[1,1,128,1024]{3,2,1,0:T(8,128)(2,1)S(1)}, bf16[1,1,128,1024]{3,2,1,0:T(8,128)(2,1)}, u32[]{:S(2)}) copy-start(bf16[1,1,128,1024]{3,2,1,0:T(8,128)(2,1)} %param.8) | copy-start | bytes 786436
  53.2 114.0 %all-to-all-start.1 = ((bf16[16,64,1024]{2,1,0:T(8,128)(2,1)}), bf16[16,64,1024]{2,1,0:T(8,128)(2,1)}, u32[]{:S(2)}, u32[]{:S(2)}) async-start(bf16[16,64,1024]{2,1,0:T(8,128)(2,1)} %broadcast_select_fusion), calls=%async_computation.1 | async-start | bytes 4194304 | tf_op jit(solution)/shard_map/all_to_all | solution.py:51
  60.8 286.3 %reduce-scatter.4.cloned.1.call-start = ((), (), s32[]{:S(2)}) async-start(), calls=%async_computation.3 | async-start | bytes 2228224
  60.8 38.4 %collective-permute-start = (bf16[128,1024]{1,0:T(8,128)(2,1)S(1)}, bf16[128,1024]{1,0:T(8,128)(2,1)S(1)}, u32[]{:S(2)}, u32[]{:S(2)}) collective-permute-start(bf16[128,1024]{1,0:T(8,128)(2,1)S(1)} %bitcast.79), channel_id=1, source_target_pairs={{0,48},{48,96},{96,144},{144,192},{192,240},{240,288},{288,336},{3... | collective-permute-start | bytes 786440 | tf_op jit(solution)/shard_map/ppermute | solution.py:11
  99.2 46.8 %copy-start.5 = (bf16[128,1024]{1,0:T(8,128)(2,1)}, bf16[128,1024]{1,0:T(8,128)(2,1)S(1)}, u32[]{:S(2)}) copy-start(bf16[128,1024]{1,0:T(8,128)(2,1)S(1)} %collective-permute-done) | copy-start | bytes 786436
  99.2 44.4 %collective-permute-start.1 = (bf16[128,1024]{1,0:T(8,128)(2,1)S(1)}, bf16[128,1024]{1,0:T(8,128)(2,1)}, u32[]{:S(2)}, u32[]{:S(2)}) collective-permute-start(bf16[128,1024]{1,0:T(8,128)(2,1)S(1)} %collective-permute-done), channel_id=1, source_target_pairs={{0,48},{48,96},{96,144},{144,192},{192,240},{240,288},{288,336},{3... | collective-permute-start | bytes 786440 | tf_op jit(solution)/shard_map/ppermute | solution.py:11
  143.6 21.3 %collective-permute-start.2 = (bf16[128,1024]{1,0:T(8,128)(2,1)}, bf16[128,1024]{1,0:T(8,128)(2,1)S(1)}, u32[]{:S(2)}, u32[]{:S(2)}) collective-permute-start(bf16[128,1024]{1,0:T(8,128)(2,1)} %collective-permute-done.1), channel_id=1, source_target_pairs={{0,48},{48,96},{96,144},{144,192},{192,240},{240,288},{288,336},{3... | collective-permute-start | bytes 786440 | tf_op jit(solution)/shard_map/ppermute | solution.py:11
  164.9 0.7 copy-start.6
  178.5 3.3 copy-start.2
  181.8 2.9 copy-start.3
  192.8 19.5 %collective-permute-start.3 = (bf16[128,1024]{1,0:T(8,128)(2,1)S(1)}, bf16[128,1024]{1,0:T(8,128)(2,1)S(1)}, u32[]{:S(2)}, u32[]{:S(2)}) collective-permute-start(bf16[128,1024]{1,0:T(8,128)(2,1)S(1)} %get-tuple-element.20), channel_id=1, source_target_pairs={{0,720},{48,0},{96,48},{144,96},{192,144},{240,192},{288,240},{336... | collective-permute-start | bytes 786440 | tf_op jit(solution)/shard_map/ppermute | solution.py:11
  194.8 17.6 %collective-permute-start.4 = (bf16[128,1024]{1,0:T(8,128)(2,1)S(1)}, bf16[128,1024]{1,0:T(8,128)(2,1)S(1)}, u32[]{:S(2)}, u32[]{:S(2)}) collective-permute-start(bf16[128,1024]{1,0:T(8,128)(2,1)S(1)} %get-tuple-element.22), channel_id=1, source_target_pairs={{0,672},{48,720},{96,0},{144,48},{192,96},{240,144},{288,192},{336... | collective-permute-start | bytes 786440 | tf_op jit(solution)/shard_map/ppermute | solution.py:11
  196.7 19.8 %collective-permute-start.5 = (bf16[128,1024]{1,0:T(8,128)(2,1)S(1)}, bf16[128,1024]{1,0:T(8,128)(2,1)S(1)}, u32[]{:S(2)}, u32[]{:S(2)}) collective-permute-start(bf16[128,1024]{1,0:T(8,128)(2,1)S(1)} %get-tuple-element.21), channel_id=1, source_target_pairs={{0,624},{48,672},{96,720},{144,0},{192,48},{240,96},{288,144},{336... | collective-permute-start | bytes 786440 | tf_op jit(solution)/shard_map/ppermute | solution.py:11
Sparse Core Ops, SparseCore 0:
  192.3 154.7 reduce-scatter.3
where the time goes:
time: 569 us
  blocking collectives  236 us (41%)
  waiting for transfers between devices  230 us (40%)
  local copies, waits for them, and re-layouts  33.5 us (6%)
  starting transfers between devices  32.8 us (6%)
  between operations  14.3 us (3%)
  matrix products  13.3 us (2%)
  other arithmetic  8.68 us (2%)
    psum x1, blocking collectives, local(): weight_grad = lax.psum(group_share, 'grp')  213 us
    unnamed x2, waiting for transfers between devices  130 us
    ppermute x6, waiting for transfers between devices, shifted(): return lax.ppermute(x, axis, [(i, (i + by) % count) for i in range(count)])  99.8 us
    ppermute x6, starting transfers between devices, shifted(): return lax.ppermute(x, axis, [(i, (i + by) % count) for i in range(count)])  25.2 us
    all_to_all x1, blocking collectives, local(): lax.all_to_all(request, 'blk', split_axis=0, concat_axis=0, tiled=True)  23.8 us
  transfers between devices with their start and end apart: 8, of which 5 were waited for; matrix products, arithmetic and copies ran while one was open for 1% of the time, Pallas kernels for 0%

commit v1 on v0

v1 whole, which is shorter than its diff:
```python
import jax
import jax.numpy as jnp
from jax import lax
from jax.experimental import pallas as pl
from jax.experimental.pallas import tpu as pltpu
from jax.sharding import Mesh, PartitionSpec as P

STOPS = 4
NEG = 7
CAP = 64
ROWS = 128
D = 1024
Z_HI, X, Y, Z_LO, CORE = 4, 4, 8, 3, 2
MEMBERS = Z_HI * X
SLOTS = MEMBERS * CAP
BLK = ("zh", "x")
GRP = ("y", "zl", "c")
F32 = jnp.float32
BF16 = jnp.bfloat16
VMEM_LIMIT = 40 * 1024 * 1024


def call(kernel, out_shape, *, flops=0, moved=0):
    return pl.pallas_call(
        kernel,
        out_shape=out_shape,
        compiler_params=pltpu.CompilerParams(vmem_limit_bytes=VMEM_LIMIT),
        cost_estimate=pl.CostEstimate(flops=flops, bytes_accessed=moved, transcendentals=0),
    )


def dot(left, right, on):
    return lax.dot_general(left, right, ((on[:1], on[1:]), ((), ())), preferred_element_type=F32)


def plan_kernel(owner_ref, slot_ref, count_ref, request_ref, mask_ref):
    owner = owner_ref[...]
    lane = lax.broadcasted_iota(jnp.int32, (ROWS, 128), 1)
    lane_owner, lane_j = lane % MEMBERS, lane // MEMBERS
    spread = jnp.full((ROWS, 128), -1, jnp.int32)
    for j in range(NEG):
        spread = jnp.where(lane_j == j, owner[:, j : j + 1], spread)
    named = (spread == lane_owner).astype(F32)
    row = lax.broadcasted_iota(jnp.int32, (ROWS, ROWS), 0)
    earlier = (lax.broadcasted_iota(jnp.int32, (ROWS, ROWS), 1) < row).astype(BF16)
    before = dot(earlier, named.astype(BF16), (1, 0))
    totals = jnp.broadcast_to(jnp.sum(named, axis=0, keepdims=True), (8, 128))
    src = lax.broadcasted_iota(jnp.int32, (128, 128), 0)
    dst = lax.broadcasted_iota(jnp.int32, (128, 128), 1)
    lower = (src % MEMBERS == dst % MEMBERS) & (src // MEMBERS < dst // MEMBERS)
    base = dot(totals.astype(BF16), lower.astype(F32).astype(BF16), (1, 0))[:1]
    place = named * (before + base + (lane_owner * CAP).astype(F32))
    slot = slot_ref[...]
    count = count_ref[...]
    column = lax.broadcasted_iota(jnp.int32, (ROWS, SLOTS), 1)
    wanted = jnp.zeros((ROWS, SLOTS), jnp.int32)
    used = jnp.zeros((ROWS, SLOTS), F32)
    for j in range(NEG):
        placed = jnp.sum(jnp.where(lane_j == j, place, 0.0), axis=1, keepdims=True).astype(jnp.int32)
        match = column == placed
        wanted = wanted + jnp.where(match, slot[:, j : j + 1], 0)
        live = (j < count).astype(F32)
        used = used + jnp.where(match, live, 0.0)
    mask_ref[...] = used.astype(BF16)
    request = jnp.sum(wanted, axis=0, keepdims=True)
    for owner_at in range(MEMBERS):
        request_ref[owner_at] = request[:, owner_at * CAP : (owner_at + 1) * CAP]


def serve_kernel(incoming_ref, store_ref, served_ref):
    pool = store_ref.shape[0]
    group = 4
    for at in range(0, MEMBERS, group):
        wanted = jnp.concatenate([incoming_ref[at + k] for k in range(group)], axis=1)
        row = lax.broadcasted_iota(jnp.int32, (pool, group * CAP), 0)
        pick = (row == wanted).astype(F32).astype(BF16)
        rows = dot(pick, store_ref[...], (0, 0)).astype(BF16)
        served_ref[at : at + group] = rows.reshape(group, CAP, D)


def attend_kernel(
    queries_ref, scores_ref, mask_ref, positive_ref, blocks_ref, replies_ref, batch_ref, query_ref
):
    factor = D**-0.5
    batch_scores = scores_ref[...]
    neg_scores = dot(queries_ref[...], replies_ref[...], (1, 1)) * factor
    neg_scores = jnp.where(mask_ref[...].astype(F32) > 0.5, neg_scores, -jnp.inf)
    top = jnp.maximum(
        jnp.max(batch_scores, axis=1, keepdims=True), jnp.max(neg_scores, axis=1, keepdims=True)
    )
    batch_exp = jnp.exp(batch_scores - top)
    neg_exp = jnp.exp(neg_scores - top)
    total = jnp.sum(batch_exp, axis=1, keepdims=True) + jnp.sum(neg_exp, axis=1, keepdims=True)
    column = lax.broadcasted_iota(jnp.int32, (ROWS, STOPS * ROWS), 1)
    hit = (column == positive_ref[...]).astype(F32)
    batch_grad = (batch_exp / total - hit).astype(BF16)
    neg_grad = (neg_exp / total).astype(BF16)
    batch_ref[...] = batch_grad
    inner = dot(batch_grad, blocks_ref[...], (1, 0)) + dot(neg_grad, replies_ref[...], (1, 0))
    query_ref[...] = (factor * inner).astype(BF16)


def around(x, axis, by):
    count = lax.axis_size(axis)
    return lax.ppermute(x, axis, [(i, (i + by) % count) for i in range(count)])


def swap(x, axis):
    return lax.all_to_all(x, axis, split_axis=0, concat_axis=0, tiled=True)


def local(query_states, passages, proj_weight, neg_store, positive, neg_owner, neg_slot, neg_count):
    factor = D**-0.5
    states = query_states.reshape(ROWS, D)
    own = passages.reshape(ROWS, D)
    store = neg_store.reshape(-1, D)
    x_at = lax.axis_index("x")

    request, mask = call(
        plan_kernel,
        (
            jax.ShapeDtypeStruct((MEMBERS, 1, CAP), jnp.int32),
            jax.ShapeDtypeStruct((ROWS, SLOTS), BF16),
        ),
        moved=1 << 20,
    )(neg_owner.reshape(ROWS, NEG), neg_slot.reshape(ROWS, NEG), neg_count.reshape(ROWS, 1))
    incoming = swap(request, BLK)
    served = call(
        serve_kernel,
        jax.ShapeDtypeStruct((MEMBERS, CAP, D), BF16),
        flops=2 * SLOTS * store.shape[0] * D,
        moved=3 << 20,
    )(incoming, store)
    replies = swap(served, BLK).reshape(SLOTS, D)

    queries = jnp.dot(states, proj_weight, preferred_element_type=F32).astype(BF16)
    below = around(own, "zh", 1)
    above = around(queries, "zh", -1)
    target = jnp.arange(X, dtype=jnp.int32)[:, None, None]
    to_row = jnp.concatenate(
        [
            jnp.where(target >= x_at, own[None], below[None]),
            jnp.where(target <= x_at, queries[None], above[None]),
        ],
        axis=1,
    )
    from_row = swap(to_row, "x")
    blocks = [own]
    asking = [queries]
    for stop in range(1, STOPS):
        blocks.append(lax.dynamic_index_in_dim(from_row, (x_at - stop) % X, 0, False)[:ROWS])
        asking.append(lax.dynamic_index_in_dim(from_row, (x_at + stop) % X, 0, False)[ROWS:])
    blocks = jnp.concatenate(blocks, axis=0)
    asking = jnp.concatenate(asking, axis=0)
    scores = dot(queries, blocks, (1, 1)) * factor

    quarter = states.reshape(ROWS, Z_HI, X, D // MEMBERS)
    quarter = quarter.transpose(2, 0, 1, 3).reshape(X, 1, ROWS, D // X)
    quarter = jnp.broadcast_to(quarter, (X, CORE, ROWS, D // X)).reshape(X * CORE, ROWS, D // X)
    row_states = swap(quarter, ("x", "c")).reshape(X * CORE * ROWS, D // X)

    batch_grad, query_grad = call(
        attend_kernel,
        (
            jax.ShapeDtypeStruct((ROWS, STOPS * ROWS), BF16),
            jax.ShapeDtypeStruct((ROWS, D), BF16),
        ),
        flops=2 * ROWS * D * (2 * SLOTS + STOPS * ROWS),
        moved=4 << 20,
    )(queries, scores, mask, positive.reshape(ROWS, 1), blocks, replies)

    half = query_grad.reshape(ROWS, CORE, D // CORE).transpose(1, 0, 2)[None]
    half = jnp.broadcast_to(half, (X, CORE, ROWS, D // CORE)).reshape(X * CORE, ROWS, D // CORE)
    row_grads = swap(half, ("x", "c")).reshape(X * CORE * ROWS, D // CORE)

    pieces = [batch_grad[:, :ROWS]]
    for stop in range(1, STOPS):
        piece = batch_grad[:, stop * ROWS : (stop + 1) * ROWS]
        pieces.append(
            lax.ppermute(
                piece, BLK, [(i, (i - stop) % MEMBERS) for i in range(MEMBERS)]
            )
        )
    passage_grads = factor * dot(jnp.concatenate(pieces, axis=0), asking, (0, 0))
    state_grads = dot(query_grad, proj_weight, (1, 1))

    part = dot(row_states, row_grads, (0, 0)).astype(BF16)
    part = swap(part.reshape(Z_HI * Y, D // MEMBERS // Y, D // CORE), ("zh", "y"))
    part = jnp.sum(part.astype(F32), axis=0).astype(BF16)
    parts = swap(jnp.broadcast_to(part[None], (Y * Z_LO * CORE,) + part.shape), GRP)
    parts = parts.reshape(Y, Z_LO, CORE, D // MEMBERS // Y, D // CORE)
    weight_grad = jnp.sum(parts.astype(F32), axis=1).transpose(0, 2, 1, 3)
    return (
        state_grads.astype(BF16).reshape(query_states.shape),
        passage_grads.astype(BF16).reshape(passages.shape),
        weight_grad.reshape(D // MEMBERS, D),
    )


def solution(mesh):
    fine = Mesh(mesh.devices.reshape(Z_HI, X, Y, Z_LO, CORE), ("zh", "x", "y", "zl", "c"))
    placed = (
        P(BLK, GRP, None, None),
        P(BLK, GRP, None, None),
        P(),
        P(BLK, GRP, None, None),
        P(BLK, GRP, None),
        P(BLK, GRP, None, None),
        P(BLK, GRP, None, None),
        P(BLK, GRP, None),
    )
    return jax.shard_map(
        local,
        mesh=fine,
        in_specs=placed,
        out_specs=(P(BLK, GRP, None, None), P(BLK, GRP, None, None), P(BLK, None)),
        check_vma=False,
    )
```

time: 569 us -> 246 us (0.43)
  the two profiles are of different devices: /device:TPU:192 before, /device:TPU:1 now
where the time goes in v1:
time: 246 us; the launch traced here: 244 us
  blocking collectives  83 us (34%)
  waiting for transfers between devices  69 us (28%)
  starting transfers between devices  63.9 us (26%)
  local copies, waits for them, and re-layouts  9.24 us (4%)
  Pallas kernels  6.78 us (3%)
  matrix products  5.94 us (2%)
  other arithmetic  4.7 us (2%)
    all_to_all x2, blocking collectives, swap(): return lax.all_to_all(x, axis, split_axis=0, concat_axis=0, tiled=True)  83 us
    all_to_all x5, waiting for transfers between devices, swap(): return lax.all_to_all(x, axis, split_axis=0, concat_axis=0, tiled=True)  63.7 us
    all_to_all x5, starting transfers between devices, swap(): return lax.all_to_all(x, axis, split_axis=0, concat_axis=0, tiled=True)  37.5 us
    ppermute x2, starting transfers between devices, around(): return lax.ppermute(x, axis, [(i, (i + by) % count) for i in range(count)])  17 us
    ppermute x3, starting transfers between devices, local(): lax.ppermute(piece, BLK, [(i, (i - stop) % MEMBERS) for i in range(MEMBER...  9.29 us
  transfers between devices with their start and end apart: 10, of which 6 were waited for; matrix products, arithmetic and copies ran while one was open for 4% of the time, Pallas kernels for 3%

profile of v1, /device:TPU:1, one launch (start us, length us, event | category | flops | bytes accessed | tf_op | source)
XLA Modules:
  0.0 243.5 jit_solution(11542451619032831199)
XLA Ops:
  0.7 1.5 copy-done
  2.2 1.4 convolution_convert_fusion.1.queries_ref
  3.6 15.1 %collective-permute-start.1 = (bf16[128,1024]{1,0:T(8,128)(2,1)S(1)}, bf16[128,1024]{1,0:T(8,128)(2,1)}, u32[]{:S(2)}, u32[]{:S(2)}) collective-permute-start(bf16[128,1024]{1,0:T(8,128)(2,1)S(1)} %convolution_convert_fusion.1.queries_ref), channel_id=1, source_target_pairs={{0,576},{192,0},{384,192},{576,384},{1,577},{193,1},{385,193},{577... | collective-permute-start | bytes 786440 | tf_op jit(solution)/shard_map/ppermute | solution.py:105
  18.8 1.9 collective-permute-start
  21.2 2.2 shard_map.103
  23.4 8.9 %all-to-all-start.1 = ((s32[16,1,64]{2,1,0:T(1,128)}), s32[16,1,64]{2,1,0:T(1,128)S(1)}, u32[]{:S(2)}, u32[]{:S(2)}) async-start(s32[16,1,64]{2,1,0:T(1,128)} %get-tuple-element.8), calls=%async_computation.1 | async-start | bytes 16384 | tf_op jit(solution)/shard_map/all_to_all | solution.py:109
  32.3 2.6 %collective-permute-done.1 = bf16[128,1024]{1,0:T(8,128)(2,1)} collective-permute-done((bf16[128,1024]{1,0:T(8,128)(2,1)S(1)}, bf16[128,1024]{1,0:T(8,128)(2,1)}, u32[]{:S(2)}, u32[]{:S(2)}) %collective-permute-start.1) | collective-permute-done | bytes 262176 | tf_op jit(solution)/shard_map/ppermute | solution.py:105
  34.9 1.1 broadcast_select_fusion
  36.2 1.5 pad_maximum_fusion
  37.7 7.6 %all-to-all-done.1.incoming_ref = s32[16,1,64]{2,1,0:T(1,128)S(1)} async-done(((s32[16,1,64]{2,1,0:T(1,128)}), s32[16,1,64]{2,1,0:T(1,128)S(1)}, u32[]{:S(2)}, u32[]{:S(2)}) %all-to-all-start.1) | async-done | bytes 4128 | tf_op jit(solution)/shard_map/all_to_all | solution.py:109
  45.3 4.4 %all-to-all-start = ((bf16[4,256,1024]{2,1,0:T(8,128)(2,1)}), bf16[4,256,1024]{2,1,0:T(8,128)(2,1)}, u32[]{:S(2)}, u32[]{:S(2)}) async-start(bf16[4,256,1024]{2,1,0:T(8,128)(2,1)} %pad_maximum_fusion), calls=%async_computation | async-start | bytes 4194304 | tf_op jit(solution)/shard_map/all_to_all | solution.py:109
  49.8 1.2 copy-done.2
  51.0 1.3 shard_map.104
  52.4 1.3 copy-done.1
  53.7 21.8 %all-to-all-done = bf16[4,256,1024]{2,1,0:T(8,128)(2,1)} async-done(((bf16[4,256,1024]{2,1,0:T(8,128)(2,1)}), bf16[4,256,1024]{2,1,0:T(8,128)(2,1)}, u32[]{:S(2)}, u32[]{:S(2)}) %all-to-all-start) | async-done | bytes 2097184 | tf_op jit(solution)/shard_map/all_to_all | solution.py:109
  75.5 4.4 %all-to-all-start.2 = ((bf16[16,64,1024]{2,1,0:T(8,128)(2,1)}), bf16[16,64,1024]{2,1,0:T(8,128)(2,1)}, u32[]{:S(2)}, u32[]{:S(2)}) async-start(bf16[16,64,1024]{2,1,0:T(8,128)(2,1)} %copy-done.1), calls=%async_computation.2 | async-start | bytes 4194304 | tf_op jit(solution)/shard_map/all_to_all | solution.py:109
  80.4 2.4 dynamic-slice_bitcast_fusion.2
  82.8 29.7 %all-to-all-done.2 = bf16[16,64,1024]{2,1,0:T(8,128)(2,1)} async-done(((bf16[16,64,1024]{2,1,0:T(8,128)(2,1)}), bf16[16,64,1024]{2,1,0:T(8,128)(2,1)}, u32[]{:S(2)}, u32[]{:S(2)}) %all-to-all-start.2) | async-done | bytes 2097184 | tf_op jit(solution)/shard_map/all_to_all | solution.py:109
  113.4 12.0 %all-to-all-start.4 = ((bf16[8,128,256]{1,2,0:T(8,128)(2,1)}), bf16[8,128,256]{1,2,0:T(8,128)(2,1)}, u32[]{:S(2)}, u32[]{:S(2)}) async-start(bf16[8,128,256]{1,2,0:T(8,128)(2,1)} %bitcast.20), calls=%async_computation.4 | async-start | bytes 1048576 | tf_op jit(solution)/shard_map/all_to_all | solution.py:109
  125.4 1.1 pad_maximum_fusion.1.blocks_ref
  127.0 3.2 %shard_map.105 = (bf16[128,512]{1,0:T(8,128)(2,1)S(1)}, bf16[128,1024]{1,0:T(8,128)(2,1)S(1)}) custom-call(bf16[128,1024]{1,0:T(8,128)(2,1)S(1)} %convolution_convert_fusion.1.queries_ref, f32[128,512]{1,0:T(8,128)S(1)} %convolution_multiply_fusion.1.scores_ref, bf16[128,1024]{1,0:T(8,128)(2,1)S(1)} %get-tuple-element.7.mask_ref, ...), custom_call_target="tpu_custom_call" | custom-call | flops 671088640 | bytes 4194304 | tf_op jit(solution)/shard_map/pallas_call | solution.py:162
  130.5 4.5 %all-to-all-done.4 = bf16[8,128,256]{1,2,0:T(8,128)(2,1)} async-done(((bf16[8,128,256]{1,2,0:T(8,128)(2,1)}), bf16[8,128,256]{1,2,0:T(8,128)(2,1)}, u32[]{:S(2)}, u32[]{:S(2)}) %all-to-all-start.4) | async-done | bytes 524320 | tf_op jit(solution)/shard_map/all_to_all | solution.py:109
  135.1 18.4 %all_to_all.35 = bf16[8,128,512]{2,1,0:T(8,128)(2,1)S(1)} all-to-all(bf16[8,128,512]{2,1,0:T(8,128)(2,1)S(1)} %bitcast.56), channel_id=1, replica_groups=mesh['zh'=4,'x'=4,'y'=8,'zl'=3,'c'=2] {'x','c'}, dimensions={0} | all-to-all | bytes 2097152 | tf_op jit(solution)/shard_map/all_to_all | solution.py:109
  153.4 1.5 fusion.3
  154.9 64.6 %all_to_all.36 = bf16[32,8,512]{2,1,0:T(8,128)(2,1)S(1)} all-to-all(bf16[32,8,512]{2,1,0:T(8,128)(2,1)S(1)} %fusion.3), channel_id=1, replica_groups=mesh['zh'=4,'x'=4,'y'=8,'zl'=3,'c'=2] {'zh','y'}, dimensions={0} | all-to-all | bytes 524288 | tf_op jit(solution)/shard_map/all_to_all | solution.py:109
  220.4 7.8 %all-to-all-start.6 = ((bf16[48,8,512]{2,1,0:T(8,128)(2,1)}), bf16[48,8,512]{2,1,0:T(8,128)(2,1)S(1)}, u32[]{:S(2)}, u32[]{:S(2)}) async-start(bf16[48,8,512]{2,1,0:T(8,128)(2,1)} %broadcast_in_dim.71), calls=%async_computation.6 | async-start | bytes 786432 | tf_op jit(solution)/shard_map/all_to_all | solution.py:109
  228.2 4.2 %collective-permute-start.2 = (bf16[128,128]{1,0:T(8,128)(2,1)S(1)}, bf16[128,128]{1,0:T(8,128)(2,1)S(1)}, u32[]{:S(2)}, u32[]{:S(2)}) collective-permute-start(bf16[128,128]{1,0:T(8,128)(2,1)S(1)} %get-tuple-element.20), channel_id=1, source_target_pairs={{0,720},{48,0},{96,48},{144,96},{192,144},{240,192},{288,240},{336... | collective-permute-start | bytes 98312 | tf_op jit(solution)/shard_map/ppermute | solution.py:180
  232.4 3.1 %collective-permute-start.3 = (bf16[128,128]{1,0:T(8,128)(2,1)S(1)}, bf16[128,128]{1,0:T(8,128)(2,1)S(1)}, u32[]{:S(2)}, u32[]{:S(2)}) collective-permute-start(bf16[128,128]{1,0:T(8,128)(2,1)S(1)} %get-tuple-element.19), channel_id=1, source_target_pairs={{0,672},{48,720},{96,0},{144,48},{192,96},{240,144},{288,192},{336... | collective-permute-start | bytes 98312 | tf_op jit(solution)/shard_map/ppermute | solution.py:180
  235.5 2.0 collective-permute-start.4
  237.5 1.5 fusion.2
  239.1 2.6 %collective-permute-done.4 = bf16[128,128]{1,0:T(8,128)(2,1)S(1)} collective-permute-done((bf16[128,128]{1,0:T(8,128)(2,1)S(1)}, bf16[128,128]{1,0:T(8,128)(2,1)S(1)}, u32[]{:S(2)}, u32[]{:S(2)}) %collective-permute-start.4) | collective-permute-done | bytes 32800 | tf_op jit(solution)/shard_map/ppermute | solution.py:180
  241.7 1.0 fusion.4
  (43 shorter events, 4.2 us)
Async XLA Ops:
  0.6 1.6 copy-start
  0.6 18.1 %copy-start.4 = (bf16[1,1,128,1024]{3,2,1,0:T(8,128)(2,1)S(1)}, bf16[1,1,128,1024]{3,2,1,0:T(8,128)(2,1)}, u32[]{:S(2)}) copy-start(bf16[1,1,128,1024]{3,2,1,0:T(8,128)(2,1)} %param.9) | copy-start | bytes 786436
  0.7 20.0 %copy-start.8 = (s32[1,1,896,1]{2,3,1,0:T(1,128)S(1)}, s32[1,1,896,1]{2,3,1,0:T(1,128)}, u32[]{:S(2)}) copy-start(s32[1,1,896,1]{2,3,1,0:T(1,128)} %param.13) | copy-start | bytes 10756
  0.7 20.3 %copy-start.9 = (s32[1,1,128,7]{2,1,3,0:T(1,128)S(1)}, s32[1,1,128,7]{2,1,3,0:T(1,128)}, u32[]{:S(2)}) copy-start(s32[1,1,128,7]{2,1,3,0:T(1,128)} %param.14) | copy-start | bytes 10756
  0.7 20.4 %copy-start.10 = (s32[1,1,128]{2,1,0:T(1,128)S(1)}, s32[1,1,128]{2,1,0:T(1,128)}, u32[]{:S(2)}) copy-start(s32[1,1,128]{2,1,0:T(1,128)} %param.15) | copy-start | bytes 1540
  3.6 31.3 %collective-permute-start.1 = (bf16[128,1024]{1,0:T(8,128)(2,1)S(1)}, bf16[128,1024]{1,0:T(8,128)(2,1)}, u32[]{:S(2)}, u32[]{:S(2)}) collective-permute-start(bf16[128,1024]{1,0:T(8,128)(2,1)S(1)} %convolution_convert_fusion.1.queries_ref), channel_id=1, source_target_pairs={{0,576},{192,0},{384,192},{576,384},{1,577},{193,1},{385,193},{577... | collective-permute-start | bytes 786440 | tf_op jit(solution)/shard_map/ppermute | solution.py:105
  18.8 17.3 %collective-permute-start = (bf16[128,1024]{1,0:T(8,128)(2,1)S(1)}, bf16[128,1024]{1,0:T(8,128)(2,1)S(1)}, u32[]{:S(2)}, u32[]{:S(2)}) collective-permute-start(bf16[128,1024]{1,0:T(8,128)(2,1)S(1)} %bitcast.61), channel_id=1, source_target_pairs={{0,192},{192,384},{384,576},{576,0},{1,193},{193,385},{385,577},{5... | collective-permute-start | bytes 786440 | tf_op jit(solution)/shard_map/ppermute | solution.py:105
  23.4 22.0 %all-to-all-start.1 = ((s32[16,1,64]{2,1,0:T(1,128)}), s32[16,1,64]{2,1,0:T(1,128)S(1)}, u32[]{:S(2)}, u32[]{:S(2)}) async-start(s32[16,1,64]{2,1,0:T(1,128)} %get-tuple-element.8), calls=%async_computation.1 | async-start | bytes 16384 | tf_op jit(solution)/shard_map/all_to_all | solution.py:109
  45.3 30.2 %all-to-all-start = ((bf16[4,256,1024]{2,1,0:T(8,128)(2,1)}), bf16[4,256,1024]{2,1,0:T(8,128)(2,1)}, u32[]{:S(2)}, u32[]{:S(2)}) async-start(bf16[4,256,1024]{2,1,0:T(8,128)(2,1)} %pad_maximum_fusion), calls=%async_computation | async-start | bytes 4194304 | tf_op jit(solution)/shard_map/all_to_all | solution.py:109
  49.8 1.2 copy-start.2
  52.4 1.3 copy-start.1
  53.7 26.3 %copy-start.3 = (bf16[1,1,128,1024]{3,2,1,0:T(8,128)(2,1)S(1)}, bf16[1,1,128,1024]{3,2,1,0:T(8,128)(2,1)}, u32[]{:S(2)}) copy-start(bf16[1,1,128,1024]{3,2,1,0:T(8,128)(2,1)} %param.8) | copy-start | bytes 786436
  53.7 26.5 %copy-start.11 = (s32[1,1,128]{2,1,0:T(1,128)S(1)}, s32[1,1,128]{2,1,0:T(1,128)}, u32[]{:S(2)}) copy-start(s32[1,1,128]{2,1,0:T(1,128)} %param.12) | copy-start | bytes 1540
  75.5 37.1 %all-to-all-start.2 = ((bf16[16,64,1024]{2,1,0:T(8,128)(2,1)}), bf16[16,64,1024]{2,1,0:T(8,128)(2,1)}, u32[]{:S(2)}, u32[]{:S(2)}) async-start(bf16[16,64,1024]{2,1,0:T(8,128)(2,1)} %copy-done.1), calls=%async_computation.2 | async-start | bytes 4194304 | tf_op jit(solution)/shard_map/all_to_all | solution.py:109
  113.4 21.6 %all-to-all-start.4 = ((bf16[8,128,256]{1,2,0:T(8,128)(2,1)}), bf16[8,128,256]{1,2,0:T(8,128)(2,1)}, u32[]{:S(2)}, u32[]{:S(2)}) async-start(bf16[8,128,256]{1,2,0:T(8,128)(2,1)} %bitcast.20), calls=%async_computation.4 | async-start | bytes 1048576 | tf_op jit(solution)/shard_map/all_to_all | solution.py:109
  219.6 22.1 %copy-start.5 = (bf16[128,1024]{1,0:T(8,128)(2,1)S(1)}, bf16[128,1024]{1,0:T(8,128)(2,1)}, u32[]{:S(2)}) copy-start(bf16[128,1024]{1,0:T(8,128)(2,1)} %get-tuple-element.11) | copy-start | bytes 786436
  220.4 22.4 %all-to-all-start.6 = ((bf16[48,8,512]{2,1,0:T(8,128)(2,1)}), bf16[48,8,512]{2,1,0:T(8,128)(2,1)S(1)}, u32[]{:S(2)}, u32[]{:S(2)}) async-start(bf16[48,8,512]{2,1,0:T(8,128)(2,1)} %broadcast_in_dim.71), calls=%async_computation.6 | async-start | bytes 786432 | tf_op jit(solution)/shard_map/all_to_all | solution.py:109
  228.2 13.6 %copy-start.6 = (bf16[128,1024]{1,0:T(8,128)(2,1)S(1)}, bf16[128,1024]{1,0:T(8,128)(2,1)}, u32[]{:S(2)}) copy-start(bf16[128,1024]{1,0:T(8,128)(2,1)} %get-tuple-element.12) | copy-start | bytes 786436
  228.2 13.5 %copy-start.7 = (bf16[128,1024]{1,0:T(8,128)(2,1)S(1)}, bf16[128,1024]{1,0:T(8,128)(2,1)}, u32[]{:S(2)}) copy-start(bf16[128,1024]{1,0:T(8,128)(2,1)} %get-tuple-element.13) | copy-start | bytes 786436
  228.2 10.9 %collective-permute-start.2 = (bf16[128,128]{1,0:T(8,128)(2,1)S(1)}, bf16[128,128]{1,0:T(8,128)(2,1)S(1)}, u32[]{:S(2)}, u32[]{:S(2)}) collective-permute-start(bf16[128,128]{1,0:T(8,128)(2,1)S(1)} %get-tuple-element.20), channel_id=1, source_target_pairs={{0,720},{48,0},{96,48},{144,96},{192,144},{240,192},{288,240},{336... | collective-permute-start | bytes 98312 | tf_op jit(solution)/shard_map/ppermute | solution.py:180
  232.4 6.6 %collective-permute-start.3 = (bf16[128,128]{1,0:T(8,128)(2,1)S(1)}, bf16[128,128]{1,0:T(8,128)(2,1)S(1)}, u32[]{:S(2)}, u32[]{:S(2)}) collective-permute-start(bf16[128,128]{1,0:T(8,128)(2,1)S(1)} %get-tuple-element.19), channel_id=1, source_target_pairs={{0,672},{48,720},{96,0},{144,48},{192,96},{240,144},{288,192},{336... | collective-permute-start | bytes 98312 | tf_op jit(solution)/shard_map/ppermute | solution.py:180
  235.5 6.2 %collective-permute-start.4 = (bf16[128,128]{1,0:T(8,128)(2,1)S(1)}, bf16[128,128]{1,0:T(8,128)(2,1)S(1)}, u32[]{:S(2)}, u32[]{:S(2)}) collective-permute-start(bf16[128,128]{1,0:T(8,128)(2,1)S(1)} %get-tuple-element.18), channel_id=1, source_target_pairs={{0,624},{48,672},{96,720},{144,0},{192,48},{240,96},{288,144},{336... | collective-permute-start | bytes 98312 | tf_op jit(solution)/shard_map/ppermute | solution.py:180

commit v2 on v1

--- a/solution.py
+++ b/solution.py
@@ -20,13 +20,19 @@
 VMEM_LIMIT = 40 * 1024 * 1024
 
 
-def call(kernel, out_shape, *, flops=0, moved=0):
-    return pl.pallas_call(
-        kernel,
-        out_shape=out_shape,
-        compiler_params=pltpu.CompilerParams(vmem_limit_bytes=VMEM_LIMIT),
-        cost_estimate=pl.CostEstimate(flops=flops, bytes_accessed=moved, transcendentals=0),
-    )
+def call(kernel, out_shape, *, scalars=0, flops=0, moved=0):
+    def run(*args):
+        specs = [pl.BlockSpec(memory_space=pltpu.SMEM)] * scalars
+        specs += [pl.BlockSpec(memory_space=pltpu.VMEM)] * (len(args) - scalars)
+        return pl.pallas_call(
+            kernel,
+            out_shape=out_shape,
+            in_specs=specs,
+            compiler_params=pltpu.CompilerParams(vmem_limit_bytes=VMEM_LIMIT),
+            cost_estimate=pl.CostEstimate(flops=flops, bytes_accessed=moved, transcendentals=0),
+        )(*args)
+
+    return run
 
 
 def dot(left, right, on):
@@ -79,7 +85,15 @@
 
 
 def attend_kernel(
-    queries_ref, scores_ref, mask_ref, positive_ref, blocks_ref, replies_ref, batch_ref, query_ref
+    queries_ref,
+    scores_ref,
+    mask_ref,
+    positive_ref,
+    blocks_ref,
+    replies_ref,
+    batch_ref,
+    query_ref,
+    halves_ref,
 ):
     factor = D**-0.5
     batch_scores = scores_ref[...]
@@ -97,7 +111,74 @@
     neg_grad = (neg_exp / total).astype(BF16)
     batch_ref[...] = batch_grad
     inner = dot(batch_grad, blocks_ref[...], (1, 0)) + dot(neg_grad, replies_ref[...], (1, 0))
-    query_ref[...] = (factor * inner).astype(BF16)
+    query_grad = (factor * inner).astype(BF16)
+    query_ref[...] = query_grad
+    for to in range(X * CORE):
+        at = to % CORE * (D // CORE)
+        halves_ref[to] = query_grad[:, at : at + D // CORE]
+
+
+def pack_kernel(place_ref, own_ref, below_ref, queries_ref, above_ref, states_ref, pair_ref, *refs):
+    x_at = place_ref[0]
+    share = D // MEMBERS
+
+    def columns(ref, x_to):
+        piece = None
+        for x_of in range(X):
+            cut = [ref[:, (z * X + x_of) * share :][:, :share] for z in range(Z_HI)]
+            cut = jnp.concatenate(cut, axis=1)
+            piece = cut if piece is None else jnp.where(x_to == x_of, cut, piece)
+        return piece
+
+    *send_refs, mine_ref = refs
+    mine_ref[0] = columns(states_ref, x_at)
+    mine_ref[1] = columns(pair_ref, x_at)
+    for step in range(1, X):
+        send_ref = send_refs[step - 1]
+        wraps = x_at + step >= X
+        send_ref[:, :D] = jnp.where(wraps, below_ref[...], own_ref[...])
+        send_ref[:, D : 2 * D] = jnp.where(wraps, queries_ref[...], above_ref[...])
+        x_to = (x_at + step) % X
+        send_ref[:, 2 * D : 2 * D + D // X] = columns(states_ref, x_to)
+        send_ref[:, 2 * D + D // X :] = columns(pair_ref, x_to)
+
+
+def scores_kernel(place_ref, own_ref, queries_ref, mine_ref, *refs):
+    *got_refs, blocks_ref, asking_ref, states_ref, scores_ref = refs
+    x_at, c_at = place_ref[0], place_ref[1]
+
+    def place(x_from, c_from, value):
+        at = pl.multiple_of((x_from * CORE + c_from) * ROWS, ROWS)
+        states_ref[pl.ds(at, ROWS), :] = value
+
+    blocks_ref[:ROWS] = own_ref[...]
+    asking_ref[:ROWS] = queries_ref[...]
+    place(x_at, c_at, mine_ref[0])
+    place(x_at, 1 - c_at, mine_ref[1])
+    for step in range(1, X):
+        got_ref = got_refs[step - 1]
+        blocks_ref[step * ROWS : (step + 1) * ROWS] = got_ref[:, :D]
+        asking_ref[(X - step) * ROWS : (X - step + 1) * ROWS] = got_ref[:, D : 2 * D]
+        x_from = (x_at + X - step) % X
+        place(x_from, c_at, got_ref[:, 2 * D : 2 * D + D // X])
+        place(x_from, 1 - c_at, got_ref[:, 2 * D + D // X :])
+    scores_ref[...] = dot(queries_ref[...], blocks_ref[...], (1, 1)) * (D**-0.5)
+
+
+def gather_kernel(parts_ref, out_ref):
+    total = parts_ref[0].astype(F32)
+    for at in range(1, Z_HI * Y):
+        total = total + parts_ref[at].astype(F32)
+    total = total.astype(BF16)
+    for to in range(Y * Z_LO * CORE):
+        out_ref[to] = total
+
+
+def part_kernel(states_ref, grads_ref, asking_ref, *refs):
+    *piece_refs, part_ref, passage_ref = refs
+    part_ref[...] = dot(states_ref[...], grads_ref[...], (0, 0)).astype(BF16)
+    pieces = jnp.concatenate([ref[...] for ref in piece_refs], axis=0)
+    passage_ref[...] = (D**-0.5 * dot(pieces, asking_ref[...], (0, 0))).astype(BF16)
 
 
 def around(x, axis, by):
@@ -114,7 +195,7 @@
     states = query_states.reshape(ROWS, D)
     own = passages.reshape(ROWS, D)
     store = neg_store.reshape(-1, D)
-    x_at = lax.axis_index("x")
+    place = jnp.stack([lax.axis_index("x"), lax.axis_index("c")]).astype(jnp.int32)
 
     request, mask = call(
         plan_kernel,
@@ -125,6 +206,12 @@
         moved=1 << 20,
     )(neg_owner.reshape(ROWS, NEG), neg_slot.reshape(ROWS, NEG), neg_count.reshape(ROWS, 1))
     incoming = swap(request, BLK)
+
+    queries = jnp.dot(states, proj_weight, preferred_element_type=F32).astype(BF16)
+    below = around(own, "zh", 1)
+    above = around(queries, "zh", -1)
+    pair = around(states, "c", 1)
+    incoming, below, above, pair = lax.optimization_barrier((incoming, below, above, pair))
     served = call(
         serve_kernel,
         jax.ShapeDtypeStruct((MEMBERS, CAP, D), BF16),
@@ -133,66 +220,67 @@
     )(incoming, store)
     replies = swap(served, BLK).reshape(SLOTS, D)
 
-    queries = jnp.dot(states, proj_weight, preferred_element_type=F32).astype(BF16)
-    below = around(own, "zh", 1)
-    above = around(queries, "zh", -1)
-    target = jnp.arange(X, dtype=jnp.int32)[:, None, None]
-    to_row = jnp.concatenate(
-        [
-            jnp.where(target >= x_at, own[None], below[None]),
-            jnp.where(target <= x_at, queries[None], above[None]),
-        ],
-        axis=1,
-    )
-    from_row = swap(to_row, "x")
-    blocks = [own]
-    asking = [queries]
-    for stop in range(1, STOPS):
-        blocks.append(lax.dynamic_index_in_dim(from_row, (x_at - stop) % X, 0, False)[:ROWS])
-        asking.append(lax.dynamic_index_in_dim(from_row, (x_at + stop) % X, 0, False)[ROWS:])
-    blocks = jnp.concatenate(blocks, axis=0)
-    asking = jnp.concatenate(asking, axis=0)
-    scores = dot(queries, blocks, (1, 1)) * factor
-
-    quarter = states.reshape(ROWS, Z_HI, X, D // MEMBERS)
-    quarter = quarter.transpose(2, 0, 1, 3).reshape(X, 1, ROWS, D // X)
-    quarter = jnp.broadcast_to(quarter, (X, CORE, ROWS, D // X)).reshape(X * CORE, ROWS, D // X)
-    row_states = swap(quarter, ("x", "c")).reshape(X * CORE * ROWS, D // X)
-
-    batch_grad, query_grad = call(
+    wide = jax.ShapeDtypeStruct((ROWS, 2 * D + CORE * (D // X)), BF16)
+    *sends, mine = call(
+        pack_kernel,
+        (wide,) * (X - 1) + (jax.ShapeDtypeStruct((CORE, ROWS, D // X), BF16),),
+        scalars=1,
+        moved=6 << 20,
+    )(place, own, below, queries, above, states, pair)
+    got = [around(send, "x", step + 1) for step, send in enumerate(sends)]
+    blocks, asking, row_states, scores = call(
+        scores_kernel,
+        (
+            jax.ShapeDtypeStruct((STOPS * ROWS, D), BF16),
+            jax.ShapeDtypeStruct((STOPS * ROWS, D), BF16),
+            jax.ShapeDtypeStruct((X * CORE * ROWS, D // X), BF16),
+            jax.ShapeDtypeStruct((ROWS, STOPS * ROWS), F32),
+        ),
+        scalars=1,
+        flops=2 * ROWS * D * STOPS * ROWS,
+        moved=6 << 20,
+    )(place, own, queries, mine, *got)
+
+    batch_grad, query_grad, halves = call(
         attend_kernel,
         (
             jax.ShapeDtypeStruct((ROWS, STOPS * ROWS), BF16),
             jax.ShapeDtypeStruct((ROWS, D), BF16),
+            jax.ShapeDtypeStruct((X * CORE, ROWS, D // CORE), BF16),
         ),
         flops=2 * ROWS * D * (2 * SLOTS + STOPS * ROWS),
         moved=4 << 20,
     )(queries, scores, mask, positive.reshape(ROWS, 1), blocks, replies)
-
-    half = query_grad.reshape(ROWS, CORE, D // CORE).transpose(1, 0, 2)[None]
-    half = jnp.broadcast_to(half, (X, CORE, ROWS, D // CORE)).reshape(X * CORE, ROWS, D // CORE)
-    row_grads = swap(half, ("x", "c")).reshape(X * CORE * ROWS, D // CORE)
+    row_grads = swap(halves, ("x", "c")).reshape(X * CORE * ROWS, D // CORE)
 
     pieces = [batch_grad[:, :ROWS]]
     for stop in range(1, STOPS):
         piece = batch_grad[:, stop * ROWS : (stop + 1) * ROWS]
         pieces.append(
-            lax.ppermute(
-                piece, BLK, [(i, (i - stop) % MEMBERS) for i in range(MEMBERS)]
-            )
+            lax.ppermute(piece, BLK, [(i, (i - stop) % MEMBERS) for i in range(MEMBERS)])
         )
-    passage_grads = factor * dot(jnp.concatenate(pieces, axis=0), asking, (0, 0))
+    part, passage_grads = call(
+        part_kernel,
+        (
+            jax.ShapeDtypeStruct((D // X, D // CORE), BF16),
+            jax.ShapeDtypeStruct((ROWS, D), BF16),
+        ),
+        flops=2 * ROWS * D * (STOPS * ROWS + D),
+        moved=4 << 20,
+    )(row_states, row_grads, asking, *pieces)
     state_grads = dot(query_grad, proj_weight, (1, 1))
 
-    part = dot(row_states, row_grads, (0, 0)).astype(BF16)
     part = swap(part.reshape(Z_HI * Y, D // MEMBERS // Y, D // CORE), ("zh", "y"))
-    part = jnp.sum(part.astype(F32), axis=0).astype(BF16)
-    parts = swap(jnp.broadcast_to(part[None], (Y * Z_LO * CORE,) + part.shape), GRP)
-    parts = parts.reshape(Y, Z_LO, CORE, D // MEMBERS // Y, D // CORE)
+    part = call(
+        gather_kernel,
+        jax.ShapeDtypeStruct((Y * Z_LO * CORE,) + part.shape[1:], BF16),
+        moved=1 << 20,
+    )(part)
+    parts = swap(part, GRP).reshape(Y, Z_LO, CORE, D // MEMBERS // Y, D // CORE)
     weight_grad = jnp.sum(parts.astype(F32), axis=1).transpose(0, 2, 1, 3)
     return (
         state_grads.astype(BF16).reshape(query_states.shape),
-        passage_grads.astype(BF16).reshape(passages.shape),
+        passage_grads.reshape(passages.shape),
         weight_grad.reshape(D // MEMBERS, D),
     )
 

time: 246 us -> 217 us (0.88)
  blocking collectives: 83 us -> 47.1 us
  waiting for transfers between devices: 69 us -> 54.2 us
  starting transfers between devices: 63.9 us -> 77.6 us
  local copies, waits for them, and re-layouts: 9.24 us -> 18.9 us
  Pallas kernels: 6.78 us -> 13.2 us
  other arithmetic: 4.7 us -> 0.85 us
  matrix products: 5.94 us -> 2.93 us
    all_to_all x5 -> x3, waiting for transfers between devices: 63.7 us -> 12.1 us  [swap(): return lax.all_to_all(x, axis, split_axis=0, concat_axis=0, tiled=True)]
    ppermute x2 -> x6, waiting for transfers between devices: 2.64 us -> 41.2 us  [around(): return lax.ppermute(x, axis, [(i, (i + by) % count) for i in range(count)])]
    all_to_all x2, blocking collectives: 83 us -> 47.1 us  [swap(): return lax.all_to_all(x, axis, split_axis=0, concat_axis=0, tiled=True)]
    ppermute x3, starting transfers between devices: 9.29 us -> 24.3 us  [local(): lax.ppermute(piece, BLK, [(i, (i - stop) % MEMBERS) for i in range(MEMBER...]
    all_to_all x5 -> x3, starting transfers between devices: 37.5 us -> 22.7 us  [swap(): return lax.all_to_all(x, axis, split_axis=0, concat_axis=0, tiled=True)]
    unnamed x26 -> x55, local copies, waits for them, and re-layouts: 4.42 us -> 18.5 us
    ppermute x2 -> x6, starting transfers between devices: 17 us -> 30.5 us  [around(): return lax.ppermute(x, axis, [(i, (i + by) % count) for i in range(count)])]
    pallas_call x3 -> x7, Pallas kernels: 6.78 us -> 13.2 us  [run(): pl.pallas_call(kernel, out_shape=out_shape, in_specs=specs, compiler_para...]
  transfers between devices with their start and end apart: 10 -> 12, of which waited for: 6 -> 5; matrix products, arithmetic and copies ran while one was open for 4% -> 1% of each run, Pallas kernels for 3% -> 3%
where the time goes in v2:
time: 217 us; the launch traced here: 216 us
  starting transfers between devices  77.6 us (36%)
  waiting for transfers between devices  54.2 us (25%)
  blocking collectives  47.1 us (22%)
  local copies, waits for them, and re-layouts  18.9 us (9%)
  Pallas kernels  13.2 us (6%)
  matrix products  2.93 us (1%)
    all_to_all x2, blocking collectives, swap(): return lax.all_to_all(x, axis, split_axis=0, concat_axis=0, tiled=True)  47.1 us
    ppermute x6, waiting for transfers between devices, around(): return lax.ppermute(x, axis, [(i, (i + by) % count) for i in range(count)])  41.2 us
    ppermute x6, starting transfers between devices, around(): return lax.ppermute(x, axis, [(i, (i + by) % count) for i in range(count)])  30.5 us
    ppermute x3, starting transfers between devices, local(): lax.ppermute(piece, BLK, [(i, (i - stop) % MEMBERS) for i in range(MEMBER...  24.3 us
    all_to_all x3, starting transfers between devices, swap(): return lax.all_to_all(x, axis, split_axis=0, concat_axis=0, tiled=True)  22.7 us
    unnamed x55, local copies, waits for them, and re-layouts  18.5 us
    pallas_call x7, Pallas kernels, run(): pl.pallas_call(kernel, out_shape=out_shape, in_specs=specs, compiler_para...  13.2 us
    all_to_all x3, waiting for transfers between devices, swap(): return lax.all_to_all(x, axis, split_axis=0, concat_axis=0, tiled=True)  12.1 us
  transfers between devices with their start and end apart: 12, of which 5 were waited for; matrix products, arithmetic and copies ran while one was open for 1% of the time, Pallas kernels for 3%

profile of v2, /device:TPU:1, one launch (start us, length us, event | category | flops | bytes accessed | tf_op | source)
XLA Modules:
  0.0 215.7 jit_solution(18400738927516056281)
XLA Ops:
  0.7 1.6 copy-done
  2.3 1.4 convolution_convert_fusion.1.queries_ref
  3.7 15.1 %collective-permute-start.1 = (bf16[128,1024]{1,0:T(8,128)(2,1)S(1)}, bf16[128,1024]{1,0:T(8,128)(2,1)S(1)}, u32[]{:S(2)}, u32[]{:S(2)}) collective-permute-start(bf16[128,1024]{1,0:T(8,128)(2,1)S(1)} %convolution_convert_fusion.1.queries_ref), channel_id=1, source_target_pairs={{0,576},{192,0},{384,192},{576,384},{1,577},{193,1},{385,193},{577... | collective-permute-start | bytes 786440 | tf_op jit(solution)/shard_map/ppermute | solution.py:186
  18.8 1.9 collective-permute-start
  20.8 3.0 %collective-permute-start.2 = (bf16[128,1024]{1,0:T(8,128)(2,1)S(1)}, bf16[128,1024]{1,0:T(8,128)(2,1)}, u32[]{:S(2)}, u32[]{:S(2)}) collective-permute-start(bf16[128,1024]{1,0:T(8,128)(2,1)S(1)} %bitcast.25), channel_id=1, source_target_pairs={{0,1},{1,0},{2,3},{3,2},{4,5},{5,4},{6,7},{7,6},{8,9},{9,8},{10,11... | collective-permute-start | bytes 786440 | tf_op jit(solution)/shard_map/ppermute | solution.py:186
  24.3 1.6 shard_map.103
  26.6 20.0 %all_to_all.25.incoming_ref = s32[16,1,64]{2,1,0:T(1,128)S(1)} all-to-all(s32[16,1,64]{2,1,0:T(1,128)S(1)} %get-tuple-element.22), channel_id=1, replica_groups=mesh['zh'=4,'x'=4,'y'=8,'zl'=3,'c'=2] {'zh','x'}, dimensions={0} | all-to-all | bytes 8192 | tf_op jit(solution)/shard_map/all_to_all | solution.py:190
  46.6 1.2 copy-done.22
  47.8 1.3 shard_map.106
  49.2 1.3 copy-done.1
  50.5 4.6 %all-to-all-start.1 = ((bf16[16,64,1024]{2,1,0:T(8,128)(2,1)}), bf16[16,64,1024]{2,1,0:T(8,128)(2,1)}, u32[]{:S(2)}, u32[]{:S(2)}) async-start(bf16[16,64,1024]{2,1,0:T(8,128)(2,1)} %copy-done.1), calls=%async_computation.1 | async-start | bytes 4194304 | tf_op jit(solution)/shard_map/all_to_all | solution.py:190
  55.2 3.0 %shard_map.104 = (bf16[128,2560]{1,0:T(8,128)(2,1)}, bf16[128,2560]{1,0:T(8,128)(2,1)}, bf16[128,2560]{1,0:T(8,128)(2,1)}, bf16[2,128,256]{2,1,0:T(8,128)(2,1)S(1)}) custom-call(s32[2]{0:T(128)S(1)} %pad_add_fusion.place_ref, bf16[128,1024]{1,0:T(8,128)(2,1)S(1)} %bitcast.28, bf16[128,1024]{1,0:T(8,128)(2,1)} %collective-permute-done.below_ref, ...), custom_call_target="tpu_custom_call" | custom-call | bytes 6291456 | tf_op jit(solution)/shard_map/pallas_call | solution.py:27
  58.8 3.1 %collective-permute-start.3 = (bf16[128,2560]{1,0:T(8,128)(2,1)}, bf16[128,2560]{1,0:T(8,128)(2,1)S(1)}, u32[]{:S(2)}, u32[]{:S(2)}) collective-permute-start(bf16[128,2560]{1,0:T(8,128)(2,1)} %get-tuple-element.27), channel_id=1, source_target_pairs={{0,48},{48,96},{96,144},{144,0},{1,49},{49,97},{97,145},{145,1},{2... | collective-permute-start | bytes 1966088 | tf_op jit(solution)/shard_map/ppermute | solution.py:186
  61.9 4.3 %collective-permute-start.4 = (bf16[128,2560]{1,0:T(8,128)(2,1)}, bf16[128,2560]{1,0:T(8,128)(2,1)}, u32[]{:S(2)}, u32[]{:S(2)}) collective-permute-start(bf16[128,2560]{1,0:T(8,128)(2,1)} %get-tuple-element.28), channel_id=1, source_target_pairs={{0,96},{48,144},{96,0},{144,48},{1,97},{49,145},{97,1},{145,49},{2... | collective-permute-start | bytes 1966088 | tf_op jit(solution)/shard_map/ppermute | solution.py:186
  66.2 3.1 %collective-permute-start.5 = (bf16[128,2560]{1,0:T(8,128)(2,1)}, bf16[128,2560]{1,0:T(8,128)(2,1)}, u32[]{:S(2)}, u32[]{:S(2)}) collective-permute-start(bf16[128,2560]{1,0:T(8,128)(2,1)} %get-tuple-element.29), channel_id=1, source_target_pairs={{0,144},{48,0},{96,48},{144,96},{1,145},{49,1},{97,49},{145,97},{2... | collective-permute-start | bytes 1966088 | tf_op jit(solution)/shard_map/ppermute | solution.py:186
  69.4 22.3 %collective-permute-done.3.refs_0_ = bf16[128,2560]{1,0:T(8,128)(2,1)S(1)} collective-permute-done((bf16[128,2560]{1,0:T(8,128)(2,1)}, bf16[128,2560]{1,0:T(8,128)(2,1)S(1)}, u32[]{:S(2)}, u32[]{:S(2)}) %collective-permute-start.3) | collective-permute-done | bytes 655392 | tf_op jit(solution)/shard_map/ppermute | solution.py:186
  92.6 15.7 %collective-permute-done.4.refs_1_ = bf16[128,2560]{1,0:T(8,128)(2,1)} collective-permute-done((bf16[128,2560]{1,0:T(8,128)(2,1)}, bf16[128,2560]{1,0:T(8,128)(2,1)}, u32[]{:S(2)}, u32[]{:S(2)}) %collective-permute-start.4) | collective-permute-done | bytes 655392 | tf_op jit(solution)/shard_map/ppermute | solution.py:186
  108.3 3.2 %collective-permute-done.5.refs_2_ = bf16[128,2560]{1,0:T(8,128)(2,1)} collective-permute-done((bf16[128,2560]{1,0:T(8,128)(2,1)}, bf16[128,2560]{1,0:T(8,128)(2,1)}, u32[]{:S(2)}, u32[]{:S(2)}) %collective-permute-start.5) | collective-permute-done | bytes 655392 | tf_op jit(solution)/shard_map/ppermute | solution.py:186
  112.4 1.1 copy-done.9
  114.4 1.9 shard_map.105
  120.7 3.2 %shard_map.107 = (bf16[128,512]{1,0:T(8,128)(2,1)S(1)}, bf16[128,1024]{1,0:T(8,128)(2,1)S(1)}, bf16[8,128,512]{2,1,0:T(8,128)(2,1)S(1)}) custom-call(bf16[128,1024]{1,0:T(8,128)(2,1)S(1)} %convolution_convert_fusion.1.queries_ref, f32[128,512]{1,0:T(8,128)S(1)} %copy-done.17, bf16[128,1024]{1,0:T(8,128)(2,1)S(1)} %copy-done.15, ...), custom_call_target="tpu_custom_call" | custom-call | flops 671088640 | bytes 4194304 | tf_op jit(solution)/shard_map/pallas_call | solution.py:27
  126.3 6.2 %all-to-all-start.2 = ((bf16[8,128,512]{2,1,0:T(8,128)(2,1)}), bf16[8,128,512]{2,1,0:T(8,128)(2,1)S(1)}, u32[]{:S(2)}, u32[]{:S(2)}) async-start(bf16[8,128,512]{2,1,0:T(8,128)(2,1)} %copy-done.4), calls=%async_computation.2 | async-start | bytes 2097152 | tf_op jit(solution)/shard_map/all_to_all | solution.py:190
  132.6 7.5 %collective-permute-start.6 = (bf16[128,128]{1,0:T(8,128)(2,1)S(1)}, bf16[128,128]{1,0:T(8,128)(2,1)S(1)}, u32[]{:S(2)}, u32[]{:S(2)}) collective-permute-start(bf16[128,128]{1,0:T(8,128)(2,1)S(1)} %get-tuple-element.43), channel_id=1, source_target_pairs={{0,720},{48,0},{96,48},{144,96},{192,144},{240,192},{288,240},{336... | collective-permute-start | bytes 98312 | tf_op jit(solution)/shard_map/ppermute | solution.py:260
  140.1 2.5 %collective-permute-start.7 = (bf16[128,128]{1,0:T(8,128)(2,1)S(1)}, bf16[128,128]{1,0:T(8,128)(2,1)S(1)}, u32[]{:S(2)}, u32[]{:S(2)}) collective-permute-start(bf16[128,128]{1,0:T(8,128)(2,1)S(1)} %get-tuple-element.42), channel_id=1, source_target_pairs={{0,672},{48,720},{96,0},{144,48},{192,96},{240,144},{288,192},{336... | collective-permute-start | bytes 98312 | tf_op jit(solution)/shard_map/ppermute | solution.py:260
  142.6 14.4 %collective-permute-start.8 = (bf16[128,128]{1,0:T(8,128)(2,1)S(1)}, bf16[128,128]{1,0:T(8,128)(2,1)S(1)}, u32[]{:S(2)}, u32[]{:S(2)}) collective-permute-start(bf16[128,128]{1,0:T(8,128)(2,1)S(1)} %get-tuple-element.41), channel_id=1, source_target_pairs={{0,624},{48,672},{96,720},{144,0},{192,48},{240,96},{288,144},{336... | collective-permute-start | bytes 98312 | tf_op jit(solution)/shard_map/ppermute | solution.py:260
  158.0 1.2 copy-done.3
  159.2 1.0 copy-done.11
  160.2 1.3 shard_map.108
  161.6 27.1 %all_to_all.26.parts_ref = bf16[32,8,512]{2,1,0:T(8,128)(2,1)S(1)} all-to-all(bf16[32,8,512]{2,1,0:T(8,128)(2,1)S(1)} %bitcast.31), channel_id=1, replica_groups=mesh['zh'=4,'x'=4,'y'=8,'zl'=3,'c'=2] {'zh','y'}, dimensions={0} | all-to-all | bytes 524288 | tf_op jit(solution)/shard_map/all_to_all | solution.py:190
  189.5 11.9 %all-to-all-start.4 = ((bf16[48,8,512]{2,1,0:T(8,128)(2,1)}), bf16[48,8,512]{2,1,0:T(8,128)(2,1)S(1)}, u32[]{:S(2)}, u32[]{:S(2)}) async-start(bf16[48,8,512]{2,1,0:T(8,128)(2,1)} %shard_map.109), calls=%async_computation.4 | async-start | bytes 786432 | tf_op jit(solution)/shard_map/all_to_all | solution.py:190
  201.4 1.5 fusion
  202.9 12.0 %all-to-all-done.4 = bf16[48,8,512]{2,1,0:T(8,128)(2,1)S(1)} async-done(((bf16[48,8,512]{2,1,0:T(8,128)(2,1)}), bf16[48,8,512]{2,1,0:T(8,128)(2,1)S(1)}, u32[]{:S(2)}, u32[]{:S(2)}) %all-to-all-start.4) | async-done | bytes 393248 | tf_op jit(solution)/shard_map/all_to_all | solution.py:190
  (65 shorter events, 14.1 us)
Async XLA Ops:
  0.6 1.7 copy-start
  0.6 20.1 %copy-start.5 = (bf16[1,1,128,1024]{3,2,1,0:T(8,128)(2,1)S(1)}, bf16[1,1,128,1024]{3,2,1,0:T(8,128)(2,1)}, u32[]{:S(2)}) copy-start(bf16[1,1,128,1024]{3,2,1,0:T(8,128)(2,1)} %param.8) | copy-start | bytes 786436
  0.7 18.2 %copy-start.6 = (bf16[1,1,128,1024]{3,2,1,0:T(8,128)(2,1)S(1)}, bf16[1,1,128,1024]{3,2,1,0:T(8,128)(2,1)}, u32[]{:S(2)}) copy-start(bf16[1,1,128,1024]{3,2,1,0:T(8,128)(2,1)} %param.9) | copy-start | bytes 786436
  0.7 23.2 %copy-start.23 = (s32[1,1,896,1]{2,3,1,0:T(1,128)S(1)}, s32[1,1,896,1]{2,3,1,0:T(1,128)}, u32[]{:S(2)}) copy-start(s32[1,1,896,1]{2,3,1,0:T(1,128)} %param.13) | copy-start | bytes 10756
  0.7 23.4 %copy-start.24 = (s32[1,1,128,7]{2,1,3,0:T(1,128)S(1)}, s32[1,1,128,7]{2,1,3,0:T(1,128)}, u32[]{:S(2)}) copy-start(s32[1,1,128,7]{2,1,3,0:T(1,128)} %param.14) | copy-start | bytes 10756
  0.7 23.5 %copy-start.25 = (s32[1,1,128]{2,1,0:T(1,128)S(1)}, s32[1,1,128]{2,1,0:T(1,128)}, u32[]{:S(2)}) copy-start(s32[1,1,128]{2,1,0:T(1,128)} %param.15) | copy-start | bytes 1540
  3.7 42.9 %collective-permute-start.1 = (bf16[128,1024]{1,0:T(8,128)(2,1)S(1)}, bf16[128,1024]{1,0:T(8,128)(2,1)S(1)}, u32[]{:S(2)}, u32[]{:S(2)}) collective-permute-start(bf16[128,1024]{1,0:T(8,128)(2,1)S(1)} %convolution_convert_fusion.1.queries_ref), channel_id=1, source_target_pairs={{0,576},{192,0},{384,192},{576,384},{1,577},{193,1},{385,193},{577... | collective-permute-start | bytes 786440 | tf_op jit(solution)/shard_map/ppermute | solution.py:186
  18.8 27.8 %collective-permute-start = (bf16[128,1024]{1,0:T(8,128)(2,1)S(1)}, bf16[128,1024]{1,0:T(8,128)(2,1)}, u32[]{:S(2)}, u32[]{:S(2)}) collective-permute-start(bf16[128,1024]{1,0:T(8,128)(2,1)S(1)} %bitcast.27), channel_id=1, source_target_pairs={{0,192},{192,384},{384,576},{576,0},{1,193},{193,385},{385,577},{5... | collective-permute-start | bytes 786440 | tf_op jit(solution)/shard_map/ppermute | solution.py:186
  20.8 25.8 %collective-permute-start.2 = (bf16[128,1024]{1,0:T(8,128)(2,1)S(1)}, bf16[128,1024]{1,0:T(8,128)(2,1)}, u32[]{:S(2)}, u32[]{:S(2)}) collective-permute-start(bf16[128,1024]{1,0:T(8,128)(2,1)S(1)} %bitcast.25), channel_id=1, source_target_pairs={{0,1},{1,0},{2,3},{3,2},{4,5},{5,4},{6,7},{7,6},{8,9},{9,8},{10,11... | collective-permute-start | bytes 786440 | tf_op jit(solution)/shard_map/ppermute | solution.py:186
  46.6 1.2 copy-start.22
  49.2 1.3 copy-start.1
  50.5 18.8 %copy-start.26 = (s32[1,1,128]{2,1,0:T(1,128)S(1)}, s32[1,1,128]{2,1,0:T(1,128)}, u32[]{:S(2)}) copy-start(s32[1,1,128]{2,1,0:T(1,128)} %param.12) | copy-start | bytes 1540
  50.5 68.3 %all-to-all-start.1 = ((bf16[16,64,1024]{2,1,0:T(8,128)(2,1)}), bf16[16,64,1024]{2,1,0:T(8,128)(2,1)}, u32[]{:S(2)}, u32[]{:S(2)}) async-start(bf16[16,64,1024]{2,1,0:T(8,128)(2,1)} %copy-done.1), calls=%async_computation.1 | async-start | bytes 4194304 | tf_op jit(solution)/shard_map/all_to_all | solution.py:190
  58.8 32.9 %collective-permute-start.3 = (bf16[128,2560]{1,0:T(8,128)(2,1)}, bf16[128,2560]{1,0:T(8,128)(2,1)S(1)}, u32[]{:S(2)}, u32[]{:S(2)}) collective-permute-start(bf16[128,2560]{1,0:T(8,128)(2,1)} %get-tuple-element.27), channel_id=1, source_target_pairs={{0,48},{48,96},{96,144},{144,0},{1,49},{49,97},{97,145},{145,1},{2... | collective-permute-start | bytes 1966088 | tf_op jit(solution)/shard_map/ppermute | solution.py:186
  61.9 46.4 %collective-permute-start.4 = (bf16[128,2560]{1,0:T(8,128)(2,1)}, bf16[128,2560]{1,0:T(8,128)(2,1)}, u32[]{:S(2)}, u32[]{:S(2)}) collective-permute-start(bf16[128,2560]{1,0:T(8,128)(2,1)} %get-tuple-element.28), channel_id=1, source_target_pairs={{0,96},{48,144},{96,0},{144,48},{1,97},{49,145},{97,1},{145,49},{2... | collective-permute-start | bytes 1966088 | tf_op jit(solution)/shard_map/ppermute | solution.py:186
  66.2 45.2 %collective-permute-start.5 = (bf16[128,2560]{1,0:T(8,128)(2,1)}, bf16[128,2560]{1,0:T(8,128)(2,1)}, u32[]{:S(2)}, u32[]{:S(2)}) collective-permute-start(bf16[128,2560]{1,0:T(8,128)(2,1)} %get-tuple-element.29), channel_id=1, source_target_pairs={{0,144},{48,0},{96,48},{144,96},{1,145},{49,1},{97,49},{145,97},{2... | collective-permute-start | bytes 1966088 | tf_op jit(solution)/shard_map/ppermute | solution.py:186
  111.5 1.0 copy-start.7
  112.4 1.1 copy-start.9
  113.5 0.9 copy-start.19
  116.3 1.0 copy-start.2
  118.8 1.0 copy-start.15
  119.8 0.9 copy-start.17
  124.0 1.0 copy-start.4
  126.3 6.2 %copy-start.21 = (bf16[128,512]{1,0:T(8,128)(2,1)S(1)}, bf16[128,512]{1,0:T(8,128)(2,1)}, u32[]{:S(2)}) copy-start(bf16[128,512]{1,0:T(8,128)(2,1)} %copy-done.20) | copy-start | bytes 393220
  126.3 31.6 %all-to-all-start.2 = ((bf16[8,128,512]{2,1,0:T(8,128)(2,1)}), bf16[8,128,512]{2,1,0:T(8,128)(2,1)S(1)}, u32[]{:S(2)}, u32[]{:S(2)}) async-start(bf16[8,128,512]{2,1,0:T(8,128)(2,1)} %copy-done.4), calls=%async_computation.2 | async-start | bytes 2097152 | tf_op jit(solution)/shard_map/all_to_all | solution.py:190
  132.6 24.4 %collective-permute-start.6 = (bf16[128,128]{1,0:T(8,128)(2,1)S(1)}, bf16[128,128]{1,0:T(8,128)(2,1)S(1)}, u32[]{:S(2)}, u32[]{:S(2)}) collective-permute-start(bf16[128,128]{1,0:T(8,128)(2,1)S(1)} %get-tuple-element.43), channel_id=1, source_target_pairs={{0,720},{48,0},{96,48},{144,96},{192,144},{240,192},{288,240},{336... | collective-permute-start | bytes 98312 | tf_op jit(solution)/shard_map/ppermute | solution.py:260
  140.1 16.9 %collective-permute-start.7 = (bf16[128,128]{1,0:T(8,128)(2,1)S(1)}, bf16[128,128]{1,0:T(8,128)(2,1)S(1)}, u32[]{:S(2)}, u32[]{:S(2)}) collective-permute-start(bf16[128,128]{1,0:T(8,128)(2,1)S(1)} %get-tuple-element.42), channel_id=1, source_target_pairs={{0,672},{48,720},{96,0},{144,48},{192,96},{240,144},{288,192},{336... | collective-permute-start | bytes 98312 | tf_op jit(solution)/shard_map/ppermute | solution.py:260
  142.6 15.4 %collective-permute-start.8 = (bf16[128,128]{1,0:T(8,128)(2,1)S(1)}, bf16[128,128]{1,0:T(8,128)(2,1)S(1)}, u32[]{:S(2)}, u32[]{:S(2)}) collective-permute-start(bf16[128,128]{1,0:T(8,128)(2,1)S(1)} %get-tuple-element.41), channel_id=1, source_target_pairs={{0,624},{48,672},{96,720},{144,0},{192,48},{240,96},{288,144},{336... | collective-permute-start | bytes 98312 | tf_op jit(solution)/shard_map/ppermute | solution.py:260
  158.0 1.2 copy-start.3
  159.2 1.0 copy-start.11
  161.6 39.8 %copy-start.13 = (bf16[128,1024]{1,0:T(8,128)(2,1)S(1)}, bf16[128,1024]{1,0:T(8,128)(2,1)}, u32[]{:S(2)}) copy-start(bf16[128,1024]{1,0:T(8,128)(2,1)} %copy-done.12) | copy-start | bytes 786436
  189.5 25.5 %all-to-all-start.4 = ((bf16[48,8,512]{2,1,0:T(8,128)(2,1)}), bf16[48,8,512]{2,1,0:T(8,128)(2,1)S(1)}, u32[]{:S(2)}, u32[]{:S(2)}) async-start(bf16[48,8,512]{2,1,0:T(8,128)(2,1)} %shard_map.109), calls=%async_computation.4 | async-start | bytes 786432 | tf_op jit(solution)/shard_map/all_to_all | solution.py:190
  (7 other events, 5.1 us)

commit v3 on v2

v3 whole, which is shorter than its diff:
```python
import jax
import jax.numpy as jnp
from jax import lax
from jax.experimental import pallas as pl
from jax.experimental.pallas import tpu as pltpu
from jax.sharding import Mesh, PartitionSpec as P

STOPS = 4
NEG = 7
CAP = 64
ROWS = 128
D = 1024
Z_HI, X, Y, Z_LO, CORE = 4, 4, 8, 3, 2
MEMBERS = Z_HI * X
SLOTS = MEMBERS * CAP
BLK = ("zh", "x")
GRP = ("y", "zl", "c")
F32 = jnp.float32
BF16 = jnp.bfloat16
LARGE = 58
PARTS = 4


def whole(x):
    return pl.BlockSpec(x.shape, lambda i, rank=len(x.shape): (0,) * rank)


def call(kernel, out_shape, *, scalars=0, flops=0, moved=0, limit=16, **kwargs):
    def run(*args):
        if "grid" not in kwargs:
            specs = [pl.BlockSpec(memory_space=pltpu.SMEM)] * scalars
            specs += [whole(arg) for arg in args[scalars:]]
            outs = jax.tree.map(whole, out_shape)
            spec = {"grid": (1,), "in_specs": specs, "out_specs": outs} | kwargs
        else:
            spec = kwargs
        return pl.pallas_call(
            kernel,
            out_shape=out_shape,
            compiler_params=pltpu.CompilerParams(vmem_limit_bytes=limit * 1024 * 1024),
            cost_estimate=pl.CostEstimate(flops=flops, bytes_accessed=moved, transcendentals=0),
            **spec,
        )(*args)

    return run


def dot(left, right, on):
    return lax.dot_general(left, right, ((on[:1], on[1:]), ((), ())), preferred_element_type=F32)


def plan_kernel(owner_ref, slot_ref, count_ref, request_ref, used_ref):
    lanes = ROWS
    row8 = lax.broadcasted_iota(jnp.int32, (8, lanes), 0)
    lane8 = lax.broadcasted_iota(jnp.int32, (8, lanes), 1)
    row = lax.broadcasted_iota(jnp.int32, (lanes, lanes), 0)
    lane = lax.broadcasted_iota(jnp.int32, (lanes, lanes), 1)

    def bits(value):
        return value.astype(F32).astype(BF16)

    owner = jnp.zeros((8, lanes), F32)
    for at in range(NEG):
        flat = owner_ref[at : at + 1, :]
        kept = jnp.where((lane8 + at * lanes) % NEG == row8, flat, 0)
        owner = owner + dot(bits(kept), bits((row + at * lanes) // NEG == lane), (1, 0))
    owner = jnp.where(row8 < NEG, owner.astype(jnp.int32), -1)
    named = (jnp.concatenate([owner] * MEMBERS, axis=0) == row // 8).astype(F32)
    before = dot(bits(named), bits(row < lane), (1, 0))
    above = bits((row // 8 == lane // 8) & (row > lane))
    base = jnp.sum(dot(above, bits(named), (1, 0)), axis=1, keepdims=True)
    place = named * (before + base + (row // 8 * CAP).astype(F32))
    placed = place[:8]
    for at in range(1, MEMBERS):
        placed = placed + place[at * 8 : (at + 1) * 8]
    placed = placed.astype(jnp.int32)
    slot = slot_ref[...]
    live = (row8 < count_ref[...]).astype(F32)
    column = lax.broadcasted_iota(jnp.int32, (SLOTS, lanes), 0)
    wanted = jnp.zeros((SLOTS, lanes), jnp.int32)
    used = jnp.zeros((SLOTS, lanes), F32)
    for j in range(NEG):
        match = column == placed[j : j + 1]
        wanted = wanted + jnp.where(match, slot[j : j + 1], 0)
        used = used + jnp.where(match, live[j : j + 1], 0.0)
    used_ref[...] = used.astype(BF16)
    ones = jnp.ones((8, lanes), BF16)
    high = dot(ones, bits(wanted // 256), (1, 1))[:1]
    low = dot(ones, bits(wanted % 256), (1, 1))[:1]
    request = (high * 256.0 + low).astype(jnp.int32)
    for owner_at in range(MEMBERS):
        request_ref[owner_at] = request[:, owner_at * CAP : (owner_at + 1) * CAP]


def serve_kernel(incoming_ref, store_ref, served_hbm, rows_ref, sems):
    pool = store_ref.shape[0]
    group = MEMBERS // PARTS
    row = lax.broadcasted_iota(jnp.int32, (pool, group * CAP), 0)
    sends = []
    for at in range(PARTS):
        wanted = [incoming_ref[at * group + k] for k in range(group)]
        pick = (row == jnp.concatenate(wanted, axis=1)).astype(F32).astype(BF16)
        rows = dot(pick, store_ref[...], (0, 0)).astype(BF16)
        rows_ref[at] = rows.reshape(group, CAP, D)
        target = served_hbm.at[pl.ds(at * group, group)]
        sends.append(pltpu.make_async_copy(rows_ref.at[at], target, sems.at[at]))
        sends[-1].start()
    for send in sends:
        send.wait()


def attend_kernel(
    queries_ref,
    scores_ref,
    mask_ref,
    positive_ref,
    blocks_ref,
    replies_ref,
    batch_ref,
    query_ref,
    halves_ref,
):
    factor = D**-0.5
    batch_scores = scores_ref[...]
    neg_scores = dot(queries_ref[...], replies_ref[...], (1, 1)) * factor
    neg_scores = jnp.where(mask_ref[...].astype(F32) > 0.5, neg_scores, -jnp.inf)
    top = jnp.maximum(
        jnp.max(batch_scores, axis=1, keepdims=True), jnp.max(neg_scores, axis=1, keepdims=True)
    )
    batch_exp = jnp.exp(batch_scores - top)
    neg_exp = jnp.exp(neg_scores - top)
    total = jnp.sum(batch_exp, axis=1, keepdims=True) + jnp.sum(neg_exp, axis=1, keepdims=True)
    column = lax.broadcasted_iota(jnp.int32, (ROWS, STOPS * ROWS), 1)
    hit = (column == positive_ref[...]).astype(F32)
    batch_grad = (batch_exp / total - hit).astype(BF16)
    neg_grad = (neg_exp / total).astype(BF16)
    batch_ref[...] = batch_grad
    inner = dot(batch_grad, blocks_ref[...], (1, 0)) + dot(neg_grad, replies_ref[...], (1, 0))
    query_grad = (factor * inner).astype(BF16)
    query_ref[...] = query_grad
    for to in range(X * CORE):
        at = to % CORE * (D // CORE)
        halves_ref[to] = query_grad[:, at : at + D // CORE]


def pack_kernel(place_ref, own_ref, below_ref, above_ref, states_ref, *refs):
    x_at = place_ref[0]
    share = D // MEMBERS

    def columns(x_to):
        piece = None
        for x_of in range(X):
            cut = [states_ref[:, (z * X + x_of) * share :][:, :share] for z in range(Z_HI)]
            cut = jnp.concatenate(cut, axis=1)
            piece = cut if piece is None else jnp.where(x_to == x_of, cut, piece)
        return piece

    *send_refs, mine_ref = refs
    mine_ref[...] = columns(x_at)
    for step in range(1, X):
        send_ref = send_refs[step - 1]
        wraps = x_at + step >= X
        send_ref[:, :D] = jnp.where(wraps, below_ref[...], own_ref[...])
        send_ref[:, D : 2 * D] = jnp.where(wraps, states_ref[...], above_ref[...])
        send_ref[:, 2 * D :] = columns((x_at + step) % X)


def unpack_kernel(place_ref, own_ref, states_ref, mine_ref, *refs):
    *got_refs, blocks_ref, asking_ref, row_ref = refs
    x_at = place_ref[0]
    blocks_ref[:ROWS] = own_ref[...]
    asking_ref[:ROWS] = states_ref[...]
    row_ref[x_at] = mine_ref[...]
    for step in range(1, X):
        got_ref = got_refs[step - 1]
        blocks_ref[step * ROWS : (step + 1) * ROWS] = got_ref[:, :D]
        asking_ref[(X - step) * ROWS : (X - step + 1) * ROWS] = got_ref[:, D : 2 * D]
        row_ref[(x_at + X - step) % X] = got_ref[:, 2 * D :]


def gather_kernel(parts_ref, out_ref):
    total = parts_ref[0].astype(F32)
    for at in range(1, Z_HI * Y):
        total = total + parts_ref[at].astype(F32)
    total = total.astype(BF16)
    for to in range(Y * Z_LO * CORE):
        out_ref[to] = total


def part_kernel(place_ref, states_ref, pair_ref, grads_ref, part_ref, total_ref):
    at = pl.program_id(0)
    c_at = place_ref[1]
    states = jnp.concatenate([states_ref[0], pair_ref[0]], axis=0)
    grads = jnp.concatenate([grads_ref[c_at], grads_ref[1 - c_at]], axis=0)
    term = dot(states, grads, (0, 0))

    @pl.when(at == 0)
    def _():
        total_ref[...] = term

    @pl.when(at > 0)
    def _():
        total_ref[...] += term

    @pl.when(at == pl.num_programs(0) - 1)
    def _():
        part_ref[...] = total_ref[...].astype(BF16)


def passage_kernel(asking_ref, *refs):
    *piece_refs, passage_ref = refs
    pieces = jnp.concatenate([ref[...] for ref in piece_refs], axis=0)
    passage_ref[...] = (D**-0.5 * dot(pieces, asking_ref[...], (0, 0))).astype(BF16)


def around(x, axis, by):
    count = lax.axis_size(axis)
    return lax.ppermute(x, axis, [(i, (i + by) % count) for i in range(count)])


def swap(x, axis):
    return lax.all_to_all(x, axis, split_axis=0, concat_axis=0, tiled=True)


def local(query_states, passages, proj_weight, neg_store, positive, neg_owner, neg_slot, neg_count):
    factor = D**-0.5
    states = query_states.reshape(ROWS, D)
    own = passages.reshape(ROWS, D)
    store = neg_store.reshape(-1, D)
    place = jnp.stack([lax.axis_index(axis) for axis in ("x", "c", "zh")]).astype(jnp.int32)

    request, used = call(
        plan_kernel,
        (
            jax.ShapeDtypeStruct((MEMBERS, 1, CAP), jnp.int32),
            jax.ShapeDtypeStruct((SLOTS, ROWS), BF16),
        ),
        moved=1 << 20,
    )(neg_owner.reshape(NEG, ROWS), neg_slot.reshape(ROWS, NEG).T, neg_count.reshape(1, ROWS))
    mask = used.T
    incoming = swap(request, BLK)

    below = around(own, "zh", 1)
    above = around(states, "zh", -1)
    incoming = lax.optimization_barrier((incoming, below, above))[0]
    served = call(
        serve_kernel,
        jax.ShapeDtypeStruct((MEMBERS, CAP, D), BF16),
        flops=2 * SLOTS * store.shape[0] * D,
        moved=3 << 20,
        limit=LARGE,
        grid=(1,),
        in_specs=[
            pl.BlockSpec((MEMBERS, 1, CAP), lambda i: (0, 0, 0)),
            pl.BlockSpec(store.shape, lambda i: (0, 0)),
        ],
        out_specs=pl.BlockSpec(memory_space=pltpu.HBM),
        scratch_shapes=[
            pltpu.VMEM((PARTS, MEMBERS // PARTS, CAP, D), BF16),
            pltpu.SemaphoreType.DMA((PARTS,)),
        ],
    )(incoming, store)
    replies = swap(served, BLK).reshape(SLOTS, D)

    wide = jax.ShapeDtypeStruct((ROWS, 2 * D + D // X), BF16)
    *sends, mine = call(
        pack_kernel,
        (wide,) * (X - 1) + (jax.ShapeDtypeStruct((ROWS, D // X), BF16),),
        scalars=1,
        moved=6 << 20,
    )(place, own, below, above, states)
    got = [around(send, "x", step + 1) for step, send in enumerate(sends)]
    blocks, asking, row_states = call(
        unpack_kernel,
        (
            jax.ShapeDtypeStruct((STOPS * ROWS, D), BF16),
            jax.ShapeDtypeStruct((STOPS * ROWS, D), BF16),
            jax.ShapeDtypeStruct((X, ROWS, D // X), BF16),
        ),
        scalars=1,
        moved=6 << 20,
    )(place, own, states, mine, *got)
    pair_states = around(row_states, "c", 1)
    asking = jnp.dot(asking, proj_weight, preferred_element_type=F32).astype(BF16)
    queries = asking[:ROWS]
    scores = dot(queries, blocks, (1, 1)) * factor
    batch_grad, query_grad, halves = call(
        attend_kernel,
        (
            jax.ShapeDtypeStruct((ROWS, STOPS * ROWS), BF16),
            jax.ShapeDtypeStruct((ROWS, D), BF16),
            jax.ShapeDtypeStruct((X * CORE, ROWS, D // CORE), BF16),
        ),
        limit=LARGE,
        flops=2 * ROWS * D * (2 * SLOTS + STOPS * ROWS),
        moved=4 << 20,
    )(queries, scores, mask, positive.reshape(ROWS, 1), blocks, replies)
    row_grads = swap(halves, ("x", "c"))

    def to_owner(stop, batch):
        piece = batch[:, stop * ROWS : (stop + 1) * ROWS]
        return lax.ppermute(piece, BLK, [(i, (i - stop) % MEMBERS) for i in range(MEMBERS)])

    pieces = [batch_grad[:, :ROWS], to_owner(1, batch_grad)]
    row_grads = lax.optimization_barrier((row_grads, pieces[1]))[0]
    part = call(
        part_kernel,
        jax.ShapeDtypeStruct((D // X, D // CORE), BF16),
        limit=LARGE,
        flops=2 * ROWS * D * D,
        moved=2 << 20,
        grid=(X,),
        in_specs=[
            pl.BlockSpec(memory_space=pltpu.SMEM),
            pl.BlockSpec((1, ROWS, D // X), lambda i: (i, 0, 0)),
            pl.BlockSpec((1, ROWS, D // X), lambda i: (i, 0, 0)),
            pl.BlockSpec((CORE, ROWS, D // CORE), lambda i: (i, 0, 0)),
        ],
        out_specs=pl.BlockSpec((D // X, D // CORE), lambda i: (0, 0)),
        scratch_shapes=[pltpu.VMEM((D // X, D // CORE), F32)],
    )(place, row_states, pair_states, row_grads)
    pieces.append(to_owner(2, lax.optimization_barrier((batch_grad, part))[0]))
    state_grads = dot(query_grad, proj_weight, (1, 1))

    part = swap(part.reshape(Z_HI * Y, D // MEMBERS // Y, D // CORE), ("zh", "y"))
    part = lax.optimization_barrier((part, pieces[2]))[0]
    part = call(
        gather_kernel,
        jax.ShapeDtypeStruct((Y * Z_LO * CORE,) + part.shape[1:], BF16),
        limit=LARGE,
        moved=1 << 20,
    )(part)
    pieces.append(to_owner(3, lax.optimization_barrier((batch_grad, part))[0]))
    passage_grads = call(
        passage_kernel,
        jax.ShapeDtypeStruct((ROWS, D), BF16),
        flops=2 * ROWS * D * STOPS * ROWS,
        moved=2 << 20,
    )(asking, *pieces)

    parts = swap(part, GRP).reshape(Y, Z_LO, CORE, D // MEMBERS // Y, D // CORE)
    weight_grad = jnp.sum(parts.astype(F32), axis=1).transpose(0, 2, 1, 3)
    return (
        state_grads.astype(BF16).reshape(query_states.shape),
        passage_grads.reshape(passages.shape),
        weight_grad.reshape(D // MEMBERS, D),
    )


def solution(mesh):
    fine = Mesh(mesh.devices.reshape(Z_HI, X, Y, Z_LO, CORE), ("zh", "x", "y", "zl", "c"))
    placed = (
        P(BLK, GRP, None, None),
        P(BLK, GRP, None, None),
        P(),
        P(BLK, GRP, None, None),
        P(BLK, GRP, None),
        P(BLK, GRP, None, None),
        P(BLK, GRP, None, None),
        P(BLK, GRP, None),
    )
    return jax.shard_map(
        local,
        mesh=fine,
        in_specs=placed,
        out_specs=(P(BLK, GRP, None, None), P(BLK, GRP, None, None), P(BLK, None)),
        check_vma=False,
    )
```

time: 217 us -> 211 us (0.972)
  blocking collectives: 47.1 us -> 19.9 us
  waiting for transfers between devices: 54.2 us -> 72.8 us
  Pallas kernels: 13.2 us -> 20.2 us
  local copies, waits for them, and re-layouts: 18.9 us -> 12.9 us
    all_to_all x2 -> x1, blocking collectives: 47.1 us -> 19.9 us  [swap(): return lax.all_to_all(x, axis, split_axis=0, concat_axis=0, tiled=True)]
    all_to_all x3 -> x4, waiting for transfers between devices: 12.1 us -> 37.8 us  [swap(): return lax.all_to_all(x, axis, split_axis=0, concat_axis=0, tiled=True)]
    ppermute x6, waiting for transfers between devices: 41.2 us -> 23.8 us  [around(): return lax.ppermute(x, axis, [(i, (i + by) % count) for i in range(count)])]
    ppermute x3, starting transfers between devices: 24.3 us -> 13.6 us  [to_owner(): lax.ppermute(piece, BLK, [(i, (i - stop) % MEMBERS) for i in range(MEMBER...]
    ppermute x3, waiting for transfers between devices: 0.99 us -> 11.3 us  [to_owner(): lax.ppermute(piece, BLK, [(i, (i - stop) % MEMBERS) for i in range(MEMBER...]
    all_to_all x3 -> x4, starting transfers between devices: 22.7 us -> 32.2 us  [swap(): return lax.all_to_all(x, axis, split_axis=0, concat_axis=0, tiled=True)]
    unnamed x55 -> x39, local copies, waits for them, and re-layouts: 18.5 us -> 9 us
    pallas_call x7 -> x8, Pallas kernels: 13.2 us -> 20.2 us  [run(): pl.pallas_call(kernel, out_shape=out_shape, compiler_params=pltpu.Compile...]
  transfers between devices with their start and end apart: 12 -> 13, of which waited for: 5 -> 10; matrix products, arithmetic and copies ran while one was open for 1% -> 5% of each run, Pallas kernels for 3% -> 3%
where the time goes in v3:
time: 211 us; the launch traced here: 210 us
  starting transfers between devices  75.6 us (36%)
  waiting for transfers between devices  72.8 us (35%)
  Pallas kernels  20.2 us (10%)
  blocking collectives  19.9 us (9%)
  local copies, waits for them, and re-layouts  12.9 us (6%)
  matrix products  4.94 us (2%)
  other arithmetic  2.55 us (1%)
    all_to_all x4, waiting for transfers between devices, swap(): return lax.all_to_all(x, axis, split_axis=0, concat_axis=0, tiled=True)  37.8 us
    all_to_all x4, starting transfers between devices, swap(): return lax.all_to_all(x, axis, split_axis=0, concat_axis=0, tiled=True)  32.2 us
    ppermute x6, starting transfers between devices, around(): return lax.ppermute(x, axis, [(i, (i + by) % count) for i in range(count)])  29.8 us
    ppermute x6, waiting for transfers between devices, around(): return lax.ppermute(x, axis, [(i, (i + by) % count) for i in range(count)])  23.8 us
    pallas_call x8, Pallas kernels, run(): pl.pallas_call(kernel, out_shape=out_shape, compiler_params=pltpu.Compile...  20.2 us
    all_to_all x1, blocking collectives, swap(): return lax.all_to_all(x, axis, split_axis=0, concat_axis=0, tiled=True)  19.9 us
    ppermute x3, starting transfers between devices, to_owner(): lax.ppermute(piece, BLK, [(i, (i - stop) % MEMBERS) for i in range(MEMBER...  13.6 us
    ppermute x3, waiting for transfers between devices, to_owner(): lax.ppermute(piece, BLK, [(i, (i - stop) % MEMBERS) for i in range(MEMBER...  11.3 us
  transfers between devices with their start and end apart: 13, of which 10 were waited for; matrix products, arithmetic and copies ran while one was open for 5% of the time, Pallas kernels for 3%

profile of v3, /device:TPU:1, one launch (start us, length us, event | category | flops | bytes accessed | tf_op | source)
XLA Modules:
  0.0 209.8 jit_solution(634457756136144043)
XLA Ops:
  0.6 8.6 %collective-permute-start = (bf16[128,1024]{1,0:T(8,128)(2,1)}, bf16[128,1024]{1,0:T(8,128)(2,1)S(1)}, u32[]{:S(2)}, u32[]{:S(2)}) collective-permute-start(bf16[128,1024]{1,0:T(8,128)(2,1)} %bitcast.30), channel_id=1, source_target_pairs={{0,192},{192,384},{384,576},{576,0},{1,193},{193,385},{385,577},{5... | collective-permute-start | bytes 786440 | tf_op jit(solution)/shard_map/ppermute | solution.py:218
  9.2 8.6 %collective-permute-start.1 = (bf16[128,1024]{1,0:T(8,128)(2,1)}, bf16[128,1024]{1,0:T(8,128)(2,1)S(1)}, u32[]{:S(2)}, u32[]{:S(2)}) collective-permute-start(bf16[128,1024]{1,0:T(8,128)(2,1)} %bitcast.33), channel_id=1, source_target_pairs={{0,576},{192,0},{384,192},{576,384},{1,577},{193,1},{385,193},{577... | collective-permute-start | bytes 786440 | tf_op jit(solution)/shard_map/ppermute | solution.py:218
  19.9 1.7 shard_map.105
  21.6 19.9 %all_to_all.25.incoming_ref = s32[16,1,64]{2,1,0:T(1,128)} all-to-all(s32[16,1,64]{2,1,0:T(1,128)S(1)} %get-tuple-element.27), channel_id=1, replica_groups=mesh['zh'=4,'x'=4,'y'=8,'zl'=3,'c'=2] {'zh','x'}, dimensions={0} | all-to-all | bytes 8192 | tf_op jit(solution)/shard_map/all_to_all | solution.py:222
  42.2 3.4 %shard_map.106 = bf16[16,64,1024]{2,1,0:T(8,128)(2,1)} custom-call(s32[16,1,64]{2,1,0:T(1,128)} %all_to_all.25.incoming_ref, bf16[512,1024]{1,0:T(8,128)(2,1)} %bitcast.44), custom_call_target="tpu_custom_call" | custom-call | flops 1073741824 | bytes 3145728 | tf_op jit(solution)/shard_map/pallas_call | solution.py:37
  45.7 6.5 %all-to-all-start.1 = ((bf16[16,64,1024]{2,1,0:T(8,128)(2,1)}), bf16[16,64,1024]{2,1,0:T(8,128)(2,1)}, u32[]{:S(2)}, u32[]{:S(2)}) async-start(bf16[16,64,1024]{2,1,0:T(8,128)(2,1)} %shard_map.106), calls=%async_computation.1 | async-start | bytes 4194304 | tf_op jit(solution)/shard_map/all_to_all | solution.py:222
  53.2 2.1 %shard_map.103 = (bf16[128,2304]{1,0:T(8,128)(2,1)}, bf16[128,2304]{1,0:T(8,128)(2,1)}, bf16[128,2304]{1,0:T(8,128)(2,1)}, bf16[128,256]{1,0:T(8,128)(2,1)S(1)}) custom-call(s32[3]{0:T(128)S(1)} %pad_add_fusion.place_ref, bf16[128,1024]{1,0:T(8,128)(2,1)S(1)} %bitcast.31, bf16[128,1024]{1,0:T(8,128)(2,1)S(1)} %collective-permute-done.below_ref, ...), custom_call_target="tpu_custom_call" | custom-call | bytes 6291456 | tf_op jit(solution)/shard_map/pallas_call | solution.py:37
  55.3 3.2 %collective-permute-start.2 = (bf16[128,2304]{1,0:T(8,128)(2,1)}, bf16[128,2304]{1,0:T(8,128)(2,1)S(1)}, u32[]{:S(2)}, u32[]{:S(2)}) collective-permute-start(bf16[128,2304]{1,0:T(8,128)(2,1)} %get-tuple-element.21), channel_id=1, source_target_pairs={{0,48},{48,96},{96,144},{144,0},{1,49},{49,97},{97,145},{145,1},{2... | collective-permute-start | bytes 1769480 | tf_op jit(solution)/shard_map/ppermute | solution.py:218
  58.5 4.3 %collective-permute-start.3 = (bf16[128,2304]{1,0:T(8,128)(2,1)}, bf16[128,2304]{1,0:T(8,128)(2,1)}, u32[]{:S(2)}, u32[]{:S(2)}) collective-permute-start(bf16[128,2304]{1,0:T(8,128)(2,1)} %get-tuple-element.22), channel_id=1, source_target_pairs={{0,96},{48,144},{96,0},{144,48},{1,97},{49,145},{97,1},{145,49},{2... | collective-permute-start | bytes 1769480 | tf_op jit(solution)/shard_map/ppermute | solution.py:218
  62.8 3.1 %collective-permute-start.4 = (bf16[128,2304]{1,0:T(8,128)(2,1)}, bf16[128,2304]{1,0:T(8,128)(2,1)}, u32[]{:S(2)}, u32[]{:S(2)}) collective-permute-start(bf16[128,2304]{1,0:T(8,128)(2,1)} %get-tuple-element.23), channel_id=1, source_target_pairs={{0,144},{48,0},{96,48},{144,96},{1,145},{49,1},{97,49},{145,97},{2... | collective-permute-start | bytes 1769480 | tf_op jit(solution)/shard_map/ppermute | solution.py:218
  67.5 7.7 %collective-permute-done.2.refs_0_ = bf16[128,2304]{1,0:T(8,128)(2,1)S(1)} collective-permute-done((bf16[128,2304]{1,0:T(8,128)(2,1)}, bf16[128,2304]{1,0:T(8,128)(2,1)S(1)}, u32[]{:S(2)}, u32[]{:S(2)}) %collective-permute-start.2) | collective-permute-done | bytes 589856 | tf_op jit(solution)/shard_map/ppermute | solution.py:218
  76.0 11.2 %collective-permute-done.3.refs_1_ = bf16[128,2304]{1,0:T(8,128)(2,1)} collective-permute-done((bf16[128,2304]{1,0:T(8,128)(2,1)}, bf16[128,2304]{1,0:T(8,128)(2,1)}, u32[]{:S(2)}, u32[]{:S(2)}) %collective-permute-start.3) | collective-permute-done | bytes 589856 | tf_op jit(solution)/shard_map/ppermute | solution.py:218
  87.2 4.9 %collective-permute-done.4.refs_2_ = bf16[128,2304]{1,0:T(8,128)(2,1)} collective-permute-done((bf16[128,2304]{1,0:T(8,128)(2,1)}, bf16[128,2304]{1,0:T(8,128)(2,1)}, u32[]{:S(2)}, u32[]{:S(2)}) %collective-permute-start.4) | collective-permute-done | bytes 589856 | tf_op jit(solution)/shard_map/ppermute | solution.py:218
  94.1 1.4 shard_map.104
  96.2 1.3 convolution_convert_fusion.asking_ref
  100.5 26.4 %all-to-all-done.1 = bf16[16,64,1024]{2,1,0:T(8,128)(2,1)} async-done(((bf16[16,64,1024]{2,1,0:T(8,128)(2,1)}), bf16[16,64,1024]{2,1,0:T(8,128)(2,1)}, u32[]{:S(2)}, u32[]{:S(2)}) %all-to-all-start.1) | async-done | bytes 2097184 | tf_op jit(solution)/shard_map/all_to_all | solution.py:222
  126.9 5.0 %shard_map.107 = (bf16[128,512]{1,0:T(8,128)(2,1)}, bf16[128,1024]{1,0:T(8,128)(2,1)}, bf16[8,128,512]{2,1,0:T(8,128)(2,1)}) custom-call(bf16[128,1024]{1,0:T(8,128)(2,1)} %slice.20.queries_ref, f32[128,512]{1,0:T(8,128)} %convolution_multiply_fusion.scores_ref, bf16[128,1024]{1,0:T(8,128)(2,1)} %bitcast.40, s32[128,1]{1,0:T(8,128)} %copy.12.positive_ref, ...), custom_call_target="tpu_custom_call" | custom-call | flops 671088640 | bytes 4194304 | tf_op jit(solution)/shard_map/pallas_call | solution.py:37
  131.9 7.4 %all-to-all-start.2 = ((bf16[8,128,512]{2,1,0:T(8,128)(2,1)}), bf16[8,128,512]{2,1,0:T(8,128)(2,1)}, u32[]{:S(2)}, u32[]{:S(2)}) async-start(bf16[8,128,512]{2,1,0:T(8,128)(2,1)} %get-tuple-element.32), calls=%async_computation.2 | async-start | bytes 2097152 | tf_op jit(solution)/shard_map/all_to_all | solution.py:222
  139.3 2.0 collective-permute-start.6
  141.4 4.3 %collective-permute-start.5 = (bf16[128,128]{1,0:T(8,128)(2,1)S(1)}, bf16[128,128]{1,0:T(8,128)(2,1)S(1)}, u32[]{:S(2)}, u32[]{:S(2)}) collective-permute-start(bf16[128,128]{1,0:T(8,128)(2,1)S(1)} %get-tuple-element.37), channel_id=1, source_target_pairs={{0,720},{48,0},{96,48},{144,96},{192,144},{240,192},{288,240},{336... | collective-permute-start | bytes 98312 | tf_op jit(solution)/shard_map/ppermute | solution.py:302
  145.6 8.7 %collective-permute-done.5.refs_1_ = bf16[128,128]{1,0:T(8,128)(2,1)S(1)} collective-permute-done((bf16[128,128]{1,0:T(8,128)(2,1)S(1)}, bf16[128,128]{1,0:T(8,128)(2,1)S(1)}, u32[]{:S(2)}, u32[]{:S(2)}) %collective-permute-start.5) | collective-permute-done | bytes 32800 | tf_op jit(solution)/shard_map/ppermute | solution.py:302
  155.2 3.7 %shard_map.108 = bf16[256,512]{1,0:T(8,128)(2,1)} custom-call(s32[3]{0:T(128)} %copy-done.13, bf16[4,128,256]{2,1,0:T(8,128)(2,1)} %copy-done.9, bf16[4,128,256]{2,1,0:T(8,128)(2,1)} %copy-done.16, bf16[8,128,512]{2,1,0:T(8,128)(2,1)} %all-to-all-done.2.grads_ref), custom_call_target="tpu_custom_call" | custom-call | flops 268435456 | bytes 2097152 | tf_op jit(solution)/shard_map/pallas_call | solution.py:37
  158.9 7.6 %all-to-all-start.3 = ((bf16[32,8,512]{2,1,0:T(8,128)(2,1)}), bf16[32,8,512]{2,1,0:T(8,128)(2,1)S(1)}, u32[]{:S(2)}, u32[]{:S(2)}) async-start(bf16[32,8,512]{2,1,0:T(8,128)(2,1)} %bitcast.39), calls=%async_computation.3 | async-start | bytes 524288 | tf_op jit(solution)/shard_map/all_to_all | solution.py:222
  167.4 7.1 %collective-permute-start.7 = (bf16[128,128]{1,0:T(8,128)(2,1)S(1)}, bf16[128,128]{1,0:T(8,128)(2,1)S(1)}, u32[]{:S(2)}, u32[]{:S(2)}) collective-permute-start(bf16[128,128]{1,0:T(8,128)(2,1)S(1)} %slice.18), channel_id=1, source_target_pairs={{0,672},{48,720},{96,0},{144,48},{192,96},{240,144},{288,192},{336... | collective-permute-start | bytes 98312 | tf_op jit(solution)/shard_map/ppermute | solution.py:302
  175.6 6.0 %all-to-all-done.3.parts_ref = bf16[32,8,512]{2,1,0:T(8,128)(2,1)S(1)} async-done(((bf16[32,8,512]{2,1,0:T(8,128)(2,1)}), bf16[32,8,512]{2,1,0:T(8,128)(2,1)S(1)}, u32[]{:S(2)}, u32[]{:S(2)}) %all-to-all-start.3) | async-done | bytes 262176 | tf_op jit(solution)/shard_map/all_to_all | solution.py:222
  182.2 1.8 shard_map.109
  184.0 10.7 %all-to-all-start.4 = ((bf16[48,8,512]{2,1,0:T(8,128)(2,1)}), bf16[48,8,512]{2,1,0:T(8,128)(2,1)}, u32[]{:S(2)}, u32[]{:S(2)}) async-start(bf16[48,8,512]{2,1,0:T(8,128)(2,1)} %shard_map.109), calls=%async_computation.4 | async-start | bytes 786432 | tf_op jit(solution)/shard_map/all_to_all | solution.py:222
  195.4 2.2 %collective-permute-start.8 = (bf16[128,128]{1,0:T(8,128)(2,1)S(1)}, bf16[128,128]{1,0:T(8,128)(2,1)S(1)}, u32[]{:S(2)}, u32[]{:S(2)}) collective-permute-start(bf16[128,128]{1,0:T(8,128)(2,1)S(1)} %slice.19), channel_id=1, source_target_pairs={{0,624},{48,672},{96,720},{144,0},{192,48},{240,96},{288,144},{336... | collective-permute-start | bytes 98312 | tf_op jit(solution)/shard_map/ppermute | solution.py:302
  197.6 2.5 %fusion = bf16[1,1,128,1024]{3,2,1,0:T(8,128)(2,1)} fusion(bf16[128,1024]{1,0:T(8,128)(2,1)} %get-tuple-element.29, bf16[1024,1024]{1,0:T(8,128)(2,1)S(1)} %copy-done), kind=kOutput, calls=%fused_computation.2 | convolution fusion | flops 268566528 | bytes 2621440 | tf_op jit(solution)/shard_map/dot_general | solution.py:49
  200.1 1.6 collective-permute-done.8.refs_3_
  202.7 5.3 %all-to-all-done.4 = bf16[48,8,512]{2,1,0:T(8,128)(2,1)} async-done(((bf16[48,8,512]{2,1,0:T(8,128)(2,1)}), bf16[48,8,512]{2,1,0:T(8,128)(2,1)}, u32[]{:S(2)}, u32[]{:S(2)}) %all-to-all-start.4) | async-done | bytes 393248 | tf_op jit(solution)/shard_map/all_to_all | solution.py:222
  208.0 1.8 convert_reduce_fusion
  (54 shorter events, 17.1 us)
Async XLA Ops:
  0.6 95.6 %copy-start = (bf16[1024,1024]{1,0:T(8,128)(2,1)S(1)}, bf16[1024,1024]{1,0:T(8,128)(2,1)}, u32[]{:S(2)}) copy-start(bf16[1024,1024]{1,0:T(8,128)(2,1)} %param.10) | copy-start | bytes 6291460
  0.6 40.8 %collective-permute-start = (bf16[128,1024]{1,0:T(8,128)(2,1)}, bf16[128,1024]{1,0:T(8,128)(2,1)S(1)}, u32[]{:S(2)}, u32[]{:S(2)}) collective-permute-start(bf16[128,1024]{1,0:T(8,128)(2,1)} %bitcast.30), channel_id=1, source_target_pairs={{0,192},{192,384},{384,576},{576,0},{1,193},{193,385},{385,577},{5... | collective-permute-start | bytes 786440 | tf_op jit(solution)/shard_map/ppermute | solution.py:218
  9.2 32.2 %collective-permute-start.1 = (bf16[128,1024]{1,0:T(8,128)(2,1)}, bf16[128,1024]{1,0:T(8,128)(2,1)S(1)}, u32[]{:S(2)}, u32[]{:S(2)}) collective-permute-start(bf16[128,1024]{1,0:T(8,128)(2,1)} %bitcast.33), channel_id=1, source_target_pairs={{0,576},{192,0},{384,192},{576,384},{1,577},{193,1},{385,193},{577... | collective-permute-start | bytes 786440 | tf_op jit(solution)/shard_map/ppermute | solution.py:218
  19.2 0.7 copy-start.14
  41.5 0.7 copy-start.11
  45.6 6.6 %copy-start.4 = (bf16[1,1,128,1024]{3,2,1,0:T(8,128)(2,1)S(1)}, bf16[1,1,128,1024]{3,2,1,0:T(8,128)(2,1)}, u32[]{:S(2)}) copy-start(bf16[1,1,128,1024]{3,2,1,0:T(8,128)(2,1)} %param.9) | copy-start | bytes 786436
  45.6 6.6 %copy-start.5 = (bf16[1,1,128,1024]{3,2,1,0:T(8,128)(2,1)S(1)}, bf16[1,1,128,1024]{3,2,1,0:T(8,128)(2,1)}, u32[]{:S(2)}) copy-start(bf16[1,1,128,1024]{3,2,1,0:T(8,128)(2,1)} %param.8) | copy-start | bytes 786436
  45.6 21.1 %copy-start.18 = (s32[1,1,128]{2,1,0:T(1,128)S(1)}, s32[1,1,128]{2,1,0:T(1,128)}, u32[]{:S(2)}) copy-start(s32[1,1,128]{2,1,0:T(1,128)} %param.12) | copy-start | bytes 1540
  45.7 81.2 %all-to-all-start.1 = ((bf16[16,64,1024]{2,1,0:T(8,128)(2,1)}), bf16[16,64,1024]{2,1,0:T(8,128)(2,1)}, u32[]{:S(2)}, u32[]{:S(2)}) async-start(bf16[16,64,1024]{2,1,0:T(8,128)(2,1)} %shard_map.106), calls=%async_computation.1 | async-start | bytes 4194304 | tf_op jit(solution)/shard_map/all_to_all | solution.py:222
  52.2 1.0 copy-start.12
  53.2 44.3 %copy-start.13 = (s32[3]{0:T(128)}, s32[3]{0:T(128)S(1)}, u32[]{:S(2)}) copy-start(s32[3]{0:T(128)S(1)} %pad_add_fusion.place_ref) | copy-start | bytes 40
  55.3 19.9 %collective-permute-start.2 = (bf16[128,2304]{1,0:T(8,128)(2,1)}, bf16[128,2304]{1,0:T(8,128)(2,1)S(1)}, u32[]{:S(2)}, u32[]{:S(2)}) collective-permute-start(bf16[128,2304]{1,0:T(8,128)(2,1)} %get-tuple-element.21), channel_id=1, source_target_pairs={{0,48},{48,96},{96,144},{144,0},{1,49},{49,97},{97,145},{145,1},{2... | collective-permute-start | bytes 1769480 | tf_op jit(solution)/shard_map/ppermute | solution.py:218
  58.5 28.7 %collective-permute-start.3 = (bf16[128,2304]{1,0:T(8,128)(2,1)}, bf16[128,2304]{1,0:T(8,128)(2,1)}, u32[]{:S(2)}, u32[]{:S(2)}) collective-permute-start(bf16[128,2304]{1,0:T(8,128)(2,1)} %get-tuple-element.22), channel_id=1, source_target_pairs={{0,96},{48,144},{96,0},{144,48},{1,97},{49,145},{97,1},{145,49},{2... | collective-permute-start | bytes 1769480 | tf_op jit(solution)/shard_map/ppermute | solution.py:218
  62.8 29.3 %collective-permute-start.4 = (bf16[128,2304]{1,0:T(8,128)(2,1)}, bf16[128,2304]{1,0:T(8,128)(2,1)}, u32[]{:S(2)}, u32[]{:S(2)}) collective-permute-start(bf16[128,2304]{1,0:T(8,128)(2,1)} %get-tuple-element.23), channel_id=1, source_target_pairs={{0,144},{48,0},{96,48},{144,96},{1,145},{49,1},{97,49},{145,97},{2... | collective-permute-start | bytes 1769480 | tf_op jit(solution)/shard_map/ppermute | solution.py:218
  75.2 0.8 copy-start.7
  92.1 0.9 copy-start.6
  93.0 1.1 copy-start.8
  95.5 0.7 copy-start.9
  96.2 2.0 copy-start.1
  99.4 1.0 copy-start.2
  126.9 12.4 %copy-start.10 = (bf16[4,128,256]{2,1,0:T(8,128)(2,1)S(1)}, bf16[4,128,256]{2,1,0:T(8,128)(2,1)}, u32[]{:S(2)}) copy-start(bf16[4,128,256]{2,1,0:T(8,128)(2,1)} %copy-done.9) | copy-start | bytes 786436
  131.8 9.5 %copy-start.17 = (bf16[128,512]{1,0:T(8,128)(2,1)S(1)}, bf16[128,512]{1,0:T(8,128)(2,1)}, u32[]{:S(2)}) copy-start(bf16[128,512]{1,0:T(8,128)(2,1)} %get-tuple-element.36) | copy-start | bytes 393220
  131.9 22.6 %all-to-all-start.2 = ((bf16[8,128,512]{2,1,0:T(8,128)(2,1)}), bf16[8,128,512]{2,1,0:T(8,128)(2,1)}, u32[]{:S(2)}, u32[]{:S(2)}) async-start(bf16[8,128,512]{2,1,0:T(8,128)(2,1)} %get-tuple-element.32), calls=%async_computation.2 | async-start | bytes 2097152 | tf_op jit(solution)/shard_map/all_to_all | solution.py:222
  139.3 15.2 %collective-permute-start.6 = (bf16[4,128,256]{2,1,0:T(8,128)(2,1)S(1)}, bf16[4,128,256]{2,1,0:T(8,128)(2,1)S(1)}, u32[]{:S(2)}, u32[]{:S(2)}) collective-permute-start(bf16[4,128,256]{2,1,0:T(8,128)(2,1)S(1)} %copy-done.10), channel_id=1, source_target_pairs={{0,1},{1,0},{2,3},{3,2},{4,5},{5,4},{6,7},{7,6},{8,9},{9,8},{10,11... | collective-permute-start | bytes 786440 | tf_op jit(solution)/shard_map/ppermute | solution.py:218
  141.4 13.0 %collective-permute-start.5 = (bf16[128,128]{1,0:T(8,128)(2,1)S(1)}, bf16[128,128]{1,0:T(8,128)(2,1)S(1)}, u32[]{:S(2)}, u32[]{:S(2)}) collective-permute-start(bf16[128,128]{1,0:T(8,128)(2,1)S(1)} %get-tuple-element.37), channel_id=1, source_target_pairs={{0,720},{48,0},{96,48},{144,96},{192,144},{240,192},{288,240},{336... | collective-permute-start | bytes 98312 | tf_op jit(solution)/shard_map/ppermute | solution.py:302
  154.5 0.7 copy-start.16
  158.9 22.6 %all-to-all-start.3 = ((bf16[32,8,512]{2,1,0:T(8,128)(2,1)}), bf16[32,8,512]{2,1,0:T(8,128)(2,1)S(1)}, u32[]{:S(2)}, u32[]{:S(2)}) async-start(bf16[32,8,512]{2,1,0:T(8,128)(2,1)} %bitcast.39), calls=%async_computation.3 | async-start | bytes 524288 | tf_op jit(solution)/shard_map/all_to_all | solution.py:222
  166.6 35.1 %copy-start.3 = (bf16[512,1024]{1,0:T(8,128)(2,1)S(1)}, bf16[512,1024]{1,0:T(8,128)(2,1)}, u32[]{:S(2)}) copy-start(bf16[512,1024]{1,0:T(8,128)(2,1)} %copy-done.2) | copy-start | bytes 3145732
  167.4 8.1 %collective-permute-start.7 = (bf16[128,128]{1,0:T(8,128)(2,1)S(1)}, bf16[128,128]{1,0:T(8,128)(2,1)S(1)}, u32[]{:S(2)}, u32[]{:S(2)}) collective-permute-start(bf16[128,128]{1,0:T(8,128)(2,1)S(1)} %slice.18), channel_id=1, source_target_pairs={{0,672},{48,720},{96,0},{144,48},{192,96},{240,144},{288,192},{336... | collective-permute-start | bytes 98312 | tf_op jit(solution)/shard_map/ppermute | solution.py:302
  181.5 0.7 copy-start.15
  184.0 24.0 %all-to-all-start.4 = ((bf16[48,8,512]{2,1,0:T(8,128)(2,1)}), bf16[48,8,512]{2,1,0:T(8,128)(2,1)}, u32[]{:S(2)}, u32[]{:S(2)}) async-start(bf16[48,8,512]{2,1,0:T(8,128)(2,1)} %shard_map.109), calls=%async_computation.4 | async-start | bytes 786432 | tf_op jit(solution)/shard_map/all_to_all | solution.py:222
  195.4 6.3 %collective-permute-start.8 = (bf16[128,128]{1,0:T(8,128)(2,1)S(1)}, bf16[128,128]{1,0:T(8,128)(2,1)S(1)}, u32[]{:S(2)}, u32[]{:S(2)}) collective-permute-start(bf16[128,128]{1,0:T(8,128)(2,1)S(1)} %slice.19), channel_id=1, source_target_pairs={{0,624},{48,672},{96,720},{144,0},{192,48},{240,96},{288,144},{336... | collective-permute-start | bytes 98312 | tf_op jit(solution)/shard_map/ppermute | solution.py:302

commit v4 on v3

--- a/solution.py
+++ b/solution.py
@@ -10,14 +10,16 @@
 CAP = 64
 ROWS = 128
 D = 1024
-Z_HI, X, Y, Z_LO, CORE = 4, 4, 8, 3, 2
+Z_HI, X, Y_HI, Y_LO, Z_LO, CORE = 4, 4, 4, 2, 3, 2
+QUARTERS = Y_LO * CORE
 MEMBERS = Z_HI * X
 SLOTS = MEMBERS * CAP
 BLK = ("zh", "x")
-GRP = ("y", "zl", "c")
+GRP = ("yh", "yl", "zl", "c")
 F32 = jnp.float32
 BF16 = jnp.bfloat16
 LARGE = 58
+STAT_ROWS = 16
 PARTS = 4
 
 
@@ -61,7 +63,7 @@
 
     owner = jnp.zeros((8, lanes), F32)
     for at in range(NEG):
-        flat = owner_ref[at : at + 1, :]
+        flat = owner_ref[at]
         kept = jnp.where((lane8 + at * lanes) % NEG == row8, flat, 0)
         owner = owner + dot(bits(kept), bits((row + at * lanes) // NEG == lane), (1, 0))
     owner = jnp.where(row8 < NEG, owner.astype(jnp.int32), -1)
@@ -74,14 +76,13 @@
     for at in range(1, MEMBERS):
         placed = placed + place[at * 8 : (at + 1) * 8]
     placed = placed.astype(jnp.int32)
-    slot = slot_ref[...]
-    live = (row8 < count_ref[...]).astype(F32)
+    live = (row8 < count_ref[0]).astype(F32)
     column = lax.broadcasted_iota(jnp.int32, (SLOTS, lanes), 0)
     wanted = jnp.zeros((SLOTS, lanes), jnp.int32)
     used = jnp.zeros((SLOTS, lanes), F32)
     for j in range(NEG):
         match = column == placed[j : j + 1]
-        wanted = wanted + jnp.where(match, slot[j : j + 1], 0)
+        wanted = wanted + jnp.where(match, slot_ref[j], 0)
         used = used + jnp.where(match, live[j : j + 1], 0.0)
     used_ref[...] = used.astype(BF16)
     ones = jnp.ones((8, lanes), BF16)
@@ -109,16 +110,14 @@
         send.wait()
 
 
+def in_three(value):
+    first = value.astype(BF16).astype(F32)
+    second = (value - first).astype(BF16).astype(F32)
+    return first, second, value - first - second
+
+
 def attend_kernel(
-    queries_ref,
-    scores_ref,
-    mask_ref,
-    positive_ref,
-    blocks_ref,
-    replies_ref,
-    batch_ref,
-    query_ref,
-    halves_ref,
+    queries_ref, scores_ref, mask_ref, positive_ref, blocks_ref, replies_ref, query_ref, quarters_ref
 ):
     factor = D**-0.5
     batch_scores = scores_ref[...]
@@ -134,13 +133,23 @@
     hit = (column == positive_ref[...]).astype(F32)
     batch_grad = (batch_exp / total - hit).astype(BF16)
     neg_grad = (neg_exp / total).astype(BF16)
-    batch_ref[...] = batch_grad
     inner = dot(batch_grad, blocks_ref[...], (1, 0)) + dot(neg_grad, replies_ref[...], (1, 0))
     query_grad = (factor * inner).astype(BF16)
     query_ref[...] = query_grad
-    for to in range(X * CORE):
-        at = to % CORE * (D // CORE)
-        halves_ref[to] = query_grad[:, at : at + D // CORE]
+
+    lane = lax.broadcasted_iota(jnp.int32, (ROWS, ROWS), 1)
+    row = lax.broadcasted_iota(jnp.int32, (ROWS, ROWS), 0)
+    stats = jnp.zeros((ROWS, ROWS), F32)
+    for at, value in enumerate(in_three(top) + in_three(total)):
+        stats = jnp.where(lane == at, value, stats)
+    turned = dot(stats.astype(BF16), (lane == row).astype(F32).astype(BF16), (0, 0))
+    turned = turned[:STAT_ROWS].astype(BF16)
+    rest = jnp.zeros((STAT_ROWS, D // QUARTERS - ROWS), BF16)
+    turned = jnp.concatenate([turned, rest], axis=1)
+    for to in range(X * QUARTERS):
+        at = to % QUARTERS * (D // QUARTERS)
+        quarters_ref[to, :ROWS] = query_grad[:, at : at + D // QUARTERS]
+        quarters_ref[to, ROWS:] = turned
 
 
 def pack_kernel(place_ref, own_ref, below_ref, above_ref, states_ref, *refs):
@@ -155,44 +164,53 @@
             piece = cut if piece is None else jnp.where(x_to == x_of, cut, piece)
         return piece
 
-    *send_refs, mine_ref = refs
+    first_refs, second_refs, mine_ref = refs[: X - 1], refs[X - 1 : 2 * X - 2], refs[-1]
     mine_ref[...] = columns(x_at)
     for step in range(1, X):
-        send_ref = send_refs[step - 1]
         wraps = x_at + step >= X
-        send_ref[:, :D] = jnp.where(wraps, below_ref[...], own_ref[...])
-        send_ref[:, D : 2 * D] = jnp.where(wraps, states_ref[...], above_ref[...])
-        send_ref[:, 2 * D :] = columns((x_at + step) % X)
-
-
-def unpack_kernel(place_ref, own_ref, states_ref, mine_ref, *refs):
-    *got_refs, blocks_ref, asking_ref, row_ref = refs
+        first_ref, second_ref = first_refs[step - 1], second_refs[step - 1]
+        first_ref[:, :D] = jnp.where(wraps, below_ref[...], own_ref[...])
+        first_ref[:, D:] = columns((x_at + step) % X)
+        second_ref[...] = jnp.where(wraps, states_ref[...], above_ref[...])
+
+
+def unpack_kernel(place_ref, own_ref, mine_ref, *refs):
+    *got_refs, blocks_ref, row_ref = refs
     x_at = place_ref[0]
     blocks_ref[:ROWS] = own_ref[...]
-    asking_ref[:ROWS] = states_ref[...]
     row_ref[x_at] = mine_ref[...]
     for step in range(1, X):
         got_ref = got_refs[step - 1]
         blocks_ref[step * ROWS : (step + 1) * ROWS] = got_ref[:, :D]
-        asking_ref[(X - step) * ROWS : (X - step + 1) * ROWS] = got_ref[:, D : 2 * D]
-        row_ref[(x_at + X - step) % X] = got_ref[:, 2 * D :]
+        row_ref[(x_at + X - step) % X] = got_ref[:, D:]
 
 
 def gather_kernel(parts_ref, out_ref):
     total = parts_ref[0].astype(F32)
-    for at in range(1, Z_HI * Y):
+    for at in range(1, Z_HI * Y_HI):
         total = total + parts_ref[at].astype(F32)
     total = total.astype(BF16)
-    for to in range(Y * Z_LO * CORE):
+    for to in range(Y_HI * Y_LO * Z_LO * CORE):
         out_ref[to] = total
 
 
-def part_kernel(place_ref, states_ref, pair_ref, grads_ref, part_ref, total_ref):
+def asking_kernel(weight_ref, own_ref, *refs):
+    *states_refs, queries_ref, scores_ref = refs
+    states = jnp.concatenate([ref[...] for ref in states_refs], axis=0)
+    queries = dot(states, weight_ref[...], (1, 0)).astype(BF16)
+    queries_ref[...] = queries
+    scores_ref[...] = dot(own_ref[...], queries, (1, 1)) * (D**-0.5)
+
+
+def part_kernel(place_ref, states_ref, pair_ref, grads_ref, part_ref, stats_ref, total_ref):
     at = pl.program_id(0)
-    c_at = place_ref[1]
-    states = jnp.concatenate([states_ref[0], pair_ref[0]], axis=0)
-    grads = jnp.concatenate([grads_ref[c_at], grads_ref[1 - c_at]], axis=0)
-    term = dot(states, grads, (0, 0))
+    c_at, y_at = place_ref[1], place_ref[3]
+    states = [states_ref[0, 0], states_ref[1, 0], pair_ref[0, 0], pair_ref[1, 0]]
+    mine, other = y_at * CORE, (1 - y_at) * CORE
+    froms = [mine + c_at, other + c_at, mine + 1 - c_at, other + 1 - c_at]
+    grads = [grads_ref[source, :ROWS] for source in froms]
+    term = dot(jnp.concatenate(states, axis=0), jnp.concatenate(grads, axis=0), (0, 0))
+    stats_ref[at] = grads_ref[mine + c_at, ROWS:, :ROWS]
 
     @pl.when(at == 0)
     def _():
@@ -207,10 +225,37 @@
         part_ref[...] = total_ref[...].astype(BF16)
 
 
-def passage_kernel(asking_ref, *refs):
-    *piece_refs, passage_ref = refs
-    pieces = jnp.concatenate([ref[...] for ref in piece_refs], axis=0)
-    passage_ref[...] = (D**-0.5 * dot(pieces, asking_ref[...], (0, 0))).astype(BF16)
+def passage_kernel(
+    place_ref, scores_ref, queries_ref, stats_ref, upper_ref, positive_ref, passage_ref
+):
+    x_at = place_ref[0]
+    row = lax.broadcasted_iota(jnp.int32, (ROWS, ROWS), 0)
+    total = jnp.zeros((ROWS, D), F32)
+    for stop in range(STOPS):
+        x_from = x_at + stop
+        here = stats_ref[x_from % X].astype(F32)
+        stats = jnp.where(x_from < X, here, upper_ref[x_from % X].astype(F32))
+        top = stats[0:1] + stats[1:2] + stats[2:3]
+        weight = stats[3:4] + stats[4:5] + stats[5:6]
+        cut = slice(stop * ROWS, (stop + 1) * ROWS)
+        grad = jnp.exp(scores_ref[:, cut] - top) / weight
+        if stop == 0:
+            grad = grad - (row == positive_ref[...]).astype(F32)
+        total = total + dot(grad.astype(BF16), queries_ref[cut], (1, 0))
+    passage_ref[...] = (D**-0.5 * total).astype(BF16)
+
+
+def finish_kernel(parts_ref, out_ref):
+    height = D // MEMBERS // Y_HI
+    for y_hi in range(Y_HI):
+        for quarter in range(QUARTERS):
+            y_lo, c_of = quarter // CORE, quarter % CORE
+            total = None
+            for z_lo in range(Z_LO):
+                block = parts_ref[((y_hi * Y_LO + y_lo) * Z_LO + z_lo) * CORE + c_of].astype(F32)
+                total = block if total is None else total + block
+            rows = slice(y_hi * height, (y_hi + 1) * height)
+            out_ref[rows, quarter * (D // QUARTERS) : (quarter + 1) * (D // QUARTERS)] = total
 
 
 def around(x, axis, by):
@@ -227,7 +272,7 @@
     states = query_states.reshape(ROWS, D)
     own = passages.reshape(ROWS, D)
     store = neg_store.reshape(-1, D)
-    place = jnp.stack([lax.axis_index(axis) for axis in ("x", "c", "zh")]).astype(jnp.int32)
+    place = jnp.stack([lax.axis_index(axis) for axis in ("x", "c", "zh", "yl")]).astype(jnp.int32)
 
     request, used = call(
         plan_kernel,
@@ -235,8 +280,13 @@
             jax.ShapeDtypeStruct((MEMBERS, 1, CAP), jnp.int32),
             jax.ShapeDtypeStruct((SLOTS, ROWS), BF16),
         ),
+        limit=LARGE,
         moved=1 << 20,
-    )(neg_owner.reshape(NEG, ROWS), neg_slot.reshape(ROWS, NEG).T, neg_count.reshape(1, ROWS))
+    )(
+        neg_owner.reshape(NEG, 1, ROWS),
+        neg_slot.reshape(ROWS, NEG).T.reshape(NEG, 1, ROWS),
+        neg_count.reshape(1, 1, ROWS),
+    )
     mask = used.T
     incoming = swap(request, BLK)
 
@@ -262,93 +312,115 @@
     )(incoming, store)
     replies = swap(served, BLK).reshape(SLOTS, D)
 
-    wide = jax.ShapeDtypeStruct((ROWS, 2 * D + D // X), BF16)
-    *sends, mine = call(
+    wide = jax.ShapeDtypeStruct((ROWS, D + D // X), BF16)
+    sends = call(
         pack_kernel,
-        (wide,) * (X - 1) + (jax.ShapeDtypeStruct((ROWS, D // X), BF16),),
+        (wide,) * (X - 1)
+        + (jax.ShapeDtypeStruct((ROWS, D), BF16),) * (X - 1)
+        + (jax.ShapeDtypeStruct((ROWS, D // X), BF16),),
         scalars=1,
         moved=6 << 20,
     )(place, own, below, above, states)
-    got = [around(send, "x", step + 1) for step, send in enumerate(sends)]
-    blocks, asking, row_states = call(
+    mine = sends[-1]
+    got = [around(send, "x", step + 1) for step, send in enumerate(sends[: X - 1])]
+    blocks, row_states = call(
         unpack_kernel,
         (
-            jax.ShapeDtypeStruct((STOPS * ROWS, D), BF16),
             jax.ShapeDtypeStruct((STOPS * ROWS, D), BF16),
             jax.ShapeDtypeStruct((X, ROWS, D // X), BF16),
         ),
         scalars=1,
-        moved=6 << 20,
-    )(place, own, states, mine, *got)
+        moved=4 << 20,
+    )(place, own, mine, *got)
+    next_states = around(row_states, "yl", 1)
+    row_states = jnp.stack([row_states, next_states])
     pair_states = around(row_states, "c", 1)
-    asking = jnp.dot(asking, proj_weight, preferred_element_type=F32).astype(BF16)
-    queries = asking[:ROWS]
+    late = lax.optimization_barrier((*sends[X - 1 : -1], *got))[: X - 1]
+    late = [around(send, "x", step + 1) for step, send in enumerate(late)]
+    asking, own_scores = call(
+        asking_kernel,
+        (
+            jax.ShapeDtypeStruct((STOPS * ROWS, D), BF16),
+            jax.ShapeDtypeStruct((ROWS, STOPS * ROWS), F32),
+        ),
+        flops=25 * 10**9,
+        moved=4 << 20,
+    )(proj_weight, own, states, *late[::-1])
+    replies = lax.optimization_barrier((replies, pair_states, own_scores))[0]
+    queries = jnp.dot(states, proj_weight, preferred_element_type=F32).astype(BF16)
     scores = dot(queries, blocks, (1, 1)) * factor
-    batch_grad, query_grad, halves = call(
+
+    query_grad, quarters = call(
         attend_kernel,
         (
-            jax.ShapeDtypeStruct((ROWS, STOPS * ROWS), BF16),
             jax.ShapeDtypeStruct((ROWS, D), BF16),
-            jax.ShapeDtypeStruct((X * CORE, ROWS, D // CORE), BF16),
+            jax.ShapeDtypeStruct((X * QUARTERS, ROWS + STAT_ROWS, D // QUARTERS), BF16),
         ),
         limit=LARGE,
         flops=2 * ROWS * D * (2 * SLOTS + STOPS * ROWS),
         moved=4 << 20,
     )(queries, scores, mask, positive.reshape(ROWS, 1), blocks, replies)
-    row_grads = swap(halves, ("x", "c"))
-
-    def to_owner(stop, batch):
-        piece = batch[:, stop * ROWS : (stop + 1) * ROWS]
-        return lax.ppermute(piece, BLK, [(i, (i - stop) % MEMBERS) for i in range(MEMBERS)])
-
-    pieces = [batch_grad[:, :ROWS], to_owner(1, batch_grad)]
-    row_grads = lax.optimization_barrier((row_grads, pieces[1]))[0]
-    part = call(
+    row_grads = swap(quarters, ("x", "yl", "c"))
+
+    part, stats = call(
         part_kernel,
-        jax.ShapeDtypeStruct((D // X, D // CORE), BF16),
+        (
+            jax.ShapeDtypeStruct((D // X, D // QUARTERS), BF16),
+            jax.ShapeDtypeStruct((X, STAT_ROWS, ROWS), BF16),
+        ),
         limit=LARGE,
         flops=2 * ROWS * D * D,
         moved=2 << 20,
         grid=(X,),
         in_specs=[
             pl.BlockSpec(memory_space=pltpu.SMEM),
-            pl.BlockSpec((1, ROWS, D // X), lambda i: (i, 0, 0)),
-            pl.BlockSpec((1, ROWS, D // X), lambda i: (i, 0, 0)),
-            pl.BlockSpec((CORE, ROWS, D // CORE), lambda i: (i, 0, 0)),
+            pl.BlockSpec((Y_LO, 1, ROWS, D // X), lambda i: (0, i, 0, 0)),
+            pl.BlockSpec((Y_LO, 1, ROWS, D // X), lambda i: (0, i, 0, 0)),
+            pl.BlockSpec((QUARTERS, ROWS + STAT_ROWS, D // QUARTERS), lambda i: (i, 0, 0)),
         ],
-        out_specs=pl.BlockSpec((D // X, D // CORE), lambda i: (0, 0)),
-        scratch_shapes=[pltpu.VMEM((D // X, D // CORE), F32)],
+        out_specs=[
+            pl.BlockSpec((D // X, D // QUARTERS), lambda i: (0, 0)),
+            pl.BlockSpec((X, STAT_ROWS, ROWS), lambda i: (0, 0, 0)),
+        ],
+        scratch_shapes=[pltpu.VMEM((D // X, D // QUARTERS), F32)],
     )(place, row_states, pair_states, row_grads)
-    pieces.append(to_owner(2, lax.optimization_barrier((batch_grad, part))[0]))
-    state_grads = dot(query_grad, proj_weight, (1, 1))
-
-    part = swap(part.reshape(Z_HI * Y, D // MEMBERS // Y, D // CORE), ("zh", "y"))
-    part = lax.optimization_barrier((part, pieces[2]))[0]
+    state_grads = dot(query_grad, proj_weight, (1, 1)).astype(BF16)
+
+    height = D // MEMBERS // Y_HI
+    part = swap(part.reshape(Z_HI * Y_HI, height, D // QUARTERS), ("zh", "yh"))
+    upper = around(stats, "zh", -1)
+    part, state_grads, upper = lax.optimization_barrier((part, state_grads, upper))
     part = call(
         gather_kernel,
-        jax.ShapeDtypeStruct((Y * Z_LO * CORE,) + part.shape[1:], BF16),
+        jax.ShapeDtypeStruct((Y_HI * Y_LO * Z_LO * CORE,) + part.shape[1:], BF16),
         limit=LARGE,
         moved=1 << 20,
     )(part)
-    pieces.append(to_owner(3, lax.optimization_barrier((batch_grad, part))[0]))
+    upper = lax.optimization_barrier((upper, part))[0]
     passage_grads = call(
         passage_kernel,
         jax.ShapeDtypeStruct((ROWS, D), BF16),
+        scalars=1,
         flops=2 * ROWS * D * STOPS * ROWS,
         moved=2 << 20,
-    )(asking, *pieces)
-
-    parts = swap(part, GRP).reshape(Y, Z_LO, CORE, D // MEMBERS // Y, D // CORE)
-    weight_grad = jnp.sum(parts.astype(F32), axis=1).transpose(0, 2, 1, 3)
+    )(place, own_scores, asking, stats, upper, positive.reshape(1, ROWS))
+
+    weight_grad = call(
+        finish_kernel,
+        jax.ShapeDtypeStruct((D // MEMBERS, D), F32),
+        limit=LARGE,
+        moved=1 << 20,
+    )(swap(part, GRP))
     return (
-        state_grads.astype(BF16).reshape(query_states.shape),
+        state_grads.reshape(query_states.shape),
         passage_grads.reshape(passages.shape),
-        weight_grad.reshape(D // MEMBERS, D),
+        weight_grad,
     )
 
 
 def solution(mesh):
-    fine = Mesh(mesh.devices.reshape(Z_HI, X, Y, Z_LO, CORE), ("zh", "x", "y", "zl", "c"))
+    shape = (Z_HI, X, Y_HI, Y_LO, Z_LO, CORE)
+    fine = Mesh(mesh.devices.reshape(shape), ("zh", "x", "yh", "yl", "zl", "c"))
     placed = (
         P(BLK, GRP, None, None),
         P(BLK, GRP, None, None),

time: 211 us -> 208 us (0.986)
  waiting for transfers between devices: 72.8 us -> 42.8 us
  blocking collectives: 19.9 us -> 45.2 us
  Pallas kernels: 20.2 us -> 24.4 us
  other arithmetic: 2.55 us -> 0.13 us
    all_to_all x1 -> x2, blocking collectives: 19.9 us -> 45.2 us  [swap(): return lax.all_to_all(x, axis, split_axis=0, concat_axis=0, tiled=True)]
    ppermute x6 -> x11, starting transfers between devices: 29.8 us -> 51.8 us  [around(): return lax.ppermute(x, axis, [(i, (i + by) % count) for i in range(count)])]
    ppermute x3 -> x0, starting transfers between devices: 13.6 us -> none  [to_owner(): lax.ppermute(piece, BLK, [(i, (i - stop) % MEMBERS) for i in range(MEMBER...]
    ppermute x3 -> x0, waiting for transfers between devices: 11.3 us -> none  [to_owner(): lax.ppermute(piece, BLK, [(i, (i - stop) % MEMBERS) for i in range(MEMBER...]
    ppermute x6 -> x11, waiting for transfers between devices: 23.8 us -> 13.8 us  [around(): return lax.ppermute(x, axis, [(i, (i + by) % count) for i in range(count)])]
    all_to_all x4 -> x3, starting transfers between devices: 32.2 us -> 22.3 us  [swap(): return lax.all_to_all(x, axis, split_axis=0, concat_axis=0, tiled=True)]
    all_to_all x4 -> x3, waiting for transfers between devices: 37.8 us -> 29.1 us  [swap(): return lax.all_to_all(x, axis, split_axis=0, concat_axis=0, tiled=True)]
    pallas_call x8 -> x10, Pallas kernels: 20.2 us -> 24.4 us  [run(): pl.pallas_call(kernel, out_shape=out_shape, compiler_params=pltpu.Compile...]
  transfers between devices with their start and end apart: 13 -> 14, of which waited for: 10 -> 6; matrix products, arithmetic and copies ran while one was open for 5% -> 4% of each run, Pallas kernels for 3% -> 4%
where the time goes in v4:
time: 208 us; the launch traced here: 206 us
  starting transfers between devices  74.1 us (36%)
  blocking collectives  45.2 us (22%)
  waiting for transfers between devices  42.8 us (21%)
  Pallas kernels  24.4 us (12%)
  local copies, waits for them, and re-layouts  14.6 us (7%)
  matrix products  4.14 us (2%)
    ppermute x11, starting transfers between devices, around(): return lax.ppermute(x, axis, [(i, (i + by) % count) for i in range(count)])  51.8 us
    all_to_all x2, blocking collectives, swap(): return lax.all_to_all(x, axis, split_axis=0, concat_axis=0, tiled=True)  45.2 us
    all_to_all x3, waiting for transfers between devices, swap(): return lax.all_to_all(x, axis, split_axis=0, concat_axis=0, tiled=True)  29.1 us
    pallas_call x10, Pallas kernels, run(): pl.pallas_call(kernel, out_shape=out_shape, compiler_params=pltpu.Compile...  24.4 us
    all_to_all x3, starting transfers between devices, swap(): return lax.all_to_all(x, axis, split_axis=0, concat_axis=0, tiled=True)  22.3 us
    ppermute x11, waiting for transfers between devices, around(): return lax.ppermute(x, axis, [(i, (i + by) % count) for i in range(count)])  13.8 us
    unnamed x57, local copies, waits for them, and re-layouts  11.5 us
  transfers between devices with their start and end apart: 14, of which 6 were waited for; matrix products, arithmetic and copies ran while one was open for 4% of the time, Pallas kernels for 4%

profile of v4, /device:TPU:1, one launch (start us, length us, event | category | flops | bytes accessed | tf_op | source)
XLA Modules:
  0.0 206.4 jit_solution(12500449854142576284)
XLA Ops:
  0.6 8.4 %collective-permute-start = (bf16[128,1024]{1,0:T(8,128)(2,1)}, bf16[128,1024]{1,0:T(8,128)(2,1)S(1)}, u32[]{:S(2)}, u32[]{:S(2)}) collective-permute-start(bf16[128,1024]{1,0:T(8,128)(2,1)} %bitcast.32), channel_id=1, source_target_pairs={{0,192},{192,384},{384,576},{576,0},{1,193},{193,385},{385,577},{5... | collective-permute-start | bytes 786440 | tf_op jit(solution)/shard_map/ppermute | solution.py:263
  9.1 8.6 %collective-permute-start.1 = (bf16[128,1024]{1,0:T(8,128)(2,1)}, bf16[128,1024]{1,0:T(8,128)(2,1)S(1)}, u32[]{:S(2)}, u32[]{:S(2)}) collective-permute-start(bf16[128,1024]{1,0:T(8,128)(2,1)} %bitcast.29), channel_id=1, source_target_pairs={{0,576},{192,0},{384,192},{576,384},{1,577},{193,1},{385,193},{577... | collective-permute-start | bytes 786440 | tf_op jit(solution)/shard_map/ppermute | solution.py:263
  19.0 3.1 %shard_map.105 = (s32[16,1,64]{2,1,0:T(1,128)}, bf16[1024,128]{1,0:T(8,128)(2,1)}) custom-call(s32[7,1,128]{2,1,0:T(1,128)} %bitcast.45, s32[7,1,128]{2,1,0:T(1,128)} %reshape.46.slot_ref, s32[1,1,128]{2,1,0:T(1,128)} %count_ref.1), custom_call_target="tpu_custom_call" | custom-call | bytes 1048576 | tf_op jit(solution)/shard_map/pallas_call | solution.py:39
  22.0 20.1 %all_to_all.25.incoming_ref = s32[16,1,64]{2,1,0:T(1,128)} all-to-all(s32[16,1,64]{2,1,0:T(1,128)} %get-tuple-element.36), channel_id=1, replica_groups=mesh['zh'=4,'x'=4,'yh'=4,'yl'=2,'zl'=3,'c'=2] {'zh','x'}, dimensions={0} | all-to-all | bytes 8192 | tf_op jit(solution)/shard_map/all_to_all | solution.py:267
  42.1 3.4 %shard_map.106 = bf16[16,64,1024]{2,1,0:T(8,128)(2,1)} custom-call(s32[16,1,64]{2,1,0:T(1,128)} %all_to_all.25.incoming_ref, bf16[512,1024]{1,0:T(8,128)(2,1)} %bitcast.46), custom_call_target="tpu_custom_call" | custom-call | flops 1073741824 | bytes 3145728 | tf_op jit(solution)/shard_map/pallas_call | solution.py:39
  45.6 5.8 %all-to-all-start.1 = ((bf16[16,64,1024]{2,1,0:T(8,128)(2,1)}), bf16[16,64,1024]{2,1,0:T(8,128)(2,1)}, u32[]{:S(2)}, u32[]{:S(2)}) async-start(bf16[16,64,1024]{2,1,0:T(8,128)(2,1)} %shard_map.106), calls=%async_computation.1 | async-start | bytes 4194304 | tf_op jit(solution)/shard_map/all_to_all | solution.py:267
  51.5 1.9 shard_map.103
  55.5 3.2 %collective-permute-start.2 = (bf16[128,1280]{1,0:T(8,128)(2,1)}, bf16[128,1280]{1,0:T(8,128)(2,1)S(1)}, u32[]{:S(2)}, u32[]{:S(2)}) collective-permute-start(bf16[128,1280]{1,0:T(8,128)(2,1)} %get-tuple-element.30), channel_id=1, source_target_pairs={{0,48},{48,96},{96,144},{144,0},{1,49},{49,97},{97,145},{145,1},{2... | collective-permute-start | bytes 983048 | tf_op jit(solution)/shard_map/ppermute | solution.py:263
  58.7 4.3 %collective-permute-start.3 = (bf16[128,1280]{1,0:T(8,128)(2,1)}, bf16[128,1280]{1,0:T(8,128)(2,1)S(1)}, u32[]{:S(2)}, u32[]{:S(2)}) collective-permute-start(bf16[128,1280]{1,0:T(8,128)(2,1)} %get-tuple-element.31), channel_id=1, source_target_pairs={{0,96},{48,144},{96,0},{144,48},{1,97},{49,145},{97,1},{145,49},{2... | collective-permute-start | bytes 983048 | tf_op jit(solution)/shard_map/ppermute | solution.py:263
  63.0 3.1 %collective-permute-start.4 = (bf16[128,1280]{1,0:T(8,128)(2,1)}, bf16[128,1280]{1,0:T(8,128)(2,1)S(1)}, u32[]{:S(2)}, u32[]{:S(2)}) collective-permute-start(bf16[128,1280]{1,0:T(8,128)(2,1)} %get-tuple-element.32), channel_id=1, source_target_pairs={{0,144},{48,0},{96,48},{144,96},{1,145},{49,1},{97,49},{145,97},{2... | collective-permute-start | bytes 983048 | tf_op jit(solution)/shard_map/ppermute | solution.py:263
  66.1 1.8 copy.11
  69.9 6.9 %collective-permute-done.3.refs_1_ = bf16[128,1280]{1,0:T(8,128)(2,1)S(1)} collective-permute-done((bf16[128,1280]{1,0:T(8,128)(2,1)}, bf16[128,1280]{1,0:T(8,128)(2,1)S(1)}, u32[]{:S(2)}, u32[]{:S(2)}) %collective-permute-start.3) | collective-permute-done | bytes 327712 | tf_op jit(solution)/shard_map/ppermute | solution.py:263
  77.6 2.4 %collective-permute-done.4.refs_2_ = bf16[128,1280]{1,0:T(8,128)(2,1)S(1)} collective-permute-done((bf16[128,1280]{1,0:T(8,128)(2,1)}, bf16[128,1280]{1,0:T(8,128)(2,1)S(1)}, u32[]{:S(2)}, u32[]{:S(2)}) %collective-permute-start.4) | collective-permute-done | bytes 327712 | tf_op jit(solution)/shard_map/ppermute | solution.py:263
  80.8 5.1 %collective-permute-start.7 = (bf16[128,1024]{1,0:T(8,128)(2,1)S(1)}, bf16[128,1024]{1,0:T(8,128)(2,1)S(1)}, u32[]{:S(2)}, u32[]{:S(2)}) collective-permute-start(bf16[128,1024]{1,0:T(8,128)(2,1)S(1)} %copy-done.24), channel_id=1, source_target_pairs={{0,144},{48,0},{96,48},{144,96},{1,145},{49,1},{97,49},{145,97},{2... | collective-permute-start | bytes 786440 | tf_op jit(solution)/shard_map/ppermute | solution.py:263
  85.9 4.0 %collective-permute-start.8 = (bf16[128,1024]{1,0:T(8,128)(2,1)S(1)}, bf16[128,1024]{1,0:T(8,128)(2,1)S(1)}, u32[]{:S(2)}, u32[]{:S(2)}) collective-permute-start(bf16[128,1024]{1,0:T(8,128)(2,1)S(1)} %copy-done.22), channel_id=1, source_target_pairs={{0,96},{48,144},{96,0},{144,48},{1,97},{49,145},{97,1},{145,49},{2... | collective-permute-start | bytes 786440 | tf_op jit(solution)/shard_map/ppermute | solution.py:263
  89.9 1.9 collective-permute-start.9
  96.4 3.2 %collective-permute-start.5 = (bf16[4,128,256]{2,1,0:T(8,128)(2,1)S(1)}, bf16[4,128,256]{2,1,0:T(8,128)(2,1)S(1)}, u32[]{:S(2)}, u32[]{:S(2)}) collective-permute-start(bf16[4,128,256]{2,1,0:T(8,128)(2,1)S(1)} %get-tuple-element.33), channel_id=1, source_target_pairs={{0,6},{6,0},{1,7},{7,1},{2,8},{8,2},{3,9},{9,3},{4,10},{10,4},{5,1... | collective-permute-start | bytes 786440 | tf_op jit(solution)/shard_map/ppermute | solution.py:263
  100.8 4.4 %collective-permute-done.5 = bf16[4,128,256]{2,1,0:T(8,128)(2,1)S(1)} collective-permute-done((bf16[4,128,256]{2,1,0:T(8,128)(2,1)S(1)}, bf16[4,128,256]{2,1,0:T(8,128)(2,1)S(1)}, u32[]{:S(2)}, u32[]{:S(2)}) %collective-permute-start.5) | collective-permute-done | bytes 262176 | tf_op jit(solution)/shard_map/ppermute | solution.py:263
  105.3 3.7 %collective-permute-start.6 = (bf16[2,4,128,256]{3,2,1,0:T(8,128)(2,1)S(1)}, bf16[2,4,128,256]{3,2,1,0:T(8,128)(2,1)}, u32[]{:S(2)}, u32[]{:S(2)}) collective-permute-start(bf16[2,4,128,256]{3,2,1,0:T(8,128)(2,1)S(1)} %pad_maximum_fusion.states_ref), channel_id=1, source_target_pairs={{0,1},{1,0},{2,3},{3,2},{4,5},{5,4},{6,7},{7,6},{8,9},{9,8},{10,11... | collective-permute-start | bytes 1572872 | tf_op jit(solution)/shard_map/ppermute | solution.py:263
  112.3 11.9 %all-to-all-done.1 = bf16[16,64,1024]{2,1,0:T(8,128)(2,1)} async-done(((bf16[16,64,1024]{2,1,0:T(8,128)(2,1)}), bf16[16,64,1024]{2,1,0:T(8,128)(2,1)}, u32[]{:S(2)}, u32[]{:S(2)}) %all-to-all-start.1) | async-done | bytes 2097184 | tf_op jit(solution)/shard_map/all_to_all | solution.py:267
  124.2 5.0 %shard_map.108 = (bf16[128,1024]{1,0:T(8,128)(2,1)}, bf16[16,144,256]{2,1,0:T(8,128)(2,1)}) custom-call(bf16[128,1024]{1,0:T(8,128)(2,1)} %copy-done.25, f32[128,512]{1,0:T(8,128)} %convolution_multiply_fusion.scores_ref, bf16[128,1024]{1,0:T(8,128)(2,1)} %bitcast.39, s32[128,1]{1,0:T(8,128)} %copy.12.positive_ref, bf16[512,1024]{1,0:T(8,128)(2,1)} %copy-done.1, ...), custom_call_target="tpu_custom_call" | custom-call | flops 671088640 | bytes 4194304 | tf_op jit(solution)/shard_map/pallas_call | solution.py:39
  129.2 25.0 %all_to_all.26.grads_ref = bf16[16,144,256]{2,1,0:T(8,128)(2,1)} all-to-all(bf16[16,144,256]{2,1,0:T(8,128)(2,1)} %get-tuple-element.46), channel_id=1, replica_groups=mesh['zh'=4,'x'=4,'yh'=4,'yl'=2,'zl'=3,'c'=2] {'x','yl','c'}, dimensions={0} | all-to-all | bytes 2359296 | tf_op jit(solution)/shard_map/all_to_all | solution.py:267
  154.2 3.8 %shard_map.109 = (bf16[256,256]{1,0:T(8,128)(2,1)}, bf16[4,16,128]{2,1,0:T(8,128)(2,1)}) custom-call(s32[4]{0:T(128)} %copy-done.16, bf16[2,4,128,256]{3,2,1,0:T(8,128)(2,1)} %copy-done.26, bf16[2,4,128,256]{3,2,1,0:T(8,128)(2,1)} %collective-permute-done.6.pair_ref, bf16[16,144,256]{2,1,0:T(8,128)(2,1)} %all_to_all.26.grads_ref), custom_call_target="tpu_custom_call" | custom-call | flops 268435456 | bytes 2097152 | tf_op jit(solution)/shard_map/pallas_call | solution.py:39
  158.1 9.1 %all-to-all-start.3 = ((bf16[16,16,256]{2,1,0:T(8,128)(2,1)}), bf16[16,16,256]{2,1,0:T(8,128)(2,1)}, u32[]{:S(2)}, u32[]{:S(2)}) async-start(bf16[16,16,256]{2,1,0:T(8,128)(2,1)} %bitcast.43), calls=%async_computation.3 | async-start | bytes 262144 | tf_op jit(solution)/shard_map/all_to_all | solution.py:267
  167.2 6.2 %collective-permute-start.10 = (bf16[4,16,128]{2,1,0:T(8,128)(2,1)}, bf16[4,16,128]{2,1,0:T(8,128)(2,1)S(1)}, u32[]{:S(2)}, u32[]{:S(2)}) collective-permute-start(bf16[4,16,128]{2,1,0:T(8,128)(2,1)} %get-tuple-element.49.stats_ref), channel_id=1, source_target_pairs={{0,576},{192,0},{384,192},{576,384},{1,577},{193,1},{385,193},{577... | collective-permute-start | bytes 49160 | tf_op jit(solution)/shard_map/ppermute | solution.py:263
  173.4 2.5 %convolution_convert_fusion = bf16[128,1024]{1,0:T(8,128)(2,1)} fusion(bf16[128,1024]{1,0:T(8,128)(2,1)} %get-tuple-element.48, bf16[1024,1024]{1,0:T(8,128)(2,1)S(1)} %copy-done), kind=kOutput, calls=%fused_computation | convolution fusion | flops 268566528 | bytes 2621440 | tf_op jit(solution)/shard_map/dot_general | solution.py:51
  175.9 5.3 %all-to-all-done.3.parts_ref = bf16[16,16,256]{2,1,0:T(8,128)(2,1)} async-done(((bf16[16,16,256]{2,1,0:T(8,128)(2,1)}), bf16[16,16,256]{2,1,0:T(8,128)(2,1)}, u32[]{:S(2)}, u32[]{:S(2)}) %all-to-all-start.3) | async-done | bytes 131104 | tf_op jit(solution)/shard_map/all_to_all | solution.py:267
  181.2 1.7 shard_map.110
  182.9 7.4 %all-to-all-start.4 = ((bf16[48,16,256]{2,1,0:T(8,128)(2,1)}), bf16[48,16,256]{2,1,0:T(8,128)(2,1)S(1)}, u32[]{:S(2)}, u32[]{:S(2)}) async-start(bf16[48,16,256]{2,1,0:T(8,128)(2,1)} %shard_map.110), calls=%async_computation.4 | async-start | bytes 786432 | tf_op jit(solution)/shard_map/all_to_all | solution.py:267
  190.3 1.7 shard_map.111
  192.0 11.9 %all-to-all-done.4.parts_ref = bf16[48,16,256]{2,1,0:T(8,128)(2,1)S(1)} async-done(((bf16[48,16,256]{2,1,0:T(8,128)(2,1)}), bf16[48,16,256]{2,1,0:T(8,128)(2,1)S(1)}, u32[]{:S(2)}, u32[]{:S(2)}) %all-to-all-start.4) | async-done | bytes 393248 | tf_op jit(solution)/shard_map/all_to_all | solution.py:267
  204.6 1.7 shard_map.112
  (73 shorter events, 16.8 us)
Async XLA Ops:
  0.6 41.5 %collective-permute-start = (bf16[128,1024]{1,0:T(8,128)(2,1)}, bf16[128,1024]{1,0:T(8,128)(2,1)S(1)}, u32[]{:S(2)}, u32[]{:S(2)}) collective-permute-start(bf16[128,1024]{1,0:T(8,128)(2,1)} %bitcast.32), channel_id=1, source_target_pairs={{0,192},{192,384},{384,576},{576,0},{1,193},{193,385},{385,577},{5... | collective-permute-start | bytes 786440 | tf_op jit(solution)/shard_map/ppermute | solution.py:263
  9.1 33.1 %collective-permute-start.1 = (bf16[128,1024]{1,0:T(8,128)(2,1)}, bf16[128,1024]{1,0:T(8,128)(2,1)S(1)}, u32[]{:S(2)}, u32[]{:S(2)}) collective-permute-start(bf16[128,1024]{1,0:T(8,128)(2,1)} %bitcast.29), channel_id=1, source_target_pairs={{0,576},{192,0},{384,192},{576,384},{1,577},{193,1},{385,193},{577... | collective-permute-start | bytes 786440 | tf_op jit(solution)/shard_map/ppermute | solution.py:263
  45.6 5.9 %copy-start.4 = (bf16[1,1,128,1024]{3,2,1,0:T(8,128)(2,1)S(1)}, bf16[1,1,128,1024]{3,2,1,0:T(8,128)(2,1)}, u32[]{:S(2)}) copy-start(bf16[1,1,128,1024]{3,2,1,0:T(8,128)(2,1)} %param.8) | copy-start | bytes 786436
  45.6 5.9 %copy-start.5 = (bf16[1,1,128,1024]{3,2,1,0:T(8,128)(2,1)S(1)}, bf16[1,1,128,1024]{3,2,1,0:T(8,128)(2,1)}, u32[]{:S(2)}) copy-start(bf16[1,1,128,1024]{3,2,1,0:T(8,128)(2,1)} %param.9) | copy-start | bytes 786436
  45.6 22.3 %copy-start.18 = (s32[1,1,128]{2,1,0:T(1,128)S(1)}, s32[1,1,128]{2,1,0:T(1,128)}, u32[]{:S(2)}) copy-start(s32[1,1,128]{2,1,0:T(1,128)} %param.12) | copy-start | bytes 1540
  45.6 23.0 %copy-start = (bf16[1024,1024]{1,0:T(8,128)(2,1)S(1)}, bf16[1024,1024]{1,0:T(8,128)(2,1)}, u32[]{:S(2)}) copy-start(bf16[1024,1024]{1,0:T(8,128)(2,1)} %weight_ref.1) | copy-start | bytes 6291460
  45.6 78.6 %all-to-all-start.1 = ((bf16[16,64,1024]{2,1,0:T(8,128)(2,1)}), bf16[16,64,1024]{2,1,0:T(8,128)(2,1)}, u32[]{:S(2)}, u32[]{:S(2)}) async-start(bf16[16,64,1024]{2,1,0:T(8,128)(2,1)} %shard_map.106), calls=%async_computation.1 | async-start | bytes 4194304 | tf_op jit(solution)/shard_map/all_to_all | solution.py:267
  51.5 40.3 %copy-start.16 = (s32[4]{0:T(128)}, s32[4]{0:T(128)S(1)}, u32[]{:S(2)}) copy-start(s32[4]{0:T(128)S(1)} %pad_add_fusion.place_ref) | copy-start | bytes 52
  55.5 13.6 %collective-permute-start.2 = (bf16[128,1280]{1,0:T(8,128)(2,1)}, bf16[128,1280]{1,0:T(8,128)(2,1)S(1)}, u32[]{:S(2)}, u32[]{:S(2)}) collective-permute-start(bf16[128,1280]{1,0:T(8,128)(2,1)} %get-tuple-element.30), channel_id=1, source_target_pairs={{0,48},{48,96},{96,144},{144,0},{1,49},{49,97},{97,145},{145,1},{2... | collective-permute-start | bytes 983048 | tf_op jit(solution)/shard_map/ppermute | solution.py:263
  58.7 18.2 %collective-permute-start.3 = (bf16[128,1280]{1,0:T(8,128)(2,1)}, bf16[128,1280]{1,0:T(8,128)(2,1)S(1)}, u32[]{:S(2)}, u32[]{:S(2)}) collective-permute-start(bf16[128,1280]{1,0:T(8,128)(2,1)} %get-tuple-element.31), channel_id=1, source_target_pairs={{0,96},{48,144},{96,0},{144,48},{1,97},{49,145},{97,1},{145,49},{2... | collective-permute-start | bytes 983048 | tf_op jit(solution)/shard_map/ppermute | solution.py:263
  63.0 17.0 %collective-permute-start.4 = (bf16[128,1280]{1,0:T(8,128)(2,1)}, bf16[128,1280]{1,0:T(8,128)(2,1)S(1)}, u32[]{:S(2)}, u32[]{:S(2)}) collective-permute-start(bf16[128,1280]{1,0:T(8,128)(2,1)} %get-tuple-element.32), channel_id=1, source_target_pairs={{0,144},{48,0},{96,48},{144,96},{1,145},{49,1},{97,49},{145,97},{2... | collective-permute-start | bytes 983048 | tf_op jit(solution)/shard_map/ppermute | solution.py:263
  68.7 12.1 %copy-start.24 = (bf16[128,1024]{1,0:T(8,128)(2,1)S(1)}, bf16[128,1024]{1,0:T(8,128)(2,1)}, u32[]{:S(2)}) copy-start(bf16[128,1024]{1,0:T(8,128)(2,1)} %copy-done.23) | copy-start | bytes 786436
  68.7 17.2 %copy-start.22 = (bf16[128,1024]{1,0:T(8,128)(2,1)S(1)}, bf16[128,1024]{1,0:T(8,128)(2,1)}, u32[]{:S(2)}) copy-start(bf16[128,1024]{1,0:T(8,128)(2,1)} %copy-done.21) | copy-start | bytes 786436
  68.7 21.2 %copy-start.20 = (bf16[128,1024]{1,0:T(8,128)(2,1)S(1)}, bf16[128,1024]{1,0:T(8,128)(2,1)}, u32[]{:S(2)}) copy-start(bf16[128,1024]{1,0:T(8,128)(2,1)} %copy-done.19) | copy-start | bytes 786436
  69.1 41.4 %copy-start.25 = (bf16[128,1024]{1,0:T(8,128)(2,1)}, bf16[128,1024]{1,0:T(8,128)(2,1)S(1)}, u32[]{:S(2)}) copy-start(bf16[128,1024]{1,0:T(8,128)(2,1)S(1)} %convolution_convert_fusion.1.queries_ref) | copy-start | bytes 786436
  80.8 28.2 %collective-permute-start.7 = (bf16[128,1024]{1,0:T(8,128)(2,1)S(1)}, bf16[128,1024]{1,0:T(8,128)(2,1)S(1)}, u32[]{:S(2)}, u32[]{:S(2)}) collective-permute-start(bf16[128,1024]{1,0:T(8,128)(2,1)S(1)} %copy-done.24), channel_id=1, source_target_pairs={{0,144},{48,0},{96,48},{144,96},{1,145},{49,1},{97,49},{145,97},{2... | collective-permute-start | bytes 786440 | tf_op jit(solution)/shard_map/ppermute | solution.py:263
  85.9 23.1 %collective-permute-start.8 = (bf16[128,1024]{1,0:T(8,128)(2,1)S(1)}, bf16[128,1024]{1,0:T(8,128)(2,1)S(1)}, u32[]{:S(2)}, u32[]{:S(2)}) collective-permute-start(bf16[128,1024]{1,0:T(8,128)(2,1)S(1)} %copy-done.22), channel_id=1, source_target_pairs={{0,96},{48,144},{96,0},{144,48},{1,97},{49,145},{97,1},{145,49},{2... | collective-permute-start | bytes 786440 | tf_op jit(solution)/shard_map/ppermute | solution.py:263
  89.9 19.1 %collective-permute-start.9 = (bf16[128,1024]{1,0:T(8,128)(2,1)S(1)}, bf16[128,1024]{1,0:T(8,128)(2,1)S(1)}, u32[]{:S(2)}, u32[]{:S(2)}) collective-permute-start(bf16[128,1024]{1,0:T(8,128)(2,1)S(1)} %copy-done.20), channel_id=1, source_target_pairs={{0,48},{48,96},{96,144},{144,0},{1,49},{49,97},{97,145},{145,1},{2... | collective-permute-start | bytes 786440 | tf_op jit(solution)/shard_map/ppermute | solution.py:263
  92.8 1.0 copy-start.8
  93.8 1.0 copy-start.10
  96.4 14.2 %copy-start.1 = (bf16[512,1024]{1,0:T(8,128)(2,1)}, bf16[512,1024]{1,0:T(8,128)(2,1)S(1)}, u32[]{:S(2)}) copy-start(bf16[512,1024]{1,0:T(8,128)(2,1)S(1)} %get-tuple-element.34.blocks_ref) | copy-start | bytes 3145732
  96.4 8.8 %collective-permute-start.5 = (bf16[4,128,256]{2,1,0:T(8,128)(2,1)S(1)}, bf16[4,128,256]{2,1,0:T(8,128)(2,1)S(1)}, u32[]{:S(2)}, u32[]{:S(2)}) collective-permute-start(bf16[4,128,256]{2,1,0:T(8,128)(2,1)S(1)} %get-tuple-element.33), channel_id=1, source_target_pairs={{0,6},{6,0},{1,7},{7,1},{2,8},{8,2},{3,9},{9,3},{4,10},{10,4},{5,1... | collective-permute-start | bytes 786440 | tf_op jit(solution)/shard_map/ppermute | solution.py:263
  105.2 5.3 %copy-start.26 = (bf16[2,4,128,256]{3,2,1,0:T(8,128)(2,1)}, bf16[2,4,128,256]{3,2,1,0:T(8,128)(2,1)S(1)}, u32[]{:S(2)}) copy-start(bf16[2,4,128,256]{3,2,1,0:T(8,128)(2,1)S(1)} %pad_maximum_fusion.states_ref) | copy-start | bytes 1572868
  105.3 7.1 %collective-permute-start.6 = (bf16[2,4,128,256]{3,2,1,0:T(8,128)(2,1)S(1)}, bf16[2,4,128,256]{3,2,1,0:T(8,128)(2,1)}, u32[]{:S(2)}, u32[]{:S(2)}) collective-permute-start(bf16[2,4,128,256]{3,2,1,0:T(8,128)(2,1)S(1)} %pad_maximum_fusion.states_ref), channel_id=1, source_target_pairs={{0,1},{1,0},{2,3},{3,2},{4,5},{5,4},{6,7},{7,6},{8,9},{9,8},{10,11... | collective-permute-start | bytes 1572872 | tf_op jit(solution)/shard_map/ppermute | solution.py:263
  110.6 1.0 copy-start.2
  158.1 32.2 %copy-start.3 = (bf16[512,1024]{1,0:T(8,128)(2,1)S(1)}, bf16[512,1024]{1,0:T(8,128)(2,1)}, u32[]{:S(2)}) copy-start(bf16[512,1024]{1,0:T(8,128)(2,1)} %copy-done.2) | copy-start | bytes 3145732
  158.1 32.3 %copy-start.14 = (f32[128,512]{1,0:T(8,128)S(1)}, f32[128,512]{1,0:T(8,128)}, u32[]{:S(2)}) copy-start(f32[128,512]{1,0:T(8,128)} %copy-done.13) | copy-start | bytes 786436
  158.1 32.3 %copy-start.15 = (bf16[4,16,128]{2,1,0:T(8,128)(2,1)S(1)}, bf16[4,16,128]{2,1,0:T(8,128)(2,1)}, u32[]{:S(2)}) copy-start(bf16[4,16,128]{2,1,0:T(8,128)(2,1)} %get-tuple-element.49.stats_ref) | copy-start | bytes 49156
  158.1 32.3 %copy-start.17 = (s32[4]{0:T(128)S(1)}, s32[4]{0:T(128)}, u32[]{:S(2)}) copy-start(s32[4]{0:T(128)} %copy-done.16) | copy-start | bytes 52
  158.1 23.1 %all-to-all-start.3 = ((bf16[16,16,256]{2,1,0:T(8,128)(2,1)}), bf16[16,16,256]{2,1,0:T(8,128)(2,1)}, u32[]{:S(2)}, u32[]{:S(2)}) async-start(bf16[16,16,256]{2,1,0:T(8,128)(2,1)} %bitcast.43), calls=%async_computation.3 | async-start | bytes 262144 | tf_op jit(solution)/shard_map/all_to_all | solution.py:267
  167.2 8.7 %collective-permute-start.10 = (bf16[4,16,128]{2,1,0:T(8,128)(2,1)}, bf16[4,16,128]{2,1,0:T(8,128)(2,1)S(1)}, u32[]{:S(2)}, u32[]{:S(2)}) collective-permute-start(bf16[4,16,128]{2,1,0:T(8,128)(2,1)} %get-tuple-element.49.stats_ref), channel_id=1, source_target_pairs={{0,576},{192,0},{384,192},{576,384},{1,577},{193,1},{385,193},{577... | collective-permute-start | bytes 49160 | tf_op jit(solution)/shard_map/ppermute | solution.py:263
  182.9 21.0 %all-to-all-start.4 = ((bf16[48,16,256]{2,1,0:T(8,128)(2,1)}), bf16[48,16,256]{2,1,0:T(8,128)(2,1)S(1)}, u32[]{:S(2)}, u32[]{:S(2)}) async-start(bf16[48,16,256]{2,1,0:T(8,128)(2,1)} %shard_map.110), calls=%async_computation.4 | async-start | bytes 786432 | tf_op jit(solution)/shard_map/all_to_all | solution.py:267
  (10 other events, 7.8 us)

commit v5 on v4

--- a/solution.py
+++ b/solution.py
@@ -178,11 +178,11 @@
     *got_refs, blocks_ref, row_ref = refs
     x_at = place_ref[0]
     blocks_ref[:ROWS] = own_ref[...]
-    row_ref[x_at] = mine_ref[...]
+    row_ref[x_at] = mine_ref[...].astype(F32).T.astype(BF16)
     for step in range(1, X):
         got_ref = got_refs[step - 1]
         blocks_ref[step * ROWS : (step + 1) * ROWS] = got_ref[:, :D]
-        row_ref[(x_at + X - step) % X] = got_ref[:, D:]
+        row_ref[(x_at + X - step) % X] = got_ref[:, D:].astype(F32).T.astype(BF16)
 
 
 def gather_kernel(parts_ref, out_ref):
@@ -202,27 +202,17 @@
     scores_ref[...] = dot(own_ref[...], queries, (1, 1)) * (D**-0.5)
 
 
-def part_kernel(place_ref, states_ref, pair_ref, grads_ref, part_ref, stats_ref, total_ref):
-    at = pl.program_id(0)
+def part_kernel(place_ref, states_ref, pair_ref, grads_ref, part_ref, stats_ref):
     c_at, y_at = place_ref[1], place_ref[3]
-    states = [states_ref[0, 0], states_ref[1, 0], pair_ref[0, 0], pair_ref[1, 0]]
     mine, other = y_at * CORE, (1 - y_at) * CORE
-    froms = [mine + c_at, other + c_at, mine + 1 - c_at, other + 1 - c_at]
-    grads = [grads_ref[source, :ROWS] for source in froms]
-    term = dot(jnp.concatenate(states, axis=0), jnp.concatenate(grads, axis=0), (0, 0))
-    stats_ref[at] = grads_ref[mine + c_at, ROWS:, :ROWS]
-
-    @pl.when(at == 0)
-    def _():
-        total_ref[...] = term
-
-    @pl.when(at > 0)
-    def _():
-        total_ref[...] += term
-
-    @pl.when(at == pl.num_programs(0) - 1)
-    def _():
-        part_ref[...] = total_ref[...].astype(BF16)
+    states, grads = [], []
+    for at in range(X):
+        states += [states_ref[0, at], states_ref[1, at], pair_ref[0, at], pair_ref[1, at]]
+        for source in (mine + c_at, other + c_at, mine + 1 - c_at, other + 1 - c_at):
+            grads.append(grads_ref[at * QUARTERS + source, :ROWS])
+        stats_ref[at] = grads_ref[at * QUARTERS + mine + c_at, ROWS:, :ROWS]
+    states, grads = jnp.concatenate(states, axis=1), jnp.concatenate(grads, axis=0)
+    part_ref[...] = dot(states, grads, (1, 0)).astype(BF16)
 
 
 def passage_kernel(
@@ -327,7 +317,7 @@
         unpack_kernel,
         (
             jax.ShapeDtypeStruct((STOPS * ROWS, D), BF16),
-            jax.ShapeDtypeStruct((X, ROWS, D // X), BF16),
+            jax.ShapeDtypeStruct((X, D // X, ROWS), BF16),
         ),
         scalars=1,
         moved=4 << 20,
@@ -369,20 +359,9 @@
             jax.ShapeDtypeStruct((X, STAT_ROWS, ROWS), BF16),
         ),
         limit=LARGE,
+        scalars=1,
         flops=2 * ROWS * D * D,
         moved=2 << 20,
-        grid=(X,),
-        in_specs=[
-            pl.BlockSpec(memory_space=pltpu.SMEM),
-            pl.BlockSpec((Y_LO, 1, ROWS, D // X), lambda i: (0, i, 0, 0)),
-            pl.BlockSpec((Y_LO, 1, ROWS, D // X), lambda i: (0, i, 0, 0)),
-            pl.BlockSpec((QUARTERS, ROWS + STAT_ROWS, D // QUARTERS), lambda i: (i, 0, 0)),
-        ],
-        out_specs=[
-            pl.BlockSpec((D // X, D // QUARTERS), lambda i: (0, 0)),
-            pl.BlockSpec((X, STAT_ROWS, ROWS), lambda i: (0, 0, 0)),
-        ],
-        scratch_shapes=[pltpu.VMEM((D // X, D // QUARTERS), F32)],
     )(place, row_states, pair_states, row_grads)
     state_grads = dot(query_grad, proj_weight, (1, 1)).astype(BF16)
 

time: 208 us -> 206 us (level)
  no operation moved by 1% of the time
where the time goes in v5:
time: 206 us; the launch traced here: 205 us
  starting transfers between devices  74.1 us (36%)
  blocking collectives  45.2 us (22%)
  waiting for transfers between devices  42.8 us (21%)
  Pallas kernels  23.4 us (11%)
  local copies, waits for them, and re-layouts  14.6 us (7%)
  matrix products  4.14 us (2%)
    ppermute x11, starting transfers between devices, around(): return lax.ppermute(x, axis, [(i, (i + by) % count) for i in range(count)])  51.8 us
    all_to_all x2, blocking collectives, swap(): return lax.all_to_all(x, axis, split_axis=0, concat_axis=0, tiled=True)  45.2 us
    all_to_all x3, waiting for transfers between devices, swap(): return lax.all_to_all(x, axis, split_axis=0, concat_axis=0, tiled=True)  29 us
    pallas_call x10, Pallas kernels, run(): pl.pallas_call(kernel, out_shape=out_shape, compiler_params=pltpu.Compile...  23.4 us
    all_to_all x3, starting transfers between devices, swap(): return lax.all_to_all(x, axis, split_axis=0, concat_axis=0, tiled=True)  22.3 us
    ppermute x11, waiting for transfers between devices, around(): return lax.ppermute(x, axis, [(i, (i + by) % count) for i in range(count)])  13.8 us
    unnamed x57, local copies, waits for them, and re-layouts  11.5 us
  transfers between devices with their start and end apart: 14, of which 6 were waited for; matrix products, arithmetic and copies ran while one was open for 4% of the time, Pallas kernels for 4%

profile of v5, /device:TPU:1, one launch (start us, length us, event | category | flops | bytes accessed | tf_op | source)
XLA Modules:
  0.0 205.2 jit_solution(10295714972758890507)
XLA Ops:
  0.6 8.4 %collective-permute-start = (bf16[128,1024]{1,0:T(8,128)(2,1)}, bf16[128,1024]{1,0:T(8,128)(2,1)S(1)}, u32[]{:S(2)}, u32[]{:S(2)}) collective-permute-start(bf16[128,1024]{1,0:T(8,128)(2,1)} %bitcast.32), channel_id=1, source_target_pairs={{0,192},{192,384},{384,576},{576,0},{1,193},{193,385},{385,577},{5... | collective-permute-start | bytes 786440 | tf_op jit(solution)/shard_map/ppermute | solution.py:253
  9.1 8.6 %collective-permute-start.1 = (bf16[128,1024]{1,0:T(8,128)(2,1)}, bf16[128,1024]{1,0:T(8,128)(2,1)S(1)}, u32[]{:S(2)}, u32[]{:S(2)}) collective-permute-start(bf16[128,1024]{1,0:T(8,128)(2,1)} %bitcast.29), channel_id=1, source_target_pairs={{0,576},{192,0},{384,192},{576,384},{1,577},{193,1},{385,193},{577... | collective-permute-start | bytes 786440 | tf_op jit(solution)/shard_map/ppermute | solution.py:253
  19.0 3.1 %shard_map.105 = (s32[16,1,64]{2,1,0:T(1,128)}, bf16[1024,128]{1,0:T(8,128)(2,1)}) custom-call(s32[7,1,128]{2,1,0:T(1,128)} %bitcast.45, s32[7,1,128]{2,1,0:T(1,128)} %reshape.46.slot_ref, s32[1,1,128]{2,1,0:T(1,128)} %count_ref.1), custom_call_target="tpu_custom_call" | custom-call | bytes 1048576 | tf_op jit(solution)/shard_map/pallas_call | solution.py:39
  22.0 20.1 %all_to_all.25.incoming_ref = s32[16,1,64]{2,1,0:T(1,128)} all-to-all(s32[16,1,64]{2,1,0:T(1,128)} %get-tuple-element.36), channel_id=1, replica_groups=mesh['zh'=4,'x'=4,'yh'=4,'yl'=2,'zl'=3,'c'=2] {'zh','x'}, dimensions={0} | all-to-all | bytes 8192 | tf_op jit(solution)/shard_map/all_to_all | solution.py:257
  42.1 3.4 %shard_map.106 = bf16[16,64,1024]{2,1,0:T(8,128)(2,1)} custom-call(s32[16,1,64]{2,1,0:T(1,128)} %all_to_all.25.incoming_ref, bf16[512,1024]{1,0:T(8,128)(2,1)} %bitcast.46), custom_call_target="tpu_custom_call" | custom-call | flops 1073741824 | bytes 3145728 | tf_op jit(solution)/shard_map/pallas_call | solution.py:39
  45.6 5.8 %all-to-all-start.1 = ((bf16[16,64,1024]{2,1,0:T(8,128)(2,1)}), bf16[16,64,1024]{2,1,0:T(8,128)(2,1)}, u32[]{:S(2)}, u32[]{:S(2)}) async-start(bf16[16,64,1024]{2,1,0:T(8,128)(2,1)} %shard_map.106), calls=%async_computation.1 | async-start | bytes 4194304 | tf_op jit(solution)/shard_map/all_to_all | solution.py:257
  51.5 1.9 shard_map.103
  55.5 3.2 %collective-permute-start.2 = (bf16[128,1280]{1,0:T(8,128)(2,1)}, bf16[128,1280]{1,0:T(8,128)(2,1)S(1)}, u32[]{:S(2)}, u32[]{:S(2)}) collective-permute-start(bf16[128,1280]{1,0:T(8,128)(2,1)} %get-tuple-element.30), channel_id=1, source_target_pairs={{0,48},{48,96},{96,144},{144,0},{1,49},{49,97},{97,145},{145,1},{2... | collective-permute-start | bytes 983048 | tf_op jit(solution)/shard_map/ppermute | solution.py:253
  58.7 4.3 %collective-permute-start.3 = (bf16[128,1280]{1,0:T(8,128)(2,1)}, bf16[128,1280]{1,0:T(8,128)(2,1)S(1)}, u32[]{:S(2)}, u32[]{:S(2)}) collective-permute-start(bf16[128,1280]{1,0:T(8,128)(2,1)} %get-tuple-element.31), channel_id=1, source_target_pairs={{0,96},{48,144},{96,0},{144,48},{1,97},{49,145},{97,1},{145,49},{2... | collective-permute-start | bytes 983048 | tf_op jit(solution)/shard_map/ppermute | solution.py:253
  63.0 3.1 %collective-permute-start.4 = (bf16[128,1280]{1,0:T(8,128)(2,1)}, bf16[128,1280]{1,0:T(8,128)(2,1)S(1)}, u32[]{:S(2)}, u32[]{:S(2)}) collective-permute-start(bf16[128,1280]{1,0:T(8,128)(2,1)} %get-tuple-element.32), channel_id=1, source_target_pairs={{0,144},{48,0},{96,48},{144,96},{1,145},{49,1},{97,49},{145,97},{2... | collective-permute-start | bytes 983048 | tf_op jit(solution)/shard_map/ppermute | solution.py:253
  66.1 1.8 copy.11
  69.9 6.9 %collective-permute-done.3.refs_1_ = bf16[128,1280]{1,0:T(8,128)(2,1)S(1)} collective-permute-done((bf16[128,1280]{1,0:T(8,128)(2,1)}, bf16[128,1280]{1,0:T(8,128)(2,1)S(1)}, u32[]{:S(2)}, u32[]{:S(2)}) %collective-permute-start.3) | collective-permute-done | bytes 327712 | tf_op jit(solution)/shard_map/ppermute | solution.py:253
  77.6 2.4 %collective-permute-done.4.refs_2_ = bf16[128,1280]{1,0:T(8,128)(2,1)S(1)} collective-permute-done((bf16[128,1280]{1,0:T(8,128)(2,1)}, bf16[128,1280]{1,0:T(8,128)(2,1)S(1)}, u32[]{:S(2)}, u32[]{:S(2)}) %collective-permute-start.4) | collective-permute-done | bytes 327712 | tf_op jit(solution)/shard_map/ppermute | solution.py:253
  80.8 5.1 %collective-permute-start.7 = (bf16[128,1024]{1,0:T(8,128)(2,1)S(1)}, bf16[128,1024]{1,0:T(8,128)(2,1)S(1)}, u32[]{:S(2)}, u32[]{:S(2)}) collective-permute-start(bf16[128,1024]{1,0:T(8,128)(2,1)S(1)} %copy-done.24), channel_id=1, source_target_pairs={{0,144},{48,0},{96,48},{144,96},{1,145},{49,1},{97,49},{145,97},{2... | collective-permute-start | bytes 786440 | tf_op jit(solution)/shard_map/ppermute | solution.py:253
  85.9 4.0 %collective-permute-start.8 = (bf16[128,1024]{1,0:T(8,128)(2,1)S(1)}, bf16[128,1024]{1,0:T(8,128)(2,1)S(1)}, u32[]{:S(2)}, u32[]{:S(2)}) collective-permute-start(bf16[128,1024]{1,0:T(8,128)(2,1)S(1)} %copy-done.22), channel_id=1, source_target_pairs={{0,96},{48,144},{96,0},{144,48},{1,97},{49,145},{97,1},{145,49},{2... | collective-permute-start | bytes 786440 | tf_op jit(solution)/shard_map/ppermute | solution.py:253
  89.9 1.9 collective-permute-start.9
  96.4 3.2 %collective-permute-start.5 = (bf16[4,256,128]{2,1,0:T(8,128)(2,1)S(1)}, bf16[4,256,128]{2,1,0:T(8,128)(2,1)S(1)}, u32[]{:S(2)}, u32[]{:S(2)}) collective-permute-start(bf16[4,256,128]{2,1,0:T(8,128)(2,1)S(1)} %get-tuple-element.33), channel_id=1, source_target_pairs={{0,6},{6,0},{1,7},{7,1},{2,8},{8,2},{3,9},{9,3},{4,10},{10,4},{5,1... | collective-permute-start | bytes 786440 | tf_op jit(solution)/shard_map/ppermute | solution.py:253
  100.8 4.4 %collective-permute-done.5 = bf16[4,256,128]{2,1,0:T(8,128)(2,1)S(1)} collective-permute-done((bf16[4,256,128]{2,1,0:T(8,128)(2,1)S(1)}, bf16[4,256,128]{2,1,0:T(8,128)(2,1)S(1)}, u32[]{:S(2)}, u32[]{:S(2)}) %collective-permute-start.5) | collective-permute-done | bytes 262176 | tf_op jit(solution)/shard_map/ppermute | solution.py:253
  105.3 3.7 %collective-permute-start.6 = (bf16[2,4,256,128]{3,2,1,0:T(8,128)(2,1)S(1)}, bf16[2,4,256,128]{3,2,1,0:T(8,128)(2,1)}, u32[]{:S(2)}, u32[]{:S(2)}) collective-permute-start(bf16[2,4,256,128]{3,2,1,0:T(8,128)(2,1)S(1)} %pad_maximum_fusion.states_ref), channel_id=1, source_target_pairs={{0,1},{1,0},{2,3},{3,2},{4,5},{5,4},{6,7},{7,6},{8,9},{9,8},{10,11... | collective-permute-start | bytes 1572872 | tf_op jit(solution)/shard_map/ppermute | solution.py:253
  112.4 11.9 %all-to-all-done.1 = bf16[16,64,1024]{2,1,0:T(8,128)(2,1)} async-done(((bf16[16,64,1024]{2,1,0:T(8,128)(2,1)}), bf16[16,64,1024]{2,1,0:T(8,128)(2,1)}, u32[]{:S(2)}, u32[]{:S(2)}) %all-to-all-start.1) | async-done | bytes 2097184 | tf_op jit(solution)/shard_map/all_to_all | solution.py:257
  124.2 5.0 %shard_map.108 = (bf16[128,1024]{1,0:T(8,128)(2,1)}, bf16[16,144,256]{2,1,0:T(8,128)(2,1)}) custom-call(bf16[128,1024]{1,0:T(8,128)(2,1)} %copy-done.25, f32[128,512]{1,0:T(8,128)} %convolution_multiply_fusion.scores_ref, bf16[128,1024]{1,0:T(8,128)(2,1)} %bitcast.39, s32[128,1]{1,0:T(8,128)} %copy.12.positive_ref, bf16[512,1024]{1,0:T(8,128)(2,1)} %copy-done.1, ...), custom_call_target="tpu_custom_call" | custom-call | flops 671088640 | bytes 4194304 | tf_op jit(solution)/shard_map/pallas_call | solution.py:39
  129.2 25.0 %all_to_all.26.grads_ref = bf16[16,144,256]{2,1,0:T(8,128)(2,1)} all-to-all(bf16[16,144,256]{2,1,0:T(8,128)(2,1)} %get-tuple-element.46), channel_id=1, replica_groups=mesh['zh'=4,'x'=4,'yh'=4,'yl'=2,'zl'=3,'c'=2] {'x','yl','c'}, dimensions={0} | all-to-all | bytes 2359296 | tf_op jit(solution)/shard_map/all_to_all | solution.py:257
  154.2 2.7 %shard_map.109 = (bf16[256,256]{1,0:T(8,128)(2,1)}, bf16[4,16,128]{2,1,0:T(8,128)(2,1)}) custom-call(s32[4]{0:T(128)} %copy-done.16, bf16[2,4,256,128]{3,2,1,0:T(8,128)(2,1)} %copy-done.26, bf16[2,4,256,128]{3,2,1,0:T(8,128)(2,1)} %collective-permute-done.6.pair_ref, bf16[16,144,256]{2,1,0:T(8,128)(2,1)} %all_to_all.26.grads_ref), custom_call_target="tpu_custom_call" | custom-call | flops 268435456 | bytes 2097152 | tf_op jit(solution)/shard_map/pallas_call | solution.py:39
  157.0 9.1 %all-to-all-start.3 = ((bf16[16,16,256]{2,1,0:T(8,128)(2,1)}), bf16[16,16,256]{2,1,0:T(8,128)(2,1)}, u32[]{:S(2)}, u32[]{:S(2)}) async-start(bf16[16,16,256]{2,1,0:T(8,128)(2,1)} %bitcast.43), calls=%async_computation.3 | async-start | bytes 262144 | tf_op jit(solution)/shard_map/all_to_all | solution.py:257
  166.1 6.2 %collective-permute-start.10 = (bf16[4,16,128]{2,1,0:T(8,128)(2,1)}, bf16[4,16,128]{2,1,0:T(8,128)(2,1)S(1)}, u32[]{:S(2)}, u32[]{:S(2)}) collective-permute-start(bf16[4,16,128]{2,1,0:T(8,128)(2,1)} %get-tuple-element.49.stats_ref), channel_id=1, source_target_pairs={{0,576},{192,0},{384,192},{576,384},{1,577},{193,1},{385,193},{577... | collective-permute-start | bytes 49160 | tf_op jit(solution)/shard_map/ppermute | solution.py:253
  172.3 2.5 %convolution_convert_fusion = bf16[128,1024]{1,0:T(8,128)(2,1)} fusion(bf16[128,1024]{1,0:T(8,128)(2,1)} %get-tuple-element.48, bf16[1024,1024]{1,0:T(8,128)(2,1)S(1)} %copy-done), kind=kOutput, calls=%fused_computation | convolution fusion | flops 268566528 | bytes 2621440 | tf_op jit(solution)/shard_map/dot_general | solution.py:51
  174.8 5.3 %all-to-all-done.3.parts_ref = bf16[16,16,256]{2,1,0:T(8,128)(2,1)} async-done(((bf16[16,16,256]{2,1,0:T(8,128)(2,1)}), bf16[16,16,256]{2,1,0:T(8,128)(2,1)}, u32[]{:S(2)}, u32[]{:S(2)}) %all-to-all-start.3) | async-done | bytes 131104 | tf_op jit(solution)/shard_map/all_to_all | solution.py:257
  180.1 1.7 shard_map.110
  181.8 7.4 %all-to-all-start.4 = ((bf16[48,16,256]{2,1,0:T(8,128)(2,1)}), bf16[48,16,256]{2,1,0:T(8,128)(2,1)S(1)}, u32[]{:S(2)}, u32[]{:S(2)}) async-start(bf16[48,16,256]{2,1,0:T(8,128)(2,1)} %shard_map.110), calls=%async_computation.4 | async-start | bytes 786432 | tf_op jit(solution)/shard_map/all_to_all | solution.py:257
  189.2 1.7 shard_map.111
  190.9 11.9 %all-to-all-done.4.parts_ref = bf16[48,16,256]{2,1,0:T(8,128)(2,1)S(1)} async-done(((bf16[48,16,256]{2,1,0:T(8,128)(2,1)}), bf16[48,16,256]{2,1,0:T(8,128)(2,1)S(1)}, u32[]{:S(2)}, u32[]{:S(2)}) %all-to-all-start.4) | async-done | bytes 393248 | tf_op jit(solution)/shard_map/all_to_all | solution.py:257
  203.5 1.7 shard_map.112
  (73 shorter events, 16.8 us)
Async XLA Ops:
  0.6 41.5 %collective-permute-start = (bf16[128,1024]{1,0:T(8,128)(2,1)}, bf16[128,1024]{1,0:T(8,128)(2,1)S(1)}, u32[]{:S(2)}, u32[]{:S(2)}) collective-permute-start(bf16[128,1024]{1,0:T(8,128)(2,1)} %bitcast.32), channel_id=1, source_target_pairs={{0,192},{192,384},{384,576},{576,0},{1,193},{193,385},{385,577},{5... | collective-permute-start | bytes 786440 | tf_op jit(solution)/shard_map/ppermute | solution.py:253
  9.1 33.1 %collective-permute-start.1 = (bf16[128,1024]{1,0:T(8,128)(2,1)}, bf16[128,1024]{1,0:T(8,128)(2,1)S(1)}, u32[]{:S(2)}, u32[]{:S(2)}) collective-permute-start(bf16[128,1024]{1,0:T(8,128)(2,1)} %bitcast.29), channel_id=1, source_target_pairs={{0,576},{192,0},{384,192},{576,384},{1,577},{193,1},{385,193},{577... | collective-permute-start | bytes 786440 | tf_op jit(solution)/shard_map/ppermute | solution.py:253
  45.6 5.9 %copy-start.4 = (bf16[1,1,128,1024]{3,2,1,0:T(8,128)(2,1)S(1)}, bf16[1,1,128,1024]{3,2,1,0:T(8,128)(2,1)}, u32[]{:S(2)}) copy-start(bf16[1,1,128,1024]{3,2,1,0:T(8,128)(2,1)} %param.8) | copy-start | bytes 786436
  45.6 5.9 %copy-start.5 = (bf16[1,1,128,1024]{3,2,1,0:T(8,128)(2,1)S(1)}, bf16[1,1,128,1024]{3,2,1,0:T(8,128)(2,1)}, u32[]{:S(2)}) copy-start(bf16[1,1,128,1024]{3,2,1,0:T(8,128)(2,1)} %param.9) | copy-start | bytes 786436
  45.6 22.3 %copy-start.18 = (s32[1,1,128]{2,1,0:T(1,128)S(1)}, s32[1,1,128]{2,1,0:T(1,128)}, u32[]{:S(2)}) copy-start(s32[1,1,128]{2,1,0:T(1,128)} %param.12) | copy-start | bytes 1540
  45.6 23.0 %copy-start = (bf16[1024,1024]{1,0:T(8,128)(2,1)S(1)}, bf16[1024,1024]{1,0:T(8,128)(2,1)}, u32[]{:S(2)}) copy-start(bf16[1024,1024]{1,0:T(8,128)(2,1)} %weight_ref.1) | copy-start | bytes 6291460
  45.6 78.6 %all-to-all-start.1 = ((bf16[16,64,1024]{2,1,0:T(8,128)(2,1)}), bf16[16,64,1024]{2,1,0:T(8,128)(2,1)}, u32[]{:S(2)}, u32[]{:S(2)}) async-start(bf16[16,64,1024]{2,1,0:T(8,128)(2,1)} %shard_map.106), calls=%async_computation.1 | async-start | bytes 4194304 | tf_op jit(solution)/shard_map/all_to_all | solution.py:257
  51.5 40.3 %copy-start.16 = (s32[4]{0:T(128)}, s32[4]{0:T(128)S(1)}, u32[]{:S(2)}) copy-start(s32[4]{0:T(128)S(1)} %pad_add_fusion.place_ref) | copy-start | bytes 52
  55.5 13.6 %collective-permute-start.2 = (bf16[128,1280]{1,0:T(8,128)(2,1)}, bf16[128,1280]{1,0:T(8,128)(2,1)S(1)}, u32[]{:S(2)}, u32[]{:S(2)}) collective-permute-start(bf16[128,1280]{1,0:T(8,128)(2,1)} %get-tuple-element.30), channel_id=1, source_target_pairs={{0,48},{48,96},{96,144},{144,0},{1,49},{49,97},{97,145},{145,1},{2... | collective-permute-start | bytes 983048 | tf_op jit(solution)/shard_map/ppermute | solution.py:253
  58.7 18.2 %collective-permute-start.3 = (bf16[128,1280]{1,0:T(8,128)(2,1)}, bf16[128,1280]{1,0:T(8,128)(2,1)S(1)}, u32[]{:S(2)}, u32[]{:S(2)}) collective-permute-start(bf16[128,1280]{1,0:T(8,128)(2,1)} %get-tuple-element.31), channel_id=1, source_target_pairs={{0,96},{48,144},{96,0},{144,48},{1,97},{49,145},{97,1},{145,49},{2... | collective-permute-start | bytes 983048 | tf_op jit(solution)/shard_map/ppermute | solution.py:253
  63.0 17.0 %collective-permute-start.4 = (bf16[128,1280]{1,0:T(8,128)(2,1)}, bf16[128,1280]{1,0:T(8,128)(2,1)S(1)}, u32[]{:S(2)}, u32[]{:S(2)}) collective-permute-start(bf16[128,1280]{1,0:T(8,128)(2,1)} %get-tuple-element.32), channel_id=1, source_target_pairs={{0,144},{48,0},{96,48},{144,96},{1,145},{49,1},{97,49},{145,97},{2... | collective-permute-start | bytes 983048 | tf_op jit(solution)/shard_map/ppermute | solution.py:253
  68.7 12.1 %copy-start.24 = (bf16[128,1024]{1,0:T(8,128)(2,1)S(1)}, bf16[128,1024]{1,0:T(8,128)(2,1)}, u32[]{:S(2)}) copy-start(bf16[128,1024]{1,0:T(8,128)(2,1)} %copy-done.23) | copy-start | bytes 786436
  68.7 17.2 %copy-start.22 = (bf16[128,1024]{1,0:T(8,128)(2,1)S(1)}, bf16[128,1024]{1,0:T(8,128)(2,1)}, u32[]{:S(2)}) copy-start(bf16[128,1024]{1,0:T(8,128)(2,1)} %copy-done.21) | copy-start | bytes 786436
  68.7 21.2 %copy-start.20 = (bf16[128,1024]{1,0:T(8,128)(2,1)S(1)}, bf16[128,1024]{1,0:T(8,128)(2,1)}, u32[]{:S(2)}) copy-start(bf16[128,1024]{1,0:T(8,128)(2,1)} %copy-done.19) | copy-start | bytes 786436
  69.1 41.5 %copy-start.25 = (bf16[128,1024]{1,0:T(8,128)(2,1)}, bf16[128,1024]{1,0:T(8,128)(2,1)S(1)}, u32[]{:S(2)}) copy-start(bf16[128,1024]{1,0:T(8,128)(2,1)S(1)} %convolution_convert_fusion.1.queries_ref) | copy-start | bytes 786436
  80.8 28.3 %collective-permute-start.7 = (bf16[128,1024]{1,0:T(8,128)(2,1)S(1)}, bf16[128,1024]{1,0:T(8,128)(2,1)S(1)}, u32[]{:S(2)}, u32[]{:S(2)}) collective-permute-start(bf16[128,1024]{1,0:T(8,128)(2,1)S(1)} %copy-done.24), channel_id=1, source_target_pairs={{0,144},{48,0},{96,48},{144,96},{1,145},{49,1},{97,49},{145,97},{2... | collective-permute-start | bytes 786440 | tf_op jit(solution)/shard_map/ppermute | solution.py:253
  85.9 23.2 %collective-permute-start.8 = (bf16[128,1024]{1,0:T(8,128)(2,1)S(1)}, bf16[128,1024]{1,0:T(8,128)(2,1)S(1)}, u32[]{:S(2)}, u32[]{:S(2)}) collective-permute-start(bf16[128,1024]{1,0:T(8,128)(2,1)S(1)} %copy-done.22), channel_id=1, source_target_pairs={{0,96},{48,144},{96,0},{144,48},{1,97},{49,145},{97,1},{145,49},{2... | collective-permute-start | bytes 786440 | tf_op jit(solution)/shard_map/ppermute | solution.py:253
  89.9 19.1 %collective-permute-start.9 = (bf16[128,1024]{1,0:T(8,128)(2,1)S(1)}, bf16[128,1024]{1,0:T(8,128)(2,1)S(1)}, u32[]{:S(2)}, u32[]{:S(2)}) collective-permute-start(bf16[128,1024]{1,0:T(8,128)(2,1)S(1)} %copy-done.20), channel_id=1, source_target_pairs={{0,48},{48,96},{96,144},{144,0},{1,49},{49,97},{97,145},{145,1},{2... | collective-permute-start | bytes 786440 | tf_op jit(solution)/shard_map/ppermute | solution.py:253
  92.8 1.0 copy-start.8
  94.7 1.0 copy-start.12
  96.4 14.2 %copy-start.1 = (bf16[512,1024]{1,0:T(8,128)(2,1)}, bf16[512,1024]{1,0:T(8,128)(2,1)S(1)}, u32[]{:S(2)}) copy-start(bf16[512,1024]{1,0:T(8,128)(2,1)S(1)} %get-tuple-element.34.blocks_ref) | copy-start | bytes 3145732
  96.4 8.8 %collective-permute-start.5 = (bf16[4,256,128]{2,1,0:T(8,128)(2,1)S(1)}, bf16[4,256,128]{2,1,0:T(8,128)(2,1)S(1)}, u32[]{:S(2)}, u32[]{:S(2)}) collective-permute-start(bf16[4,256,128]{2,1,0:T(8,128)(2,1)S(1)} %get-tuple-element.33), channel_id=1, source_target_pairs={{0,6},{6,0},{1,7},{7,1},{2,8},{8,2},{3,9},{9,3},{4,10},{10,4},{5,1... | collective-permute-start | bytes 786440 | tf_op jit(solution)/shard_map/ppermute | solution.py:253
  105.3 5.3 %copy-start.26 = (bf16[2,4,256,128]{3,2,1,0:T(8,128)(2,1)}, bf16[2,4,256,128]{3,2,1,0:T(8,128)(2,1)S(1)}, u32[]{:S(2)}) copy-start(bf16[2,4,256,128]{3,2,1,0:T(8,128)(2,1)S(1)} %pad_maximum_fusion.states_ref) | copy-start | bytes 1572868
  105.3 7.1 %collective-permute-start.6 = (bf16[2,4,256,128]{3,2,1,0:T(8,128)(2,1)S(1)}, bf16[2,4,256,128]{3,2,1,0:T(8,128)(2,1)}, u32[]{:S(2)}, u32[]{:S(2)}) collective-permute-start(bf16[2,4,256,128]{3,2,1,0:T(8,128)(2,1)S(1)} %pad_maximum_fusion.states_ref), channel_id=1, source_target_pairs={{0,1},{1,0},{2,3},{3,2},{4,5},{5,4},{6,7},{7,6},{8,9},{9,8},{10,11... | collective-permute-start | bytes 1572872 | tf_op jit(solution)/shard_map/ppermute | solution.py:253
  110.6 1.0 copy-start.2
  156.9 32.2 %copy-start.3 = (bf16[512,1024]{1,0:T(8,128)(2,1)S(1)}, bf16[512,1024]{1,0:T(8,128)(2,1)}, u32[]{:S(2)}) copy-start(bf16[512,1024]{1,0:T(8,128)(2,1)} %copy-done.2) | copy-start | bytes 3145732
  156.9 32.2 %copy-start.14 = (f32[128,512]{1,0:T(8,128)S(1)}, f32[128,512]{1,0:T(8,128)}, u32[]{:S(2)}) copy-start(f32[128,512]{1,0:T(8,128)} %copy-done.13) | copy-start | bytes 786436
  156.9 32.3 %copy-start.15 = (bf16[4,16,128]{2,1,0:T(8,128)(2,1)S(1)}, bf16[4,16,128]{2,1,0:T(8,128)(2,1)}, u32[]{:S(2)}) copy-start(bf16[4,16,128]{2,1,0:T(8,128)(2,1)} %get-tuple-element.49.stats_ref) | copy-start | bytes 49156
  156.9 32.3 %copy-start.17 = (s32[4]{0:T(128)S(1)}, s32[4]{0:T(128)}, u32[]{:S(2)}) copy-start(s32[4]{0:T(128)} %copy-done.16) | copy-start | bytes 52
  157.0 23.1 %all-to-all-start.3 = ((bf16[16,16,256]{2,1,0:T(8,128)(2,1)}), bf16[16,16,256]{2,1,0:T(8,128)(2,1)}, u32[]{:S(2)}, u32[]{:S(2)}) async-start(bf16[16,16,256]{2,1,0:T(8,128)(2,1)} %bitcast.43), calls=%async_computation.3 | async-start | bytes 262144 | tf_op jit(solution)/shard_map/all_to_all | solution.py:257
  166.1 8.7 %collective-permute-start.10 = (bf16[4,16,128]{2,1,0:T(8,128)(2,1)}, bf16[4,16,128]{2,1,0:T(8,128)(2,1)S(1)}, u32[]{:S(2)}, u32[]{:S(2)}) collective-permute-start(bf16[4,16,128]{2,1,0:T(8,128)(2,1)} %get-tuple-element.49.stats_ref), channel_id=1, source_target_pairs={{0,576},{192,0},{384,192},{576,384},{1,577},{193,1},{385,193},{577... | collective-permute-start | bytes 49160 | tf_op jit(solution)/shard_map/ppermute | solution.py:253
  181.8 21.0 %all-to-all-start.4 = ((bf16[48,16,256]{2,1,0:T(8,128)(2,1)}), bf16[48,16,256]{2,1,0:T(8,128)(2,1)S(1)}, u32[]{:S(2)}, u32[]{:S(2)}) async-start(bf16[48,16,256]{2,1,0:T(8,128)(2,1)} %shard_map.110), calls=%async_computation.4 | async-start | bytes 786432 | tf_op jit(solution)/shard_map/all_to_all | solution.py:257
  (10 other events, 7.8 us)

commit v6 on v5

--- a/solution.py
+++ b/solution.py
@@ -152,7 +152,7 @@
         quarters_ref[to, ROWS:] = turned
 
 
-def pack_kernel(place_ref, own_ref, below_ref, above_ref, states_ref, *refs):
+def pack_kernel(place_ref, own_ref, below_ref, states_ref, *refs):
     x_at = place_ref[0]
     share = D // MEMBERS
 
@@ -164,14 +164,18 @@
             piece = cut if piece is None else jnp.where(x_to == x_of, cut, piece)
         return piece
 
-    first_refs, second_refs, mine_ref = refs[: X - 1], refs[X - 1 : 2 * X - 2], refs[-1]
+    *first_refs, mine_ref = refs
     mine_ref[...] = columns(x_at)
     for step in range(1, X):
-        wraps = x_at + step >= X
-        first_ref, second_ref = first_refs[step - 1], second_refs[step - 1]
-        first_ref[:, :D] = jnp.where(wraps, below_ref[...], own_ref[...])
+        first_ref = first_refs[step - 1]
+        first_ref[:, :D] = jnp.where(x_at + step >= X, below_ref[...], own_ref[...])
         first_ref[:, D:] = columns((x_at + step) % X)
-        second_ref[...] = jnp.where(wraps, states_ref[...], above_ref[...])
+
+
+def second_kernel(place_ref, above_ref, states_ref, *refs):
+    for step in range(1, X):
+        wraps = place_ref[0] + step >= X
+        refs[step - 1][...] = jnp.where(wraps, states_ref[...], above_ref[...])
 
 
 def unpack_kernel(place_ref, own_ref, mine_ref, *refs):
@@ -281,8 +285,8 @@
     incoming = swap(request, BLK)
 
     below = around(own, "zh", 1)
-    above = around(states, "zh", -1)
-    incoming = lax.optimization_barrier((incoming, below, above))[0]
+    incoming = lax.optimization_barrier((incoming, below))[0]
+    above = around(lax.optimization_barrier((states, incoming))[0], "zh", -1)
     served = call(
         serve_kernel,
         jax.ShapeDtypeStruct((MEMBERS, CAP, D), BF16),
@@ -305,13 +309,18 @@
     wide = jax.ShapeDtypeStruct((ROWS, D + D // X), BF16)
     sends = call(
         pack_kernel,
-        (wide,) * (X - 1)
-        + (jax.ShapeDtypeStruct((ROWS, D), BF16),) * (X - 1)
-        + (jax.ShapeDtypeStruct((ROWS, D // X), BF16),),
+        (wide,) * (X - 1) + (jax.ShapeDtypeStruct((ROWS, D // X), BF16),),
         scalars=1,
-        moved=6 << 20,
-    )(place, own, below, above, states)
+        moved=4 << 20,
+    )(place, own, lax.optimization_barrier((below, served))[0], states)
     mine = sends[-1]
+    second = call(
+        second_kernel,
+        (jax.ShapeDtypeStruct((ROWS, D), BF16),) * (X - 1),
+        scalars=1,
+        flops=32 * 10**9,
+        moved=4 << 20,
+    )(place, above, states)
     got = [around(send, "x", step + 1) for step, send in enumerate(sends[: X - 1])]
     blocks, row_states = call(
         unpack_kernel,
@@ -325,7 +334,7 @@
     next_states = around(row_states, "yl", 1)
     row_states = jnp.stack([row_states, next_states])
     pair_states = around(row_states, "c", 1)
-    late = lax.optimization_barrier((*sends[X - 1 : -1], *got))[: X - 1]
+    late = lax.optimization_barrier((*second, *got))[: X - 1]
     late = [around(send, "x", step + 1) for step, send in enumerate(late)]
     asking, own_scores = call(
         asking_kernel,

time: 206 us -> 216 us (1.049)
  blocking collectives: 45.2 us -> 57.1 us
  starting transfers between devices: 74.1 us -> 85 us
  local copies, waits for them, and re-layouts: 14.6 us -> 5.39 us
  waiting for transfers between devices: 42.8 us -> 38.1 us
    all_to_all x3, starting transfers between devices: 22.3 us -> 35.4 us  [swap(): return lax.all_to_all(x, axis, split_axis=0, concat_axis=0, tiled=True)]
    all_to_all x2, blocking collectives: 45.2 us -> 57.1 us  [swap(): return lax.all_to_all(x, axis, split_axis=0, concat_axis=0, tiled=True)]
    all_to_all x3, waiting for transfers between devices: 29 us -> 17.2 us  [swap(): return lax.all_to_all(x, axis, split_axis=0, concat_axis=0, tiled=True)]
    unnamed x57 -> x37, local copies, waits for them, and re-layouts: 11.5 us -> 3.21 us
    ppermute x11, waiting for transfers between devices: 13.8 us -> 20.9 us  [around(): return lax.ppermute(x, axis, [(i, (i + by) % count) for i in range(count)])]
    pallas_call x10 -> x11, Pallas kernels: 23.4 us -> 23.7 us  [run(): pl.pallas_call(kernel, out_shape=out_shape, compiler_params=pltpu.Compile...]
  transfers between devices with their start and end apart: 14 -> 14, of which waited for: 6 -> 7; matrix products, arithmetic and copies ran while one was open for 4% -> 4% of each run, Pallas kernels for 4% -> 6%
where the time goes in v6:
time: 216 us; the launch traced here: 215 us
  starting transfers between devices  85 us (39%)
  blocking collectives  57.1 us (26%)
  waiting for transfers between devices  38.1 us (18%)
  Pallas kernels  23.7 us (11%)
  local copies, waits for them, and re-layouts  5.39 us (2%)
  matrix products  4.84 us (2%)
    all_to_all x2, blocking collectives, swap(): return lax.all_to_all(x, axis, split_axis=0, concat_axis=0, tiled=True)  57.1 us
    ppermute x11, starting transfers between devices, around(): return lax.ppermute(x, axis, [(i, (i + by) % count) for i in range(count)])  49.7 us
    all_to_all x3, starting transfers between devices, swap(): return lax.all_to_all(x, axis, split_axis=0, concat_axis=0, tiled=True)  35.4 us
    pallas_call x11, Pallas kernels, run(): pl.pallas_call(kernel, out_shape=out_shape, compiler_params=pltpu.Compile...  23.7 us
    ppermute x11, waiting for transfers between devices, around(): return lax.ppermute(x, axis, [(i, (i + by) % count) for i in range(count)])  20.9 us
    all_to_all x3, waiting for transfers between devices, swap(): return lax.all_to_all(x, axis, split_axis=0, concat_axis=0, tiled=True)  17.2 us
  transfers between devices with their start and end apart: 14, of which 7 were waited for; matrix products, arithmetic and copies ran while one was open for 4% of the time, Pallas kernels for 6%

profile of v6, /device:TPU:1, one launch (start us, length us, event | category | flops | bytes accessed | tf_op | source)
XLA Modules:
  0.0 215.2 jit_solution(18154599649886151322)
XLA Ops:
  0.6 8.4 %collective-permute-start = (bf16[128,1024]{1,0:T(8,128)(2,1)}, bf16[128,1024]{1,0:T(8,128)(2,1)S(1)}, u32[]{:S(2)}, u32[]{:S(2)}) collective-permute-start(bf16[128,1024]{1,0:T(8,128)(2,1)} %bitcast.33), channel_id=1, source_target_pairs={{0,192},{192,384},{384,576},{576,0},{1,193},{193,385},{385,577},{5... | collective-permute-start | bytes 786440 | tf_op jit(solution)/shard_map/ppermute | solution.py:257
  10.4 3.1 %shard_map.103 = (s32[16,1,64]{2,1,0:T(1,128)}, bf16[1024,128]{1,0:T(8,128)(2,1)}) custom-call(s32[7,1,128]{2,1,0:T(1,128)} %bitcast.46, s32[7,1,128]{2,1,0:T(1,128)} %reshape.45.slot_ref, s32[1,1,128]{2,1,0:T(1,128)} %count_ref.1), custom_call_target="tpu_custom_call" | custom-call | bytes 1048576 | tf_op jit(solution)/shard_map/pallas_call | solution.py:39
  13.4 26.6 %all_to_all.25.incoming_ref = s32[16,1,64]{2,1,0:T(1,128)} all-to-all(s32[16,1,64]{2,1,0:T(1,128)} %get-tuple-element.31), channel_id=1, replica_groups=mesh['zh'=4,'x'=4,'yh'=4,'yl'=2,'zl'=3,'c'=2] {'zh','x'}, dimensions={0} | all-to-all | bytes 8192 | tf_op jit(solution)/shard_map/all_to_all | solution.py:261
  40.0 2.2 %collective-permute-start.6 = (bf16[128,1024]{1,0:T(8,128)(2,1)}, bf16[128,1024]{1,0:T(8,128)(2,1)}, u32[]{:S(2)}, u32[]{:S(2)}) collective-permute-start(bf16[128,1024]{1,0:T(8,128)(2,1)} %bitcast.29), channel_id=1, source_target_pairs={{0,576},{192,0},{384,192},{576,384},{1,577},{193,1},{385,193},{577... | collective-permute-start | bytes 786440 | tf_op jit(solution)/shard_map/ppermute | solution.py:257
  42.3 3.4 %shard_map.104 = bf16[16,64,1024]{2,1,0:T(8,128)(2,1)} custom-call(s32[16,1,64]{2,1,0:T(1,128)} %all_to_all.25.incoming_ref, bf16[512,1024]{1,0:T(8,128)(2,1)} %bitcast.47), custom_call_target="tpu_custom_call" | custom-call | flops 1073741824 | bytes 3145728 | tf_op jit(solution)/shard_map/pallas_call | solution.py:39
  45.8 6.3 %all-to-all-start.1 = ((bf16[16,64,1024]{2,1,0:T(8,128)(2,1)}), bf16[16,64,1024]{2,1,0:T(8,128)(2,1)}, u32[]{:S(2)}, u32[]{:S(2)}) async-start(bf16[16,64,1024]{2,1,0:T(8,128)(2,1)} %shard_map.104), calls=%async_computation.1 | async-start | bytes 4194304 | tf_op jit(solution)/shard_map/all_to_all | solution.py:261
  55.9 3.2 %collective-permute-start.1 = (bf16[128,1280]{1,0:T(8,128)(2,1)S(1)}, bf16[128,1280]{1,0:T(8,128)(2,1)S(1)}, u32[]{:S(2)}, u32[]{:S(2)}) collective-permute-start(bf16[128,1280]{1,0:T(8,128)(2,1)S(1)} %get-tuple-element.35), channel_id=1, source_target_pairs={{0,48},{48,96},{96,144},{144,0},{1,49},{49,97},{97,145},{145,1},{2... | collective-permute-start | bytes 983048 | tf_op jit(solution)/shard_map/ppermute | solution.py:257
  59.1 4.3 %collective-permute-start.2 = (bf16[128,1280]{1,0:T(8,128)(2,1)S(1)}, bf16[128,1280]{1,0:T(8,128)(2,1)S(1)}, u32[]{:S(2)}, u32[]{:S(2)}) collective-permute-start(bf16[128,1280]{1,0:T(8,128)(2,1)S(1)} %get-tuple-element.36), channel_id=1, source_target_pairs={{0,96},{48,144},{96,0},{144,48},{1,97},{49,145},{97,1},{145,49},{2... | collective-permute-start | bytes 983048 | tf_op jit(solution)/shard_map/ppermute | solution.py:257
  63.5 3.2 %collective-permute-start.3 = (bf16[128,1280]{1,0:T(8,128)(2,1)S(1)}, bf16[128,1280]{1,0:T(8,128)(2,1)S(1)}, u32[]{:S(2)}, u32[]{:S(2)}) collective-permute-start(bf16[128,1280]{1,0:T(8,128)(2,1)S(1)} %get-tuple-element.37), channel_id=1, source_target_pairs={{0,144},{48,0},{96,48},{144,96},{1,145},{49,1},{97,49},{145,97},{2... | collective-permute-start | bytes 983048 | tf_op jit(solution)/shard_map/ppermute | solution.py:257
  67.8 3.7 %collective-permute-done.1.refs_0_ = bf16[128,1280]{1,0:T(8,128)(2,1)S(1)} collective-permute-done((bf16[128,1280]{1,0:T(8,128)(2,1)S(1)}, bf16[128,1280]{1,0:T(8,128)(2,1)S(1)}, u32[]{:S(2)}, u32[]{:S(2)}) %collective-permute-start.1) | collective-permute-done | bytes 327712 | tf_op jit(solution)/shard_map/ppermute | solution.py:257
  71.4 7.4 %collective-permute-done.2.refs_1_ = bf16[128,1280]{1,0:T(8,128)(2,1)S(1)} collective-permute-done((bf16[128,1280]{1,0:T(8,128)(2,1)S(1)}, bf16[128,1280]{1,0:T(8,128)(2,1)S(1)}, u32[]{:S(2)}, u32[]{:S(2)}) %collective-permute-start.2) | collective-permute-done | bytes 327712 | tf_op jit(solution)/shard_map/ppermute | solution.py:257
  80.0 5.2 %collective-permute-start.7 = (bf16[128,1024]{1,0:T(8,128)(2,1)S(1)}, bf16[128,1024]{1,0:T(8,128)(2,1)S(1)}, u32[]{:S(2)}, u32[]{:S(2)}) collective-permute-start(bf16[128,1024]{1,0:T(8,128)(2,1)S(1)} %get-tuple-element.45), channel_id=1, source_target_pairs={{0,144},{48,0},{96,48},{144,96},{1,145},{49,1},{97,49},{145,97},{2... | collective-permute-start | bytes 786440 | tf_op jit(solution)/shard_map/ppermute | solution.py:257
  85.2 7.9 %collective-permute-start.8 = (bf16[128,1024]{1,0:T(8,128)(2,1)S(1)}, bf16[128,1024]{1,0:T(8,128)(2,1)S(1)}, u32[]{:S(2)}, u32[]{:S(2)}) collective-permute-start(bf16[128,1024]{1,0:T(8,128)(2,1)S(1)} %get-tuple-element.46), channel_id=1, source_target_pairs={{0,96},{48,144},{96,0},{144,48},{1,97},{49,145},{97,1},{145,49},{2... | collective-permute-start | bytes 786440 | tf_op jit(solution)/shard_map/ppermute | solution.py:257
  93.1 1.9 collective-permute-start.9
  95.7 3.2 %collective-permute-start.4 = (bf16[4,256,128]{2,1,0:T(8,128)(2,1)S(1)}, bf16[4,256,128]{2,1,0:T(8,128)(2,1)S(1)}, u32[]{:S(2)}, u32[]{:S(2)}) collective-permute-start(bf16[4,256,128]{2,1,0:T(8,128)(2,1)S(1)} %get-tuple-element.38), channel_id=1, source_target_pairs={{0,6},{6,0},{1,7},{7,1},{2,8},{8,2},{3,9},{9,3},{4,10},{10,4},{5,1... | collective-permute-start | bytes 786440 | tf_op jit(solution)/shard_map/ppermute | solution.py:257
  99.0 1.2 convolution_multiply_fusion.scores_ref
  100.1 4.3 %collective-permute-done.4 = bf16[4,256,128]{2,1,0:T(8,128)(2,1)S(1)} collective-permute-done((bf16[4,256,128]{2,1,0:T(8,128)(2,1)S(1)}, bf16[4,256,128]{2,1,0:T(8,128)(2,1)S(1)}, u32[]{:S(2)}, u32[]{:S(2)}) %collective-permute-start.4) | collective-permute-done | bytes 262176 | tf_op jit(solution)/shard_map/ppermute | solution.py:257
  104.5 3.8 %collective-permute-start.5 = (bf16[2,4,256,128]{3,2,1,0:T(8,128)(2,1)S(1)}, bf16[2,4,256,128]{3,2,1,0:T(8,128)(2,1)S(1)}, u32[]{:S(2)}, u32[]{:S(2)}) collective-permute-start(bf16[2,4,256,128]{3,2,1,0:T(8,128)(2,1)S(1)} %pad_maximum_fusion.states_ref), channel_id=1, source_target_pairs={{0,1},{1,0},{2,3},{3,2},{4,5},{5,4},{6,7},{7,6},{8,9},{9,8},{10,11... | collective-permute-start | bytes 1572872 | tf_op jit(solution)/shard_map/ppermute | solution.py:257
  108.3 4.4 %collective-permute-done.9.refs_3_ = bf16[128,1024]{1,0:T(8,128)(2,1)S(1)} collective-permute-done((bf16[128,1024]{1,0:T(8,128)(2,1)S(1)}, bf16[128,1024]{1,0:T(8,128)(2,1)S(1)}, u32[]{:S(2)}, u32[]{:S(2)}) %collective-permute-start.9) | collective-permute-done | bytes 262176 | tf_op jit(solution)/shard_map/ppermute | solution.py:257
  112.7 1.5 shard_map.108
  116.0 5.1 %shard_map.109 = (bf16[128,1024]{1,0:T(8,128)(2,1)}, bf16[16,144,256]{2,1,0:T(8,128)(2,1)}) custom-call(bf16[128,1024]{1,0:T(8,128)(2,1)} %convolution_convert_fusion.1.queries_ref, f32[128,512]{1,0:T(8,128)} %convolution_multiply_fusion.scores_ref, bf16[128,1024]{1,0:T(8,128)(2,1)} %bitcast.40, s32[128,1]{1,0:T(8,128)} %copy.12.positive_ref, ...), custom_call_target="tpu_custom_call" | custom-call | flops 671088640 | bytes 4194304 | tf_op jit(solution)/shard_map/pallas_call | solution.py:39
  121.1 30.4 %all_to_all.26.grads_ref = bf16[16,144,256]{2,1,0:T(8,128)(2,1)} all-to-all(bf16[16,144,256]{2,1,0:T(8,128)(2,1)} %get-tuple-element.50), channel_id=1, replica_groups=mesh['zh'=4,'x'=4,'yh'=4,'yl'=2,'zl'=3,'c'=2] {'x','yl','c'}, dimensions={0} | all-to-all | bytes 2359296 | tf_op jit(solution)/shard_map/all_to_all | solution.py:261
  151.6 2.7 %shard_map.110 = (bf16[256,256]{1,0:T(8,128)(2,1)}, bf16[4,16,128]{2,1,0:T(8,128)(2,1)}) custom-call(s32[4]{0:T(128)} %copy-done.10, bf16[2,4,256,128]{3,2,1,0:T(8,128)(2,1)} %copy-done.14, bf16[2,4,256,128]{3,2,1,0:T(8,128)(2,1)} %copy-done.16, bf16[16,144,256]{2,1,0:T(8,128)(2,1)} %all_to_all.26.grads_ref), custom_call_target="tpu_custom_call" | custom-call | flops 268435456 | bytes 2097152 | tf_op jit(solution)/shard_map/pallas_call | solution.py:39
  154.3 13.4 %all-to-all-start.3 = ((bf16[16,16,256]{2,1,0:T(8,128)(2,1)}), bf16[16,16,256]{2,1,0:T(8,128)(2,1)}, u32[]{:S(2)}, u32[]{:S(2)}) async-start(bf16[16,16,256]{2,1,0:T(8,128)(2,1)} %bitcast.44), calls=%async_computation.3 | async-start | bytes 262144 | tf_op jit(solution)/shard_map/all_to_all | solution.py:261
  167.7 6.2 %collective-permute-start.10 = (bf16[4,16,128]{2,1,0:T(8,128)(2,1)}, bf16[4,16,128]{2,1,0:T(8,128)(2,1)S(1)}, u32[]{:S(2)}, u32[]{:S(2)}) collective-permute-start(bf16[4,16,128]{2,1,0:T(8,128)(2,1)} %get-tuple-element.53.stats_ref), channel_id=1, source_target_pairs={{0,576},{192,0},{384,192},{576,384},{1,577},{193,1},{385,193},{577... | collective-permute-start | bytes 49160 | tf_op jit(solution)/shard_map/ppermute | solution.py:257
  173.9 2.5 %convolution_convert_fusion = bf16[128,1024]{1,0:T(8,128)(2,1)} fusion(bf16[128,1024]{1,0:T(8,128)(2,1)} %get-tuple-element.52, bf16[1024,1024]{1,0:T(8,128)(2,1)S(1)} %copy-done), kind=kOutput, calls=%fused_computation | convolution fusion | flops 268566528 | bytes 2621440 | tf_op jit(solution)/shard_map/dot_general | solution.py:51
  176.4 5.3 %all-to-all-done.3.parts_ref = bf16[16,16,256]{2,1,0:T(8,128)(2,1)} async-done(((bf16[16,16,256]{2,1,0:T(8,128)(2,1)}), bf16[16,16,256]{2,1,0:T(8,128)(2,1)}, u32[]{:S(2)}, u32[]{:S(2)}) %all-to-all-start.3) | async-done | bytes 131104 | tf_op jit(solution)/shard_map/all_to_all | solution.py:261
  181.7 1.7 shard_map.111
  183.4 15.7 %all-to-all-start.4 = ((bf16[48,16,256]{2,1,0:T(8,128)(2,1)}), bf16[48,16,256]{2,1,0:T(8,128)(2,1)S(1)}, u32[]{:S(2)}, u32[]{:S(2)}) async-start(bf16[48,16,256]{2,1,0:T(8,128)(2,1)} %shard_map.111), calls=%async_computation.4 | async-start | bytes 786432 | tf_op jit(solution)/shard_map/all_to_all | solution.py:261
  199.2 1.7 shard_map.112
  200.8 11.9 %all-to-all-done.4.parts_ref = bf16[48,16,256]{2,1,0:T(8,128)(2,1)S(1)} async-done(((bf16[48,16,256]{2,1,0:T(8,128)(2,1)}), bf16[48,16,256]{2,1,0:T(8,128)(2,1)S(1)}, u32[]{:S(2)}, u32[]{:S(2)}) %all-to-all-start.4) | async-done | bytes 393248 | tf_op jit(solution)/shard_map/all_to_all | solution.py:261
  213.5 1.7 shard_map.113
  (54 shorter events, 10.5 us)
Async XLA Ops:
  0.6 39.4 %collective-permute-start = (bf16[128,1024]{1,0:T(8,128)(2,1)}, bf16[128,1024]{1,0:T(8,128)(2,1)S(1)}, u32[]{:S(2)}, u32[]{:S(2)}) collective-permute-start(bf16[128,1024]{1,0:T(8,128)(2,1)} %bitcast.33), channel_id=1, source_target_pairs={{0,192},{192,384},{384,576},{576,0},{1,193},{193,385},{385,577},{5... | collective-permute-start | bytes 786440 | tf_op jit(solution)/shard_map/ppermute | solution.py:257
  40.0 26.6 %collective-permute-start.6 = (bf16[128,1024]{1,0:T(8,128)(2,1)}, bf16[128,1024]{1,0:T(8,128)(2,1)}, u32[]{:S(2)}, u32[]{:S(2)}) collective-permute-start(bf16[128,1024]{1,0:T(8,128)(2,1)} %bitcast.29), channel_id=1, source_target_pairs={{0,576},{192,0},{384,192},{576,384},{1,577},{193,1},{385,193},{577... | collective-permute-start | bytes 786440 | tf_op jit(solution)/shard_map/ppermute | solution.py:257
  45.7 6.3 %copy-start = (bf16[1024,1024]{1,0:T(8,128)(2,1)S(1)}, bf16[1024,1024]{1,0:T(8,128)(2,1)}, u32[]{:S(2)}) copy-start(bf16[1024,1024]{1,0:T(8,128)(2,1)} %weight_ref.1) | copy-start | bytes 6291460
  45.8 6.3 %copy-start.4 = (bf16[1,1,128,1024]{3,2,1,0:T(8,128)(2,1)S(1)}, bf16[1,1,128,1024]{3,2,1,0:T(8,128)(2,1)}, u32[]{:S(2)}) copy-start(bf16[1,1,128,1024]{3,2,1,0:T(8,128)(2,1)} %param.8) | copy-start | bytes 786436
  45.8 70.2 %all-to-all-start.1 = ((bf16[16,64,1024]{2,1,0:T(8,128)(2,1)}), bf16[16,64,1024]{2,1,0:T(8,128)(2,1)}, u32[]{:S(2)}, u32[]{:S(2)}) async-start(bf16[16,64,1024]{2,1,0:T(8,128)(2,1)} %shard_map.104), calls=%async_computation.1 | async-start | bytes 4194304 | tf_op jit(solution)/shard_map/all_to_all | solution.py:261
  52.1 1.2 copy-start.12
  52.1 1.9 copy-start.17
  52.1 2.9 %copy-start.5 = (bf16[1,1,128,1024]{3,2,1,0:T(8,128)(2,1)S(1)}, bf16[1,1,128,1024]{3,2,1,0:T(8,128)(2,1)}, u32[]{:S(2)}) copy-start(bf16[1,1,128,1024]{3,2,1,0:T(8,128)(2,1)} %param.9) | copy-start | bytes 786436
  54.9 40.1 %copy-start.10 = (s32[4]{0:T(128)}, s32[4]{0:T(128)S(1)}, u32[]{:S(2)}) copy-start(s32[4]{0:T(128)S(1)} %pad_add_fusion.place_ref) | copy-start | bytes 52
  55.9 15.5 %collective-permute-start.1 = (bf16[128,1280]{1,0:T(8,128)(2,1)S(1)}, bf16[128,1280]{1,0:T(8,128)(2,1)S(1)}, u32[]{:S(2)}, u32[]{:S(2)}) collective-permute-start(bf16[128,1280]{1,0:T(8,128)(2,1)S(1)} %get-tuple-element.35), channel_id=1, source_target_pairs={{0,48},{48,96},{96,144},{144,0},{1,49},{49,97},{97,145},{145,1},{2... | collective-permute-start | bytes 983048 | tf_op jit(solution)/shard_map/ppermute | solution.py:257
  59.1 19.7 %collective-permute-start.2 = (bf16[128,1280]{1,0:T(8,128)(2,1)S(1)}, bf16[128,1280]{1,0:T(8,128)(2,1)S(1)}, u32[]{:S(2)}, u32[]{:S(2)}) collective-permute-start(bf16[128,1280]{1,0:T(8,128)(2,1)S(1)} %get-tuple-element.36), channel_id=1, source_target_pairs={{0,96},{48,144},{96,0},{144,48},{1,97},{49,145},{97,1},{145,49},{2... | collective-permute-start | bytes 983048 | tf_op jit(solution)/shard_map/ppermute | solution.py:257
  63.4 31.6 %copy-start.6 = (bf16[1,1,128,1024]{3,2,1,0:T(8,128)(2,1)S(1)}, bf16[1,1,128,1024]{3,2,1,0:T(8,128)(2,1)}, u32[]{:S(2)}) copy-start(bf16[1,1,128,1024]{3,2,1,0:T(8,128)(2,1)} %param.9) | copy-start | bytes 786436
  63.4 35.5 %copy-start.13 = (bf16[128,1024]{1,0:T(8,128)(2,1)S(1)}, bf16[128,1024]{1,0:T(8,128)(2,1)}, u32[]{:S(2)}) copy-start(bf16[128,1024]{1,0:T(8,128)(2,1)} %convolution_convert_fusion.1.queries_ref) | copy-start | bytes 786436
  63.5 16.5 %collective-permute-start.3 = (bf16[128,1280]{1,0:T(8,128)(2,1)S(1)}, bf16[128,1280]{1,0:T(8,128)(2,1)S(1)}, u32[]{:S(2)}, u32[]{:S(2)}) collective-permute-start(bf16[128,1280]{1,0:T(8,128)(2,1)S(1)} %get-tuple-element.37), channel_id=1, source_target_pairs={{0,144},{48,0},{96,48},{144,96},{1,145},{49,1},{97,49},{145,97},{2... | collective-permute-start | bytes 983048 | tf_op jit(solution)/shard_map/ppermute | solution.py:257
  80.0 28.3 %collective-permute-start.7 = (bf16[128,1024]{1,0:T(8,128)(2,1)S(1)}, bf16[128,1024]{1,0:T(8,128)(2,1)S(1)}, u32[]{:S(2)}, u32[]{:S(2)}) collective-permute-start(bf16[128,1024]{1,0:T(8,128)(2,1)S(1)} %get-tuple-element.45), channel_id=1, source_target_pairs={{0,144},{48,0},{96,48},{144,96},{1,145},{49,1},{97,49},{145,97},{2... | collective-permute-start | bytes 786440 | tf_op jit(solution)/shard_map/ppermute | solution.py:257
  85.2 23.1 %collective-permute-start.8 = (bf16[128,1024]{1,0:T(8,128)(2,1)S(1)}, bf16[128,1024]{1,0:T(8,128)(2,1)S(1)}, u32[]{:S(2)}, u32[]{:S(2)}) collective-permute-start(bf16[128,1024]{1,0:T(8,128)(2,1)S(1)} %get-tuple-element.46), channel_id=1, source_target_pairs={{0,96},{48,144},{96,0},{144,48},{1,97},{49,145},{97,1},{145,49},{2... | collective-permute-start | bytes 786440 | tf_op jit(solution)/shard_map/ppermute | solution.py:257
  93.1 19.6 %collective-permute-start.9 = (bf16[128,1024]{1,0:T(8,128)(2,1)S(1)}, bf16[128,1024]{1,0:T(8,128)(2,1)S(1)}, u32[]{:S(2)}, u32[]{:S(2)}) collective-permute-start(bf16[128,1024]{1,0:T(8,128)(2,1)S(1)} %get-tuple-element.47), channel_id=1, source_target_pairs={{0,48},{48,96},{96,144},{144,0},{1,49},{49,97},{97,145},{145,1},{2... | collective-permute-start | bytes 786440 | tf_op jit(solution)/shard_map/ppermute | solution.py:257
  95.7 18.5 %copy-start.1 = (bf16[512,1024]{1,0:T(8,128)(2,1)}, bf16[512,1024]{1,0:T(8,128)(2,1)S(1)}, u32[]{:S(2)}) copy-start(bf16[512,1024]{1,0:T(8,128)(2,1)S(1)} %get-tuple-element.39.blocks_ref) | copy-start | bytes 3145732
  95.7 8.7 %collective-permute-start.4 = (bf16[4,256,128]{2,1,0:T(8,128)(2,1)S(1)}, bf16[4,256,128]{2,1,0:T(8,128)(2,1)S(1)}, u32[]{:S(2)}, u32[]{:S(2)}) collective-permute-start(bf16[4,256,128]{2,1,0:T(8,128)(2,1)S(1)} %get-tuple-element.38), channel_id=1, source_target_pairs={{0,6},{6,0},{1,7},{7,1},{2,8},{8,2},{3,9},{9,3},{4,10},{10,4},{5,1... | collective-permute-start | bytes 786440 | tf_op jit(solution)/shard_map/ppermute | solution.py:257
  104.5 9.8 %copy-start.14 = (bf16[2,4,256,128]{3,2,1,0:T(8,128)(2,1)}, bf16[2,4,256,128]{3,2,1,0:T(8,128)(2,1)S(1)}, u32[]{:S(2)}) copy-start(bf16[2,4,256,128]{3,2,1,0:T(8,128)(2,1)S(1)} %pad_maximum_fusion.states_ref) | copy-start | bytes 1572868
  104.5 11.5 %collective-permute-start.5 = (bf16[2,4,256,128]{3,2,1,0:T(8,128)(2,1)S(1)}, bf16[2,4,256,128]{3,2,1,0:T(8,128)(2,1)S(1)}, u32[]{:S(2)}, u32[]{:S(2)}) collective-permute-start(bf16[2,4,256,128]{3,2,1,0:T(8,128)(2,1)S(1)} %pad_maximum_fusion.states_ref), channel_id=1, source_target_pairs={{0,1},{1,0},{2,3},{3,2},{4,5},{5,4},{6,7},{7,6},{8,9},{9,8},{10,11... | collective-permute-start | bytes 1572872 | tf_op jit(solution)/shard_map/ppermute | solution.py:257
  114.3 1.0 copy-start.2
  115.3 0.7 copy-start.7
  116.0 35.6 %copy-start.16 = (bf16[2,4,256,128]{3,2,1,0:T(8,128)(2,1)}, bf16[2,4,256,128]{3,2,1,0:T(8,128)(2,1)S(1)}, u32[]{:S(2)}) copy-start(bf16[2,4,256,128]{3,2,1,0:T(8,128)(2,1)S(1)} %collective-permute-done.5.pair_ref) | copy-start | bytes 1572868
  154.3 44.8 %copy-start.3 = (bf16[512,1024]{1,0:T(8,128)(2,1)S(1)}, bf16[512,1024]{1,0:T(8,128)(2,1)}, u32[]{:S(2)}) copy-start(bf16[512,1024]{1,0:T(8,128)(2,1)} %copy-done.2) | copy-start | bytes 3145732
  154.3 44.8 %copy-start.8 = (f32[128,512]{1,0:T(8,128)S(1)}, f32[128,512]{1,0:T(8,128)}, u32[]{:S(2)}) copy-start(f32[128,512]{1,0:T(8,128)} %copy-done.7) | copy-start | bytes 786436
  154.3 44.9 %copy-start.9 = (bf16[4,16,128]{2,1,0:T(8,128)(2,1)S(1)}, bf16[4,16,128]{2,1,0:T(8,128)(2,1)}, u32[]{:S(2)}) copy-start(bf16[4,16,128]{2,1,0:T(8,128)(2,1)} %get-tuple-element.53.stats_ref) | copy-start | bytes 49156
  154.3 44.9 %copy-start.11 = (s32[4]{0:T(128)S(1)}, s32[4]{0:T(128)}, u32[]{:S(2)}) copy-start(s32[4]{0:T(128)} %copy-done.10) | copy-start | bytes 52
  154.3 27.4 %all-to-all-start.3 = ((bf16[16,16,256]{2,1,0:T(8,128)(2,1)}), bf16[16,16,256]{2,1,0:T(8,128)(2,1)}, u32[]{:S(2)}, u32[]{:S(2)}) async-start(bf16[16,16,256]{2,1,0:T(8,128)(2,1)} %bitcast.44), calls=%async_computation.3 | async-start | bytes 262144 | tf_op jit(solution)/shard_map/all_to_all | solution.py:261
  167.7 8.7 %collective-permute-start.10 = (bf16[4,16,128]{2,1,0:T(8,128)(2,1)}, bf16[4,16,128]{2,1,0:T(8,128)(2,1)S(1)}, u32[]{:S(2)}, u32[]{:S(2)}) collective-permute-start(bf16[4,16,128]{2,1,0:T(8,128)(2,1)} %get-tuple-element.53.stats_ref), channel_id=1, source_target_pairs={{0,576},{192,0},{384,192},{576,384},{1,577},{193,1},{385,193},{577... | collective-permute-start | bytes 49160 | tf_op jit(solution)/shard_map/ppermute | solution.py:257
  183.4 29.3 %all-to-all-start.4 = ((bf16[48,16,256]{2,1,0:T(8,128)(2,1)}), bf16[48,16,256]{2,1,0:T(8,128)(2,1)S(1)}, u32[]{:S(2)}, u32[]{:S(2)}) async-start(bf16[48,16,256]{2,1,0:T(8,128)(2,1)} %shard_map.111), calls=%async_computation.4 | async-start | bytes 786432 | tf_op jit(solution)/shard_map/all_to_all | solution.py:261
  212.7 0.7 copy-start.15
